TPU v7x, 32 devices: a whole 2x2x4 slice. The times are simulated.
32 devices in a mesh: groups: 2 (over y), docs: 4 (over z), cent: 2 (over x), sub: 2 (over core).
Axes of the slice: x: 2, y: 2, z: 4, core: 2. Of those that a mesh axis runs over, the one named last changes fastest.
Arguments:
- queries: float32 [256, 128], P(('groups', 'cent', 'sub')), parts along dimension 0, may hold values from -0.6 to 0.6
- token_codes: int32 [4, 256, 8192], P(('cent', 'sub'), ('groups', 'docs')), parts along dimension 1, may hold values from 0 to 255
- centroid_ids: int32 [4, 32768], P(('cent', 'sub'), ('groups', 'docs')), parts along dimension 1, may hold values from 0 to 4095
- slot_counts: int32 [4, 256], P(('cent', 'sub'), ('groups', 'docs')), parts along dimension 1, may hold values from 0 to 128, as said below
- centroids: bfloat16 [16384, 128], P(('cent', 'sub')), may hold values from -3 to 3
- bucket_values: float32 [16, 128], replicated, may hold values from -1.5 to 1.5
- candidates: int32 [8, 64], P(('groups', 'docs')), parts along dimension 0, may hold values from 0 to 127, as said below
- input_proj: float32 [32, 256], replicated, may hold values from -1 to 1
- gain_one: float32 [256], replicated, may hold values from 0.5 to 1.5
- query_proj: bfloat16 [256, 256], replicated, may hold values from -32 to 32, as said below
- key_proj: bfloat16 [256, 256], replicated, may hold values from -1 to 1, as said below
- value_proj: bfloat16 [256, 256], replicated, may hold values from -0.375 to 0.375
- output_proj: bfloat16 [256, 256], replicated, may hold values from -0.375 to 0.375
- gain_two: float32 [256], replicated, may hold values from 0.5 to 1.5
- up_proj: bfloat16 [256, 1024], replicated, may hold values from -0.375 to 0.375
- down_proj: bfloat16 [1024, 256], replicated, may hold values from -0.1875 to 0.1875
Outputs:
- set_states: float32 [8, 64, 256], P(('groups', 'docs'), ('cent', 'sub')), parts along dimension 0
There are 2 independent parts, one for each index of `groups`. A program takes and returns all parts, laid end to end along the dimension named above; an argument that names none is the same for every part. Nothing has to cross between parts.
Inputs may be any that keep to these rules, and one draw needn't show every extreme that they name: `slot_counts`: for every document the counts over the 4 members sum to 256; some member holds 128 live slots of every document. The candidates of one query are distinct. `query_proj`: entries lie within the bounds below. `key_proj`: entries lie within the bounds below.
All inputs are finite; a program needn't handle non-finite values.
Results may differ from a plain program's by a relative error of at most 0.0045.
Values may be sent and summed in bfloat16 or wider, within the bound.
No kernel may reach another device: no remote copies, remote signals or barrier semaphores. Data moves between devices by JAX's collectives and lax.ppermute only.
A program may use at most 64 MiB of HBM per device.

v0:
```python
import math

import jax
import jax.numpy as jnp
from jax import lax
from jax.sharding import PartitionSpec as P

DIM = 128
QT = 32
H = 256
HEADS = 4
HEAD = 64


def dequantize(code_rows, cent_rows, centroid_table, bucket_table):
    lower = jnp.bitwise_and(code_rows, 15)
    upper = jnp.right_shift(code_rows, 4)
    nibbles = jnp.stack([lower, upper], axis=-1).reshape(code_rows.shape[0], -1)
    residual = jnp.zeros(nibbles.shape, jnp.float32)
    for level_id in range(bucket_table.shape[0]):
        residual = residual + jnp.where(
            nibbles == level_id, bucket_table[level_id][None, :], jnp.float32(0.0)
        )
    anchor = jnp.take(centroid_table, cent_rows, axis=0).astype(jnp.float32)
    return (anchor + residual).astype(jnp.bfloat16)


def block_maxima(
    code_rows, cent_rows, live_counts, centroid_table, bucket_table, query_bf, pad_slots
):
    embedded = dequantize(code_rows, cent_rows, centroid_table, bucket_table)
    scores = lax.dot_general(
        embedded, query_bf, (((1,), (1,)), ((), ())), preferred_element_type=jnp.float32
    )
    positions = jnp.arange(pad_slots, dtype=jnp.int32)
    live_slot = (positions[None, :] < live_counts[:, None]).reshape(-1)
    scores = jnp.where(live_slot[:, None], scores, jnp.float32(-1e30))
    return jnp.max(scores.reshape(live_counts.shape[0], pad_slots, scores.shape[1]), axis=1)


def rms_scale(values, gain):
    mean_square = jnp.mean(values * values, axis=-1, keepdims=True)
    return (values * lax.rsqrt(mean_square + 1e-06) * gain).astype(jnp.bfloat16)


def first_hidden(features, input_proj):
    return jnp.einsum("qrt,th->qrh", features, input_proj, precision=lax.Precision.HIGHEST)


def project_rows(normed, weight):
    return jnp.einsum("qrh,hk->qrk", normed, weight, preferred_element_type=jnp.float32).astype(
        jnp.bfloat16
    )


def pick_rows(table, row_ids):
    return jnp.take(table, row_ids, axis=0)


def fold_keys(carry, pieces, query_heads):
    peak, summed, accum = carry
    key_piece, value_piece = pieces
    query_count, piece_rows = (key_piece.shape[0], key_piece.shape[1])
    key_four = key_piece.reshape(query_count, piece_rows, HEADS, HEAD)
    value_four = value_piece.reshape(query_count, piece_rows, HEADS, HEAD)
    scores = jnp.einsum(
        "qrhd,qkhd->qhrk", query_heads, key_four, preferred_element_type=jnp.float32
    ) * HEAD ** (-0.5)
    new_peak = jnp.maximum(peak, jnp.max(scores, axis=-1))
    expon = jnp.exp(scores - new_peak[..., None])
    summed = jnp.sum(expon, axis=-1)
    accum = jnp.einsum(
        "qhrk,qkhd->qhrd",
        expon.astype(jnp.bfloat16),
        value_four,
        preferred_element_type=jnp.float32,
    )
    return (new_peak, summed, accum)


def on_device(
    queries,
    token_codes,
    centroid_ids,
    slot_counts,
    centroids,
    bucket_values,
    candidates,
    input_proj,
    gain_one,
    query_proj,
    key_proj,
    value_proj,
    output_proj,
    gain_two,
    up_proj,
    down_proj,
):
    query_bf = lax.all_gather(queries.astype(jnp.bfloat16), ("cent", "sub"), axis=0, tiled=True)
    docs_local = token_codes.shape[1]
    pad_slots = token_codes.shape[2] * 2 // DIM
    block_docs = math.gcd(docs_local, max(1, 2048 // pad_slots))
    block_count = docs_local // block_docs
    code_blocks = token_codes.reshape(block_count, block_docs * pad_slots, DIM // 2)
    cent_blocks = centroid_ids.reshape(block_count, block_docs * pad_slots)
    count_blocks = slot_counts.reshape(block_count, block_docs)

    def one_block(inputs):
        code_rows, cent_rows, live_counts = inputs
        return block_maxima(
            code_rows, cent_rows, live_counts, centroids, bucket_values, query_bf, pad_slots
        )

    local_best = lax.map(one_block, (code_blocks, cent_blocks, count_blocks)).reshape(
        docs_local, -1
    )
    width_cs = lax.axis_size(("cent", "sub"))
    doc_best = lax.pmax(local_best, ("cent", "sub"))
    owner_best = lax.all_to_all(doc_best, "docs", split_axis=1, concat_axis=0, tiled=True)
    query_count = candidates.shape[0]
    per_query = owner_best.reshape(owner_best.shape[0], query_count, QT).transpose(1, 0, 2)
    rows_dev = candidates.shape[1] // width_cs
    row_start = lax.axis_index(("cent", "sub")) * rows_dev
    init = (
        jnp.full((query_count, HEADS, rows_dev), -1e30, jnp.float32),
        jnp.zeros((query_count, HEADS, rows_dev), jnp.float32),
        jnp.zeros((query_count, HEADS, rows_dev, HEAD), jnp.float32),
    )
    all_features = jax.vmap(pick_rows)(per_query, candidates)
    all_hidden = first_hidden(all_features, input_proj)
    all_normed = rms_scale(all_hidden, gain_one)
    hidden_zero = lax.dynamic_slice_in_dim(all_hidden, row_start, rows_dev, 1)
    normed_one = lax.dynamic_slice_in_dim(all_normed, row_start, rows_dev, 1)
    query_heads = project_rows(normed_one, query_proj).reshape(query_count, rows_dev, HEADS, HEAD)
    key_rows = project_rows(all_normed, key_proj)
    value_rows = project_rows(all_normed, value_proj)
    peak, summed, accum = fold_keys(init, (key_rows, value_rows), query_heads)
    attended = (
        (accum / summed[..., None])
        .transpose(0, 2, 1, 3)
        .reshape(query_count * rows_dev, H)
        .astype(jnp.bfloat16)
    )
    hidden_one = hidden_zero.reshape(query_count * rows_dev, H) + jnp.dot(
        attended, output_proj, preferred_element_type=jnp.float32
    )
    normed_two = rms_scale(hidden_one, gain_two)
    inner = jax.nn.gelu(jnp.dot(normed_two, up_proj, preferred_element_type=jnp.float32)).astype(
        jnp.bfloat16
    )
    set_states = hidden_one + jnp.dot(inner, down_proj, preferred_element_type=jnp.float32)
    return set_states.reshape(query_count, rows_dev, H)


def solution(mesh):
    in_specs = (
        P(("groups", "cent", "sub"), None),
        P(("cent", "sub"), ("groups", "docs"), None),
        P(("cent", "sub"), ("groups", "docs")),
        P(("cent", "sub"), ("groups", "docs")),
        P(("cent", "sub"), None),
        P(),
        P(("groups", "docs"), None),
        P(),
        P(),
        P(),
        P(),
        P(),
        P(),
        P(),
        P(),
        P(),
    )
    out_specs = P(("groups", "docs"), ("cent", "sub"), None)
    return jax.shard_map(
        on_device, mesh=mesh, in_specs=in_specs, out_specs=out_specs, check_vma=False
    )
```

profile of v0, /device:TPU:0, one launch (start us, length us, event | category | flops | bytes accessed | tf_op | source)
XLA Modules:
  0.0 183.2 jit_solution(2810963080451517649)
XLA Ops:
  3.9 3.1 %reshape.243 = s32[2,2048,64]{2,1,0:T(8,128)} reshape(s32[1,32,8192]{2,1,0:T(8,128)} %param.19) | data formatting | bytes 2097152 | tf_op jit(solution)/shard_map/reshape | solution.py:104
  7.0 2.9 %copy.53 = s32[2,2048,64]{1,0,2:T(2,128)} copy(s32[2,2048,64]{2,1,0:T(8,128)} %reshape.243) | data formatting | bytes 2097152 | tf_op jit(solution)/shard_map/while | solution.py:114
  9.9 6.2 %all_gather.3 = bf16[128,128]{1,0:T(8,128)(2,1)S(1)} all-gather(bf16[32,128]{1,0:T(8,128)(2,1)S(1)} %convert_element_type.47), channel_id=1, replica_groups=mesh['groups'=2,'docs'=4,'cent'=2,'sub'=2] {'cent','sub'}, dimensions={0}, use_global_device_ids=true | all-gather | bytes 40960 | tf_op jit(solution)/shard_map/all_gather | solution.py:99
  16.1 134.4 %while.10 = (s32[]{:T(128)}, f32[2,16,128]{2,1,0:T(8,128)S(1)}, s32[2,16]{1,0:T(2,128)}, s32[2,2048]{1,0:T(2,128)S(1)}, bf16[4096,128]{1,0:T(8,128)(2,1)S(1)}, /...) while((s32[]{:T(128)}, f32[2,16,128]{2,1,0:T(8,128)S(1)}, ...), condition=%wide.region_2.3_spmd, body=%wide.region_0.2_spmd.sunk | while | flops 81809408 | bytes 37896688 | solution.py:114
  16.1 2.0 %and_bitcast_fusion.3 = (s32[2048,64,1]{0,2,1:T(1,128)S(1)}, s32[2048,64,1]{0,2,1:T(1,128)S(1)}) fusion(s32[2,2048,64]{1,0,2:T(2,128)} %get-tuple-element.258, s32[]{:T(128)} %get-tuple-element.244), kind=kLoop, calls=%fused_computation.23.clone.1 | loop fusion | flops 262144 | bytes 1572868 | tf_op jit(solution)/shard_map/while/body/eval_jaxpr/and | solution.py:16
  18.1 6.9 %broadcast_compare_fusion.19 = (pred[2048,64,2]{0,2,1:T(4,128)(4,1)}, pred[2048,64,2]{0,2,1:T(4,128)(4,1)S(1)}, pred[2048,64,2]{0,2,1:T(4,128)(4,1)}, pred[2048,...) fusion(s32[2048,64,1]{0,2,1:T(1,128)S(1)} %get-tuple-element.19, ...), kind=kLoop, calls=%fused_computation.21.clone.1 | loop fusion | flops 2621440 | bytes 3407872 | tf_op jit(solution)/shard_map/while/body/eval_jaxpr/eq | solution.py:22
  25.0 1.7 eq.147
  27.8 1.7 eq.139
  30.5 1.7 eq.140
  33.3 1.7 eq.141
  36.0 1.7 eq.142
  38.8 1.7 eq.143
  41.5 1.7 eq.144
  44.3 1.7 eq.145
  48.9 6.0 %broadcast_compare_fusion.18 = (pred[2048,64,2]{0,2,1:T(4,128)(4,1)S(1)}, pred[2048,64,2]{0,2,1:T(4,128)(4,1)}, pred[2048,64,2]{0,2,1:T(4,128)(4,1)}, pred[2048,...) fusion(s32[2048,64,1]{0,2,1:T(1,128)S(1)} %get-tuple-element.19, ...), kind=kLoop, calls=%fused_computation.12.clone.1 | loop fusion | flops 2097152 | bytes 2883584 | tf_op jit(solution)/shard_map/while/body/eval_jaxpr/eq | solution.py:22
  54.8 1.7 eq.132
  57.6 1.7 eq.133
  60.4 1.7 eq.134
  63.2 1.7 eq.135
  72.1 6.2 %gather_fusion = bf16[2048,128]{1,0:T(8,128)(2,1)S(1)} fusion(bf16[4096,128]{1,0:T(8,128)(2,1)S(1)} %get-tuple-element.257, s32[2048]{0:T(1024)S(1)} %broadcast_clamp_fusion.2), kind=kCustom, calls=%fused_computation.clone.1 | custom fusion | bytes 1056768 | tf_op jit(solution)/shard_map/while/body/eval_jaxpr/jit(_take)/gather | solution.py:24
  79.1 4.2 %bitcast_reduce_fusion.2 = f32[16,128]{1,0:T(8,128)S(1)} fusion(bf16[128,128]{1,0:T(8,128)(2,1)S(1)} %get-tuple-element.260, pred[2048]{0:T(1024)(128)(4,1)S(1)} %fusion.66, pred[2048,128]{1,0:T(32,128)(4,1)} %copy.85, pred[2048,128]{1,0:T(32,128)(4,1)} %copy.86, pred[2048,128]{1,0:T(32,128)(4,1)} %copy.87, pred[2048,128]{1,0:T(32,128)(4,1)} %copy.88, ...), kind=kOutput, calls=%fused_computation.4.clone.1 | convolution fusion | flops 76806144 | bytes 4771840 | tf_op jit(solution)/shard_map/while/body/eval_jaxpr/dot_general | solution.py:32
  83.3 2.0 %and_bitcast_fusion.3 = (s32[2048,64,1]{0,2,1:T(1,128)S(1)}, s32[2048,64,1]{0,2,1:T(1,128)S(1)}) fusion(s32[2,2048,64]{1,0,2:T(2,128)} %get-tuple-element.258, s32[]{:T(128)} %get-tuple-element.244), kind=kLoop, calls=%fused_computation.23.clone.1 | loop fusion | flops 262144 | bytes 1572868 | tf_op jit(solution)/shard_map/while/body/eval_jaxpr/and | solution.py:16
  85.3 6.9 %broadcast_compare_fusion.19 = (pred[2048,64,2]{0,2,1:T(4,128)(4,1)}, pred[2048,64,2]{0,2,1:T(4,128)(4,1)S(1)}, pred[2048,64,2]{0,2,1:T(4,128)(4,1)}, pred[2048,...) fusion(s32[2048,64,1]{0,2,1:T(1,128)S(1)} %get-tuple-element.19, ...), kind=kLoop, calls=%fused_computation.21.clone.1 | loop fusion | flops 2621440 | bytes 3407872 | tf_op jit(solution)/shard_map/while/body/eval_jaxpr/eq | solution.py:22
  111.5 1.7 eq.145
  116.1 6.0 %broadcast_compare_fusion.18 = (pred[2048,64,2]{0,2,1:T(4,128)(4,1)S(1)}, pred[2048,64,2]{0,2,1:T(4,128)(4,1)}, pred[2048,64,2]{0,2,1:T(4,128)(4,1)}, pred[2048,...) fusion(s32[2048,64,1]{0,2,1:T(1,128)S(1)} %get-tuple-element.19, ...), kind=kLoop, calls=%fused_computation.12.clone.1 | loop fusion | flops 2097152 | bytes 2883584 | tf_op jit(solution)/shard_map/while/body/eval_jaxpr/eq | solution.py:22
  124.8 1.7 eq.133
  127.6 1.7 eq.134
  139.3 6.2 %gather_fusion = bf16[2048,128]{1,0:T(8,128)(2,1)S(1)} fusion(bf16[4096,128]{1,0:T(8,128)(2,1)S(1)} %get-tuple-element.257, s32[2048]{0:T(1024)S(1)} %broadcast_clamp_fusion.2), kind=kCustom, calls=%fused_computation.clone.1 | custom fusion | bytes 1056768 | tf_op jit(solution)/shard_map/while/body/eval_jaxpr/jit(_take)/gather | solution.py:24
  146.3 4.2 %bitcast_reduce_fusion.2 = f32[16,128]{1,0:T(8,128)S(1)} fusion(bf16[128,128]{1,0:T(8,128)(2,1)S(1)} %get-tuple-element.260, pred[2048]{0:T(1024)(128)(4,1)S(1)} %fusion.66, pred[2048,128]{1,0:T(32,128)(4,1)} %copy.85, pred[2048,128]{1,0:T(32,128)(4,1)} %copy.86, pred[2048,128]{1,0:T(32,128)(4,1)} %copy.87, pred[2048,128]{1,0:T(32,128)(4,1)} %copy.88, ...), kind=kOutput, calls=%fused_computation.4.clone.1 | convolution fusion | flops 76806144 | bytes 4771840 | tf_op jit(solution)/shard_map/while/body/eval_jaxpr/dot_general | solution.py:32
  150.6 12.6 %pmax.7 = f32[32,4,32]{2,0,1:T(8,128)S(1)} all-reduce(f32[32,4,32]{2,0,1:T(8,128)S(1)} %copy.54), channel_id=1, replica_groups=mesh['groups'=2,'docs'=4,'cent'=2,'sub'=2] {'cent','sub'}, use_global_device_ids=true, to_apply=%region_3.4 | all-reduce | flops 4096 | bytes 32768 | tf_op jit(solution)/shard_map/pmax | solution.py:118
  164.0 4.9 %all-to-all-start = ((f32[4,1,1024]{2,1,0:T(1,128)}), f32[4,1,1024]{2,1,0:T(1,128)S(1)}, u32[]{:S(2)}, u32[]{:S(2)}) async-start(f32[4,1,1024]{2,1,0:T(1,128)} %reshape.285), calls=%async_computation | async-start | bytes 32768 | tf_op jit(solution)/shard_map/all_to_all | solution.py:119
  170.2 4.3 %all-to-all-done = f32[4,1,1024]{2,1,0:T(1,128)S(1)} async-done(((f32[4,1,1024]{2,1,0:T(1,128)}), f32[4,1,1024]{2,1,0:T(1,128)S(1)}, u32[]{:S(2)}, u32[]{:S(2)}) %all-to-all-start) | async-done | bytes 16416 | tf_op jit(solution)/shard_map/all_to_all | solution.py:119
  (143 shorter events, 72.5 us)
Async XLA Ops:
  0.0 182.2 %copy-start = (bf16[1024,256]{1,0:T(8,128)(2,1)S(1)}, bf16[1024,256]{1,0:T(8,128)(2,1)}, u32[]{:S(2)}) copy-start(bf16[1024,256]{1,0:T(8,128)(2,1)} %param.33) | copy-start | bytes 1572868
  7.0 2.9 %copy-start.13 = (f32[32,128]{1,0:T(8,128)S(1)}, f32[32,128]{1,0:T(8,128)}, u32[]{:S(2)}) copy-start(f32[32,128]{1,0:T(8,128)} %param.18) | copy-start | bytes 49156
  7.0 9.0 %copy-start.1 = (bf16[4096,128]{1,0:T(8,128)(2,1)S(1)}, bf16[4096,128]{1,0:T(8,128)(2,1)}, u32[]{:S(2)}) copy-start(bf16[4096,128]{1,0:T(8,128)(2,1)} %param.22) | copy-start | bytes 3145732
  7.0 9.0 %copy-start.10 = (f32[16,128]{1,0:T(8,128)S(1)}, f32[16,128]{1,0:T(8,128)}, u32[]{:S(2)}) copy-start(f32[16,128]{1,0:T(8,128)} %param.23) | copy-start | bytes 24580
  16.1 160.5 %copy-start.12 = (f32[32,256]{1,0:T(8,128)S(1)}, f32[32,256]{1,0:T(8,128)}, u32[]{:S(2)}) copy-start(f32[32,256]{1,0:T(8,128)} %param.25) | copy-start | bytes 98308
  57.6 8.4 %copy-start.3 = (pred[2048,64,2]{0,2,1:T(4,128)(4,1)S(1)}, pred[2048,64,2]{0,2,1:T(4,128)(4,1)}, u32[]{:S(2)}) copy-start(pred[2048,64,2]{0,2,1:T(4,128)(4,1)} %get-tuple-element.205) | copy-start | bytes 786436 | tf_op jit(solution)/shard_map/while
  60.4 7.4 %copy-start.2 = (pred[2048,64,2]{0,2,1:T(4,128)(4,1)S(1)}, pred[2048,64,2]{0,2,1:T(4,128)(4,1)}, u32[]{:S(2)}) copy-start(pred[2048,64,2]{0,2,1:T(4,128)(4,1)} %get-tuple-element.206) | copy-start | bytes 786436 | tf_op jit(solution)/shard_map/while
  72.0 7.0 %copy-start.4 = (pred[2048,128]{1,0:T(32,128)(4,1)S(1)}, pred[2048,128]{1,0:T(32,128)(4,1)}, u32[]{:S(2)}) copy-start(pred[2048,128]{1,0:T(32,128)(4,1)} %copy.100) | copy-start | bytes 786436 | tf_op jit(solution)/shard_map/while
  72.0 7.0 %copy-start.5 = (pred[2048,128]{1,0:T(32,128)(4,1)S(1)}, pred[2048,128]{1,0:T(32,128)(4,1)}, u32[]{:S(2)}) copy-start(pred[2048,128]{1,0:T(32,128)(4,1)} %copy.92) | copy-start | bytes 786436 | tf_op jit(solution)/shard_map/while
  72.0 7.0 %copy-start.6 = (pred[2048,128]{1,0:T(32,128)(4,1)S(1)}, pred[2048,128]{1,0:T(32,128)(4,1)}, u32[]{:S(2)}) copy-start(pred[2048,128]{1,0:T(32,128)(4,1)} %copy.93) | copy-start | bytes 786436 | tf_op jit(solution)/shard_map/while
  72.0 7.0 %copy-start.7 = (pred[2048,128]{1,0:T(32,128)(4,1)S(1)}, pred[2048,128]{1,0:T(32,128)(4,1)}, u32[]{:S(2)}) copy-start(pred[2048,128]{1,0:T(32,128)(4,1)} %copy.94) | copy-start | bytes 786436 | tf_op jit(solution)/shard_map/while
  72.0 7.0 %copy-start.8 = (pred[2048,128]{1,0:T(32,128)(4,1)S(1)}, pred[2048,128]{1,0:T(32,128)(4,1)}, u32[]{:S(2)}) copy-start(pred[2048,128]{1,0:T(32,128)(4,1)} %copy.95) | copy-start | bytes 786436 | tf_op jit(solution)/shard_map/while
  124.8 8.4 %copy-start.3 = (pred[2048,64,2]{0,2,1:T(4,128)(4,1)S(1)}, pred[2048,64,2]{0,2,1:T(4,128)(4,1)}, u32[]{:S(2)}) copy-start(pred[2048,64,2]{0,2,1:T(4,128)(4,1)} %get-tuple-element.205) | copy-start | bytes 786436 | tf_op jit(solution)/shard_map/while
  127.6 7.4 %copy-start.2 = (pred[2048,64,2]{0,2,1:T(4,128)(4,1)S(1)}, pred[2048,64,2]{0,2,1:T(4,128)(4,1)}, u32[]{:S(2)}) copy-start(pred[2048,64,2]{0,2,1:T(4,128)(4,1)} %get-tuple-element.206) | copy-start | bytes 786436 | tf_op jit(solution)/shard_map/while
  139.2 7.0 %copy-start.4 = (pred[2048,128]{1,0:T(32,128)(4,1)S(1)}, pred[2048,128]{1,0:T(32,128)(4,1)}, u32[]{:S(2)}) copy-start(pred[2048,128]{1,0:T(32,128)(4,1)} %copy.100) | copy-start | bytes 786436 | tf_op jit(solution)/shard_map/while
  139.2 7.0 %copy-start.5 = (pred[2048,128]{1,0:T(32,128)(4,1)S(1)}, pred[2048,128]{1,0:T(32,128)(4,1)}, u32[]{:S(2)}) copy-start(pred[2048,128]{1,0:T(32,128)(4,1)} %copy.92) | copy-start | bytes 786436 | tf_op jit(solution)/shard_map/while
  139.2 7.0 %copy-start.6 = (pred[2048,128]{1,0:T(32,128)(4,1)S(1)}, pred[2048,128]{1,0:T(32,128)(4,1)}, u32[]{:S(2)}) copy-start(pred[2048,128]{1,0:T(32,128)(4,1)} %copy.93) | copy-start | bytes 786436 | tf_op jit(solution)/shard_map/while
  139.2 7.0 %copy-start.7 = (pred[2048,128]{1,0:T(32,128)(4,1)S(1)}, pred[2048,128]{1,0:T(32,128)(4,1)}, u32[]{:S(2)}) copy-start(pred[2048,128]{1,0:T(32,128)(4,1)} %copy.94) | copy-start | bytes 786436 | tf_op jit(solution)/shard_map/while
  139.2 7.0 %copy-start.8 = (pred[2048,128]{1,0:T(32,128)(4,1)S(1)}, pred[2048,128]{1,0:T(32,128)(4,1)}, u32[]{:S(2)}) copy-start(pred[2048,128]{1,0:T(32,128)(4,1)} %copy.95) | copy-start | bytes 786436 | tf_op jit(solution)/shard_map/while
  150.5 31.4 %copy-start.11 = (bf16[256,256]{1,0:T(8,128)(2,1)S(1)}, bf16[256,256]{1,0:T(8,128)(2,1)}, u32[]{:S(2)}) copy-start(bf16[256,256]{1,0:T(8,128)(2,1)} %param.30) | copy-start | bytes 393220
  150.5 31.7 %copy-start.9 = (bf16[256,1024]{1,0:T(8,128)(2,1)S(1)}, bf16[256,1024]{1,0:T(8,128)(2,1)}, u32[]{:S(2)}) copy-start(bf16[256,1024]{1,0:T(8,128)(2,1)} %param.32) | copy-start | bytes 1572868
  150.5 31.7 %copy-start.14 = (f32[256]{0:T(256)S(1)}, f32[256]{0:T(256)}, u32[]{:S(2)}) copy-start(f32[256]{0:T(256)} %param.31) | copy-start | bytes 3076
  164.0 10.5 %all-to-all-start = ((f32[4,1,1024]{2,1,0:T(1,128)}), f32[4,1,1024]{2,1,0:T(1,128)S(1)}, u32[]{:S(2)}, u32[]{:S(2)}) async-start(f32[4,1,1024]{2,1,0:T(1,128)} %reshape.285), calls=%async_computation | async-start | bytes 32768 | tf_op jit(solution)/shard_map/all_to_all | solution.py:119
where the time goes:
time: 184 us; the launch traced here: 183 us
  local copies, waits for them, and re-layouts  105 us (57%)
  other arithmetic  35.7 us (19%)
  blocking collectives  18.8 us (10%)
  matrix products  13.6 us (7%)
  starting transfers between devices  4.87 us (3%)
  waiting for transfers between devices  4.27 us (2%)
    eq x64, local copies, waits for them, and re-layouts, dequantize(): nibbles == level_id  80.4 us
    eq x4, other arithmetic, dequantize(): nibbles == level_id  25.7 us
    pmax x1, blocking collectives, on_device(): doc_best = lax.pmax(local_best, ('cent', 'sub'))  12.6 us
    gather x2, local copies, waits for them, and re-layouts, dequantize(): anchor = jnp.take(centroid_table, cent_rows, axis=0).astype(jnp.float32)  12.4 us
    dot_general x2, matrix products, block_maxima(): lax.dot_general(embedded, query_bf, (((1,), (1,)), ((), ())), preferred_e...  8.36 us
    all_gather x1, blocking collectives, on_device(): lax.all_gather(queries.astype(jnp.bfloat16), ('cent', 'sub'), axis=0, til...  6.17 us
    all_to_all x1, starting transfers between devices, on_device(): lax.all_to_all(doc_best, 'docs', split_axis=1, concat_axis=0, tiled=True)  4.87 us
    all_to_all x1, waiting for transfers between devices, on_device(): lax.all_to_all(doc_best, 'docs', split_axis=1, concat_axis=0, tiled=True)  4.27 us
  transfers between devices with their start and end apart: 1, of which 1 were waited for; matrix products, arithmetic and copies ran while one was open for 1% of the time, Pallas kernels for 0%

commit v1 on v0

v1 whole, which is shorter than its diff:
```python
import functools

import jax
import jax.numpy as jnp
from jax import lax
from jax.experimental import pallas as pl
from jax.experimental.pallas import tpu as pltpu
from jax.sharding import PartitionSpec as P

DIM = 128
QT = 32
H = 256
HEADS = 4
HEAD = 64
MEMBERS = ("cent", "sub")
SMALL = 4


def exchange(values, axes):
    width = lax.axis_size(axes)
    if width > SMALL:
        return [lax.all_gather(values, axes, axis=0, tiled=True)]
    pieces = [values]
    for step in range(1, width):
        pieces.append(lax.ppermute(values, axes, [(i, i ^ step) for i in range(width)]))
    return pieces


def place(pieces, out_ref, axes):
    if len(pieces) == 1:
        out_ref[...] = pieces[0][...]
        return
    me = lax.axis_index(axes)
    for step, piece in enumerate(pieces):
        rows = piece.shape[0]
        start = pl.multiple_of(jnp.bitwise_xor(me, step) * rows, rows)
        out_ref[pl.ds(start, rows), :] = piece[...]


def pair_columns(shape, axis):
    wide = lax.broadcasted_iota(jnp.int32, shape, axis)
    dim = lax.broadcasted_iota(jnp.int32, shape, 1 - axis)
    wanted = 2 * jnp.bitwise_and(wide, 63) + jnp.right_shift(wide, 7)
    return jnp.where(wanted == dim, 1.0, 0.0).astype(jnp.bfloat16)


def score_kernel(n_pieces, block, ids, counts, codes, centroids, buckets, *refs):
    pieces, (out_ref, table, anchors, query_all, right) = refs[:n_pieces], refs[n_pieces:]
    docs, columns = codes.shape
    pairs = columns // DIM
    slots = 2 * pairs
    query_rows = query_all.shape[0]

    chunk = 256

    def widen(i, carry):
        start = pl.multiple_of(i * chunk, chunk)
        table[pl.ds(start, chunk), :] = centroids[pl.ds(start, chunk), :].astype(jnp.float32)
        return carry

    lax.fori_loop(0, centroids.shape[0] // chunk, widen, 0)

    def gather(p, carry):
        base = pl.multiple_of(p * docs, docs)
        for n in range(docs):
            row = ids[0, n * slots + p]
            anchors[pl.ds(base + n, 1), :] = table[pl.ds(row, 1), :]
        return carry

    lax.fori_loop(0, slots, gather, 0)

    place(pieces, query_all, MEMBERS)
    query_bf = query_all[...].astype(jnp.bfloat16)
    spread = pair_columns((DIM, 2 * DIM), 1)
    query_pair = jnp.dot(query_bf, spread, preferred_element_type=jnp.float32)
    lane = lax.broadcasted_iota(jnp.int32, (query_rows, 2 * DIM), 1)
    first = jnp.bitwise_and(lane, 64) == 0
    none = jnp.zeros((query_rows, DIM), jnp.bfloat16)
    right[:query_rows, :DIM] = query_bf
    right[:query_rows, DIM : 2 * DIM] = none
    right[:query_rows, 2 * DIM :] = jnp.where(first, query_pair, 0.0).astype(jnp.bfloat16)
    right[query_rows:, :DIM] = none
    right[query_rows:, DIM : 2 * DIM] = query_bf
    right[query_rows:, 2 * DIM :] = jnp.where(first, 0.0, query_pair).astype(jnp.bfloat16)

    levels = jnp.dot(
        buckets[...].astype(jnp.bfloat16), spread, preferred_element_type=jnp.float32
    )
    tables = [[levels[i : i + 8, k : k + DIM] for i in (0, 8)] for k in (0, DIM)]

    def look_up(nibbles, halves):
        index = jnp.bitwise_and(nibbles, 7)
        lower = jnp.take_along_axis(halves[0], index, axis=0)
        upper = jnp.take_along_axis(halves[1], index, axis=0)
        return jnp.where(nibbles >= 8, upper, lower)

    doc_row = lax.broadcasted_iota(jnp.int32, (docs, DIM), 0)
    live = jnp.zeros((docs, DIM), jnp.int32)
    for n in range(docs):
        live = jnp.where(doc_row == n, counts[0, n], live)
    live = jnp.concatenate([live] * (query_rows // DIM), axis=1)

    def score(i, best):
        lefts = []
        for k in range(block):
            pair = i * block + k
            column = pl.multiple_of(pair * DIM, DIM)
            lows, highs = [], []
            for b in range(docs // 8):
                code = codes[b * 8 : b * 8 + 8, pl.ds(column, DIM)]
                lows.append(look_up(jnp.bitwise_and(code, 15), tables[0]))
                highs.append(look_up(jnp.right_shift(code, 4), tables[1]))
            start = pl.multiple_of(pair * (2 * docs), 2 * docs)
            lefts.append(
                jnp.concatenate(
                    [
                        anchors[pl.ds(start, docs), :].astype(jnp.bfloat16),
                        anchors[pl.ds(start + docs, docs), :].astype(jnp.bfloat16),
                        jnp.concatenate(lows, axis=0).astype(jnp.bfloat16),
                        jnp.concatenate(highs, axis=0).astype(jnp.bfloat16),
                    ],
                    axis=1,
                )
            )
        left = jnp.concatenate(lefts, axis=0)
        scores = lax.dot_general(
            left, right[...], (((1,), (1,)), ((), ())), preferred_element_type=jnp.float32
        )
        for k in range(block):
            slot = 2 * (i * block + k)
            rows = scores[k * docs : (k + 1) * docs]
            best = jnp.maximum(best, jnp.where(live > slot, rows[:, :query_rows], -1e30))
            best = jnp.maximum(best, jnp.where(live > slot + 1, rows[:, query_rows:], -1e30))
        return best

    best = jnp.full((docs, query_rows), -1e30, jnp.float32)
    out_ref[...] = lax.fori_loop(0, pairs // block, score, best)


def vmem():
    return pl.BlockSpec(memory_space=pltpu.VMEM)


def smem():
    return pl.BlockSpec(memory_space=pltpu.SMEM)


def local_maxima(ids, counts, codes, centroids, buckets, pieces):
    docs, columns = codes.shape
    query_rows = sum(piece.shape[0] for piece in pieces)
    slots = 2 * columns // DIM
    block = 4
    return pl.pallas_call(
        functools.partial(score_kernel, len(pieces), block),
        out_shape=jax.ShapeDtypeStruct((docs, query_rows), jnp.float32),
        in_specs=[smem(), smem()] + [vmem()] * (3 + len(pieces)),
        out_specs=vmem(),
        scratch_shapes=[
            pltpu.VMEM(centroids.shape, jnp.float32),
            pltpu.VMEM((docs * slots, DIM), jnp.float32),
            pltpu.VMEM((query_rows, DIM), jnp.float32),
            pltpu.VMEM((2 * query_rows, 4 * DIM), jnp.bfloat16),
        ],
        compiler_params=pltpu.CompilerParams(vmem_limit_bytes=40 * 2**20),
        name="local_maxima",
    )(ids, counts, codes, centroids, buckets, *pieces)


def rms_scale(values, gain):
    mean_square = jnp.mean(values * values, axis=-1, keepdims=True)
    return (values * lax.rsqrt(mean_square + 1e-06) * gain).astype(jnp.bfloat16)


def product(left, right):
    return jnp.dot(left, right, preferred_element_type=jnp.float32)


def rerank_kernel(n_pieces, candidates, *refs):
    pieces, refs = refs[:n_pieces], refs[n_pieces:]
    (
        input_proj,
        gain_one,
        query_proj,
        key_proj,
        value_proj,
        output_proj,
        gain_two,
        up_proj,
        down_proj,
        out_ref,
        maxima,
        features,
        first,
        hidden,
        normed,
    ) = refs
    cand = candidates.shape[1]
    rows = out_ref.shape[0]
    place(pieces, maxima, "docs")

    unroll = 32

    def pick(i, carry):
        base = pl.multiple_of(i * unroll, unroll)
        for k in range(unroll):
            features[pl.ds(base + k, 1), :] = maxima[pl.ds(candidates[0, base + k], 1), :]
        return carry

    lax.fori_loop(0, cand // unroll, pick, 0)

    first[...] = jnp.zeros_like(first)
    start = pl.multiple_of(lax.axis_index("docs") * QT, QT)
    first[pl.ds(start, QT), :] = input_proj[...]
    all_hidden = jnp.dot(
        features[...],
        first[...],
        precision=lax.Precision.HIGHEST,
        preferred_element_type=jnp.float32,
    )
    all_normed = rms_scale(all_hidden, gain_one[...])
    hidden[...] = all_hidden
    normed[...] = all_normed
    mine = pl.multiple_of(lax.axis_index(MEMBERS) * rows, rows)
    hidden_zero = hidden[pl.ds(mine, rows), :]
    query_heads = product(normed[pl.ds(mine, rows), :], query_proj[...]).astype(jnp.bfloat16)
    key_heads = product(all_normed, key_proj[...]).astype(jnp.bfloat16)
    value_heads = product(all_normed, value_proj[...]).astype(jnp.bfloat16)
    heads = []
    for h in range(HEADS):
        cut = slice(h * HEAD, (h + 1) * HEAD)
        scores = lax.dot_general(
            query_heads[:, cut],
            key_heads[:, cut],
            (((1,), (1,)), ((), ())),
            preferred_element_type=jnp.float32,
        ) * (HEAD ** (-0.5))
        expon = jnp.exp(scores - jnp.max(scores, axis=-1, keepdims=True))
        summed = jnp.sum(expon, axis=-1, keepdims=True)
        heads.append(product(expon.astype(jnp.bfloat16), value_heads[:, cut]) / summed)
    attended = jnp.concatenate(heads, axis=1).astype(jnp.bfloat16)
    hidden_one = hidden_zero + product(attended, output_proj[...])
    normed_two = rms_scale(hidden_one, gain_two[...])
    inner = jax.nn.gelu(product(normed_two, up_proj[...])).astype(jnp.bfloat16)
    out_ref[...] = hidden_one + product(inner, down_proj[...])


def rerank(candidates, pieces, weights, rows):
    docs_all = sum(piece.shape[0] for piece in pieces)
    query_rows = pieces[0].shape[1]
    cand = candidates.shape[1]
    return pl.pallas_call(
        functools.partial(rerank_kernel, len(pieces)),
        out_shape=jax.ShapeDtypeStruct((rows, H), jnp.float32),
        in_specs=[smem()] + [vmem()] * (len(pieces) + len(weights)),
        out_specs=vmem(),
        scratch_shapes=[
            pltpu.VMEM((docs_all, query_rows), jnp.float32),
            pltpu.VMEM((cand, query_rows), jnp.float32),
            pltpu.VMEM((query_rows, H), jnp.float32),
            pltpu.VMEM((cand, H), jnp.float32),
            pltpu.VMEM((cand, H), jnp.bfloat16),
        ],
        compiler_params=pltpu.CompilerParams(vmem_limit_bytes=40 * 2**20),
        name="rerank",
    )(candidates, *pieces, *weights)


def on_device(
    queries,
    token_codes,
    centroid_ids,
    slot_counts,
    centroids,
    bucket_values,
    candidates,
    input_proj,
    gain_one,
    query_proj,
    key_proj,
    value_proj,
    output_proj,
    gain_two,
    up_proj,
    down_proj,
):
    query_pieces = exchange(queries, MEMBERS)
    local_best = local_maxima(
        centroid_ids, slot_counts, token_codes[0], centroids, bucket_values, query_pieces
    )
    if lax.axis_size(MEMBERS) > SMALL:
        doc_best = lax.pmax(local_best, MEMBERS)
    else:
        doc_best = functools.reduce(jnp.maximum, exchange(local_best, MEMBERS))
    doc_pieces = exchange(doc_best, "docs")
    rows = candidates.shape[1] // lax.axis_size(MEMBERS)
    weights = (
        input_proj,
        gain_one[None, :],
        query_proj,
        key_proj,
        value_proj,
        output_proj,
        gain_two[None, :],
        up_proj,
        down_proj,
    )
    return rerank(candidates, doc_pieces, weights, rows)[None]


def solution(mesh):
    in_specs = (
        P(("groups", "cent", "sub"), None),
        P(("cent", "sub"), ("groups", "docs"), None),
        P(("cent", "sub"), ("groups", "docs")),
        P(("cent", "sub"), ("groups", "docs")),
        P(("cent", "sub"), None),
        P(),
        P(("groups", "docs"), None),
        P(),
        P(),
        P(),
        P(),
        P(),
        P(),
        P(),
        P(),
        P(),
    )
    out_specs = P(("groups", "docs"), ("cent", "sub"), None)
    return jax.shard_map(
        on_device, mesh=mesh, in_specs=in_specs, out_specs=out_specs, check_vma=False
    )
```

time: 184 us -> 36.7 us (0.20)
  local copies, waits for them, and re-layouts: 105 us -> 5.22 us
  other arithmetic: 35.7 us -> 0.01 us
  blocking collectives: 18.8 us -> 0 us
  matrix products: 13.6 us -> 0 us
  Pallas kernels: 0 us -> 11.9 us
  starting transfers between devices: 4.87 us -> 10 us
  waiting for transfers between devices: 4.27 us -> 9.07 us
    eq x64 -> x0, local copies, waits for them, and re-layouts: 80.4 us -> none  [dequantize(): nibbles == level_id]
    eq x4 -> x0, other arithmetic: 25.7 us -> none  [dequantize(): nibbles == level_id]
    dot_general x10 -> x0, matrix products: 13.6 us -> none  [the longest x2 8.36 us: block_maxima(): lax.dot_general(embedded, query_bf, (((1,), (1,)), ((), ())), preferred_e...]
    gather x4 -> x0, local copies, waits for them, and re-layouts: 13.2 us -> none  [the longest x2 12.4 us: dequantize(): anchor = jnp.take(centroid_table, cent_rows, axis=0).astype(jnp.float32)]
    pmax x1 -> x0, blocking collectives: 12.6 us -> none  [on_device(): doc_best = lax.pmax(local_best, ('cent', 'sub'))]
    pallas_call x0 -> x2, Pallas kernels: none -> 11.9 us  [the longest x1 8.69 us: local_maxima(): pl.pallas_call(functools.partial(score_kernel, len(pieces), block), out_s...]
    ppermute x0 -> x9, starting transfers between devices: none -> 10 us  [exchange(): lax.ppermute(values, axes, [(i, i ^ step) for i in range(width)])]
    ppermute x0 -> x9, waiting for transfers between devices: none -> 9.07 us  [exchange(): lax.ppermute(values, axes, [(i, i ^ step) for i in range(width)])]
  transfers between devices with their start and end apart: 1 -> 9, of which waited for: 1 -> 6; matrix products, arithmetic and copies ran while one was open for 1% -> 0% of each run, Pallas kernels for 0% -> 0%
where the time goes in v1:
time: 36.7 us; the launch traced here: 36.3 us
  Pallas kernels  11.9 us (32%)
  starting transfers between devices  10 us (27%)
  waiting for transfers between devices  9.07 us (25%)
  local copies, waits for them, and re-layouts  5.22 us (14%)
    ppermute x9, starting transfers between devices, exchange(): lax.ppermute(values, axes, [(i, i ^ step) for i in range(width)])  10 us
    ppermute x9, waiting for transfers between devices, exchange(): lax.ppermute(values, axes, [(i, i ^ step) for i in range(width)])  9.07 us
    pallas_call x1, Pallas kernels, local_maxima(): pl.pallas_call(functools.partial(score_kernel, len(pieces), block), out_s...  8.69 us
    unnamed x32, local copies, waits for them, and re-layouts  5.22 us
    pallas_call x1, Pallas kernels, rerank(): pl.pallas_call(functools.partial(rerank_kernel, len(pieces)), out_shape=j...  3.16 us
  transfers between devices with their start and end apart: 9, of which 6 were waited for; matrix products, arithmetic and copies ran while one was open for 0% of the time, Pallas kernels for 0%

profile of v1, /device:TPU:0, one launch (start us, length us, event | category | flops | bytes accessed | tf_op | source)
XLA Modules:
  0.0 36.3 jit_solution(16249775634147567585)
XLA Ops:
  0.0 2.9 %collective-permute-start.1 = (f32[32,128]{1,0:T(8,128)}, f32[32,128]{1,0:T(8,128)S(1)}, u32[]{:S(2)}, u32[]{:S(2)}) collective-permute-start(f32[32,128]{1,0:T(8,128)} %refs_0_.1), channel_id=1, source_target_pairs={{0,2},{1,3},{2,0},{3,1},{4,6},{5,7},{6,4},{7,5},{8,10},{9,11},{10,... | collective-permute-start | bytes 49160 | tf_op jit(solution)/shard_map/ppermute | solution.py:25
  2.9 0.0 collective-permute-start
  2.9 0.2 collective-permute-start.2
  3.1 1.7 %collective-permute-done.1.refs_2_ = f32[32,128]{1,0:T(8,128)S(1)} collective-permute-done((f32[32,128]{1,0:T(8,128)}, f32[32,128]{1,0:T(8,128)S(1)}, u32[]{:S(2)}, u32[]{:S(2)}) %collective-permute-start.1) | collective-permute-done | bytes 16416 | tf_op jit(solution)/shard_map/ppermute | solution.py:25
  4.9 0.0 collective-permute-done.refs_1_
  4.9 1.4 %collective-permute-done.2.refs_3_ = f32[32,128]{1,0:T(8,128)S(1)} collective-permute-done((f32[32,128]{1,0:T(8,128)}, f32[32,128]{1,0:T(8,128)S(1)}, u32[]{:S(2)}, u32[]{:S(2)}) %collective-permute-start.2) | collective-permute-done | bytes 16416 | tf_op jit(solution)/shard_map/ppermute | solution.py:25
  6.3 0.0 copy-done.14
  6.3 1.2 %copy-done = s32[1,32,8192]{2,1,0:T(8,128)S(1)} copy-done((s32[1,32,8192]{2,1,0:T(8,128)S(1)}, s32[1,32,8192]{2,1,0:T(8,128)}, u32[]{:S(2)}) %copy-start) | copy-done | bytes 1048600
  7.6 1.2 %copy-done.1 = bf16[4096,128]{1,0:T(8,128)(2,1)S(1)} copy-done((bf16[4096,128]{1,0:T(8,128)(2,1)S(1)}, bf16[4096,128]{1,0:T(8,128)(2,1)}, u32[]{:S(2)}) %copy-start.1) | copy-done | bytes 1048600
  8.8 0.7 %copy-done.9 = s32[1,4096]{1,0:T(1,128)S(1)} copy-done((s32[1,4096]{1,0:T(1,128)S(1)}, s32[1,4096]{1,0:T(1,128)}, u32[]{:S(2)}) %copy-start.9) | copy-done | bytes 16408
  9.5 0.7 %copy-done.10 = f32[32,128]{1,0:T(8,128)S(1)} copy-done((f32[32,128]{1,0:T(8,128)S(1)}, f32[32,128]{1,0:T(8,128)}, u32[]{:S(2)}) %copy-start.10) | copy-done | bytes 16408
  10.2 0.7 %copy-done.11 = f32[16,128]{1,0:T(8,128)S(1)} copy-done((f32[16,128]{1,0:T(8,128)S(1)}, f32[16,128]{1,0:T(8,128)}, u32[]{:S(2)}) %copy-start.11) | copy-done | bytes 8216
  10.9 0.0 copy-start.6
  10.9 0.0 copy-start.7
  10.9 8.7 %local_maxima.1 = f32[32,128]{1,0:T(8,128)S(1)} custom-call(s32[1,4096]{1,0:T(1,128)S(1)} %copy-done.9, s32[1,32]{1,0:T(1,128)S(1)} %copy-done.14, s32[32,8192]{1,0:T(8,128)S(1)} %bitcast.4, bf16[4096,128]{1,0:T(8,128)(2,1)S(1)} %copy-done.1, f32[16,128]{1,0:T(8,128)S(1)} %copy-done.11, f32[32,128]{1,0:T(8,128)S(1)} %copy-done.10, ...), custom_call_target="tpu_custom_call" | custom-call | tf_op jit(solution)/shard_map/local_maxima/pallas_call | solution.py:153
  19.6 0.0 copy-start.8
  19.7 0.4 collective-permute-start.5
  20.0 1.8 %collective-permute-start.4 = (f32[32,128]{1,0:T(8,128)S(1)}, f32[32,128]{1,0:T(8,128)S(1)}, u32[]{:S(2)}, u32[]{:S(2)}) collective-permute-start(f32[32,128]{1,0:T(8,128)S(1)} %local_maxima.1), channel_id=1, source_target_pairs={{0,2},{1,3},{2,0},{3,1},{4,6},{5,7},{6,4},{7,5},{8,10},{9,11},{10,... | collective-permute-start | bytes 49160 | tf_op jit(solution)/shard_map/ppermute | solution.py:25
  21.9 0.0 collective-permute-start.3
  21.9 1.0 %collective-permute-done.5 = f32[32,128]{1,0:T(8,128)S(1)} collective-permute-done((f32[32,128]{1,0:T(8,128)S(1)}, f32[32,128]{1,0:T(8,128)S(1)}, u32[]{:S(2)}, u32[]{:S(2)}) %collective-permute-start.5) | collective-permute-done | bytes 16416 | tf_op jit(solution)/shard_map/ppermute | solution.py:25
  22.9 0.9 %collective-permute-done.4 = f32[32,128]{1,0:T(8,128)S(1)} collective-permute-done((f32[32,128]{1,0:T(8,128)S(1)}, f32[32,128]{1,0:T(8,128)S(1)}, u32[]{:S(2)}, u32[]{:S(2)}) %collective-permute-start.4) | collective-permute-done | bytes 16416 | tf_op jit(solution)/shard_map/ppermute | solution.py:25
  23.8 0.0 collective-permute-done.3
  23.8 4.0 %collective-permute-start.8 = (f32[32,128]{1,0:T(8,128)S(1)}, f32[32,128]{1,0:T(8,128)S(1)}, u32[]{:S(2)}, u32[]{:S(2)}) collective-permute-start(f32[32,128]{1,0:T(8,128)S(1)} %maximum_maximum_fusion.refs_0_), channel_id=1, source_target_pairs={{0,12},{4,8},{8,4},{12,0},{1,13},{5,9},{9,5},{13,1},{2,14},{6,10},... | collective-permute-start | bytes 49160 | tf_op jit(solution)/shard_map/ppermute | solution.py:25
  27.8 0.0 collective-permute-start.7
  27.8 0.6 %collective-permute-start.6 = (f32[32,128]{1,0:T(8,128)S(1)}, f32[32,128]{1,0:T(8,128)S(1)}, u32[]{:S(2)}, u32[]{:S(2)}) collective-permute-start(f32[32,128]{1,0:T(8,128)S(1)} %maximum_maximum_fusion.refs_0_), channel_id=1, source_target_pairs={{0,4},{4,0},{8,12},{12,8},{1,5},{5,1},{9,13},{13,9},{2,6},{6,2},{1... | collective-permute-start | bytes 49160 | tf_op jit(solution)/shard_map/ppermute | solution.py:25
  28.4 1.3 %collective-permute-done.8.refs_3_ = f32[32,128]{1,0:T(8,128)S(1)} collective-permute-done((f32[32,128]{1,0:T(8,128)S(1)}, f32[32,128]{1,0:T(8,128)S(1)}, u32[]{:S(2)}, u32[]{:S(2)}) %collective-permute-start.8) | collective-permute-done | bytes 16416 | tf_op jit(solution)/shard_map/ppermute | solution.py:25
  29.7 2.7 %collective-permute-done.7.refs_2_ = f32[32,128]{1,0:T(8,128)S(1)} collective-permute-done((f32[32,128]{1,0:T(8,128)S(1)}, f32[32,128]{1,0:T(8,128)S(1)}, u32[]{:S(2)}, u32[]{:S(2)}) %collective-permute-start.7) | collective-permute-done | bytes 16416 | tf_op jit(solution)/shard_map/ppermute | solution.py:25
  32.4 0.0 collective-permute-done.6.refs_1_
  32.4 0.0 copy-done.2
  32.5 0.6 %copy-done.12 = f32[256]{0:T(256)S(1)} copy-done((f32[256]{0:T(256)S(1)}, f32[256]{0:T(256)}, u32[]{:S(2)}) %copy-start.12) | copy-done | bytes 1048
  33.1 0.0 copy-done.15
  33.1 3.2 %rerank.1 = f32[16,256]{1,0:T(8,128)} custom-call(s32[1,64]{1,0:T(1,128)S(1)} %copy-done.15, f32[32,128]{1,0:T(8,128)S(1)} %maximum_maximum_fusion.refs_0_, f32[32,128]{1,0:T(8,128)S(1)} %collective-permute-done.6.refs_1_, f32[32,128]{1,0:T(8,128)S(1)} %collective-permute-done.7.refs_2_, f32[32,128]{1,0:T(8,128)S(1)} %collective-permute-done.8.refs_3_, ...), custom_call_target="tpu_custom_call" | custom-call | tf_op jit(solution)/shard_map/rerank/pallas_call | solution.py:251
  (21 shorter events, 0.0 us)
Async XLA Ops:
  0.0 6.3 %copy-start.14 = (s32[1,32]{1,0:T(1,128)S(1)}, s32[1,32]{1,0:T(1,128)}, u32[]{:S(2)}) copy-start(s32[1,32]{1,0:T(1,128)} %counts.1) | copy-start | bytes 388
  0.0 4.9 %collective-permute-start.1 = (f32[32,128]{1,0:T(8,128)}, f32[32,128]{1,0:T(8,128)S(1)}, u32[]{:S(2)}, u32[]{:S(2)}) collective-permute-start(f32[32,128]{1,0:T(8,128)} %refs_0_.1), channel_id=1, source_target_pairs={{0,2},{1,3},{2,0},{3,1},{4,6},{5,7},{6,4},{7,5},{8,10},{9,11},{10,... | collective-permute-start | bytes 49160 | tf_op jit(solution)/shard_map/ppermute | solution.py:25
  2.9 1.9 %collective-permute-start = (f32[32,128]{1,0:T(8,128)}, f32[32,128]{1,0:T(8,128)S(1)}, u32[]{:S(2)}, u32[]{:S(2)}) collective-permute-start(f32[32,128]{1,0:T(8,128)} %refs_0_.1), channel_id=1, source_target_pairs={{0,1},{1,0},{2,3},{3,2},{4,5},{5,4},{6,7},{7,6},{8,9},{9,8},{10,11... | collective-permute-start | bytes 49160 | tf_op jit(solution)/shard_map/ppermute | solution.py:25
  2.9 3.4 %collective-permute-start.2 = (f32[32,128]{1,0:T(8,128)}, f32[32,128]{1,0:T(8,128)S(1)}, u32[]{:S(2)}, u32[]{:S(2)}) collective-permute-start(f32[32,128]{1,0:T(8,128)} %refs_0_.1), channel_id=1, source_target_pairs={{0,3},{1,2},{2,1},{3,0},{4,7},{5,6},{6,5},{7,4},{8,11},{9,10},{10,... | collective-permute-start | bytes 49160 | tf_op jit(solution)/shard_map/ppermute | solution.py:25
  6.3 1.2 %copy-start = (s32[1,32,8192]{2,1,0:T(8,128)S(1)}, s32[1,32,8192]{2,1,0:T(8,128)}, u32[]{:S(2)}) copy-start(s32[1,32,8192]{2,1,0:T(8,128)} %param.17) | copy-start | bytes 3145732
  7.5 1.2 %copy-start.1 = (bf16[4096,128]{1,0:T(8,128)(2,1)S(1)}, bf16[4096,128]{1,0:T(8,128)(2,1)}, u32[]{:S(2)}) copy-start(bf16[4096,128]{1,0:T(8,128)(2,1)} %centroids.1) | copy-start | bytes 3145732
  8.8 0.7 %copy-start.9 = (s32[1,4096]{1,0:T(1,128)S(1)}, s32[1,4096]{1,0:T(1,128)}, u32[]{:S(2)}) copy-start(s32[1,4096]{1,0:T(1,128)} %ids.1) | copy-start | bytes 49156
  9.5 0.7 %copy-start.10 = (f32[32,128]{1,0:T(8,128)S(1)}, f32[32,128]{1,0:T(8,128)}, u32[]{:S(2)}) copy-start(f32[32,128]{1,0:T(8,128)} %refs_0_.1) | copy-start | bytes 49156
  10.2 0.7 %copy-start.11 = (f32[16,128]{1,0:T(8,128)S(1)}, f32[16,128]{1,0:T(8,128)}, u32[]{:S(2)}) copy-start(f32[16,128]{1,0:T(8,128)} %buckets.1) | copy-start | bytes 24580
  10.9 21.5 %copy-start.2 = (bf16[256,1024]{1,0:T(8,128)(2,1)S(1)}, bf16[256,1024]{1,0:T(8,128)(2,1)}, u32[]{:S(2)}) copy-start(bf16[256,1024]{1,0:T(8,128)(2,1)} %refs_11_.1) | copy-start | bytes 1572868
  10.9 21.5 %copy-start.3 = (bf16[1024,256]{1,0:T(8,128)(2,1)S(1)}, bf16[1024,256]{1,0:T(8,128)(2,1)}, u32[]{:S(2)}) copy-start(bf16[1024,256]{1,0:T(8,128)(2,1)} %refs_12_.1) | copy-start | bytes 1572868
  10.9 21.5 %copy-start.4 = (bf16[256,256]{1,0:T(8,128)(2,1)S(1)}, bf16[256,256]{1,0:T(8,128)(2,1)}, u32[]{:S(2)}) copy-start(bf16[256,256]{1,0:T(8,128)(2,1)} %refs_6_.1) | copy-start | bytes 393220
  10.9 21.6 %copy-start.5 = (bf16[256,256]{1,0:T(8,128)(2,1)S(1)}, bf16[256,256]{1,0:T(8,128)(2,1)}, u32[]{:S(2)}) copy-start(bf16[256,256]{1,0:T(8,128)(2,1)} %refs_7_.1) | copy-start | bytes 393220
  10.9 21.6 %copy-start.6 = (bf16[256,256]{1,0:T(8,128)(2,1)S(1)}, bf16[256,256]{1,0:T(8,128)(2,1)}, u32[]{:S(2)}) copy-start(bf16[256,256]{1,0:T(8,128)(2,1)} %refs_8_.1) | copy-start | bytes 393220
  10.9 21.6 %copy-start.7 = (bf16[256,256]{1,0:T(8,128)(2,1)S(1)}, bf16[256,256]{1,0:T(8,128)(2,1)}, u32[]{:S(2)}) copy-start(bf16[256,256]{1,0:T(8,128)(2,1)} %refs_9_.1) | copy-start | bytes 393220
  19.6 12.9 %copy-start.8 = (f32[32,256]{1,0:T(8,128)S(1)}, f32[32,256]{1,0:T(8,128)}, u32[]{:S(2)}) copy-start(f32[32,256]{1,0:T(8,128)} %refs_4_.1) | copy-start | bytes 98308
  19.7 3.2 %collective-permute-start.5 = (f32[32,128]{1,0:T(8,128)S(1)}, f32[32,128]{1,0:T(8,128)S(1)}, u32[]{:S(2)}, u32[]{:S(2)}) collective-permute-start(f32[32,128]{1,0:T(8,128)S(1)} %local_maxima.1), channel_id=1, source_target_pairs={{0,3},{1,2},{2,1},{3,0},{4,7},{5,6},{6,5},{7,4},{8,11},{9,10},{10,... | collective-permute-start | bytes 49160 | tf_op jit(solution)/shard_map/ppermute | solution.py:25
  20.0 3.7 %collective-permute-start.4 = (f32[32,128]{1,0:T(8,128)S(1)}, f32[32,128]{1,0:T(8,128)S(1)}, u32[]{:S(2)}, u32[]{:S(2)}) collective-permute-start(f32[32,128]{1,0:T(8,128)S(1)} %local_maxima.1), channel_id=1, source_target_pairs={{0,2},{1,3},{2,0},{3,1},{4,6},{5,7},{6,4},{7,5},{8,10},{9,11},{10,... | collective-permute-start | bytes 49160 | tf_op jit(solution)/shard_map/ppermute | solution.py:25
  21.9 1.9 %collective-permute-start.3 = (f32[32,128]{1,0:T(8,128)S(1)}, f32[32,128]{1,0:T(8,128)S(1)}, u32[]{:S(2)}, u32[]{:S(2)}) collective-permute-start(f32[32,128]{1,0:T(8,128)S(1)} %local_maxima.1), channel_id=1, source_target_pairs={{0,1},{1,0},{2,3},{3,2},{4,5},{5,4},{6,7},{7,6},{8,9},{9,8},{10,11... | collective-permute-start | bytes 49160 | tf_op jit(solution)/shard_map/ppermute | solution.py:25
  23.8 8.7 %copy-start.13 = (f32[256]{0:T(256)S(1)}, f32[256]{0:T(256)}, u32[]{:S(2)}) copy-start(f32[256]{0:T(256)} %param.29) | copy-start | bytes 3076
  23.8 6.0 %collective-permute-start.8 = (f32[32,128]{1,0:T(8,128)S(1)}, f32[32,128]{1,0:T(8,128)S(1)}, u32[]{:S(2)}, u32[]{:S(2)}) collective-permute-start(f32[32,128]{1,0:T(8,128)S(1)} %maximum_maximum_fusion.refs_0_), channel_id=1, source_target_pairs={{0,12},{4,8},{8,4},{12,0},{1,13},{5,9},{9,5},{13,1},{2,14},{6,10},... | collective-permute-start | bytes 49160 | tf_op jit(solution)/shard_map/ppermute | solution.py:25
  27.8 4.6 %collective-permute-start.7 = (f32[32,128]{1,0:T(8,128)S(1)}, f32[32,128]{1,0:T(8,128)S(1)}, u32[]{:S(2)}, u32[]{:S(2)}) collective-permute-start(f32[32,128]{1,0:T(8,128)S(1)} %maximum_maximum_fusion.refs_0_), channel_id=1, source_target_pairs={{0,8},{4,12},{8,0},{12,4},{1,9},{5,13},{9,1},{13,5},{2,10},{6,14},... | collective-permute-start | bytes 49160 | tf_op jit(solution)/shard_map/ppermute | solution.py:25
  27.8 4.6 %collective-permute-start.6 = (f32[32,128]{1,0:T(8,128)S(1)}, f32[32,128]{1,0:T(8,128)S(1)}, u32[]{:S(2)}, u32[]{:S(2)}) collective-permute-start(f32[32,128]{1,0:T(8,128)S(1)} %maximum_maximum_fusion.refs_0_), channel_id=1, source_target_pairs={{0,4},{4,0},{8,12},{12,8},{1,5},{5,1},{9,13},{13,9},{2,6},{6,2},{1... | collective-permute-start | bytes 49160 | tf_op jit(solution)/shard_map/ppermute | solution.py:25
  32.4 0.7 %copy-start.12 = (f32[256]{0:T(256)S(1)}, f32[256]{0:T(256)}, u32[]{:S(2)}) copy-start(f32[256]{0:T(256)} %param.24) | copy-start | bytes 3076
  32.4 0.7 %copy-start.15 = (s32[1,64]{1,0:T(1,128)S(1)}, s32[1,64]{1,0:T(1,128)}, u32[]{:S(2)}) copy-start(s32[1,64]{1,0:T(1,128)} %candidates.1) | copy-start | bytes 772

commit v2 on v1

v2 whole, which is shorter than its diff:
```python
import functools

import jax
import jax.numpy as jnp
from jax import lax
from jax.experimental import pallas as pl
from jax.experimental.pallas import tpu as pltpu
from jax.sharding import PartitionSpec as P

DIM = 128
QT = 32
H = 256
HEADS = 4
HEAD = 64
MEMBERS = ("cent", "sub")
NOTHING = -1e30
DOC_STEPS = ((2, 3, 1, 0), (3, 2, 0, 1), (1, 0, 3, 2))


def compact():
    return (
        lax.axis_size("cent") == 2
        and lax.axis_size("sub") == 2
        and lax.axis_size("docs") == len(DOC_STEPS) + 1
    )


def gather_queries(queries):
    if not compact():
        return [lax.all_gather(queries, MEMBERS, axis=0, tiled=True)], [None]
    pieces, sources = [queries], [[0, 1, 2, 3]]
    for step in (1, 2, 3):
        sources.append([i ^ step for i in range(4)])
        pieces.append(lax.ppermute(queries, MEMBERS, [(i, i ^ step) for i in range(4)]))
    return pieces, sources


def best_of_members(values):
    if not compact():
        return lax.pmax(values, MEMBERS)
    values = jnp.maximum(values, lax.ppermute(values, "sub", [(0, 1), (1, 0)]))
    return jnp.maximum(values, lax.ppermute(values, MEMBERS, [(i, i ^ 3) for i in range(4)]))


def gather_docs(values):
    if not compact():
        return [lax.all_gather(values, "docs", axis=0, tiled=True)], [None]
    pieces, sources = [values], [[0, 1, 2, 3]]
    for step in reversed(DOC_STEPS):
        pairs = [(2 * d + c, 2 * step[d] + 1 - c) for d in range(4) for c in range(2)]
        pieces.append(lax.ppermute(values, ("docs", "sub"), pairs))
        sources.append([step.index(d) for d in range(4)])
    return pieces, sources


def place(pieces, sources, out_ref, axes):
    if len(pieces) == 1:
        out_ref[...] = pieces[0][...]
        return
    me = lax.axis_index(axes)
    for piece, source in zip(pieces, sources):
        rows = piece.shape[0]
        place_of = jnp.int32(source[0])
        for i in range(1, len(source)):
            place_of = jnp.where(me == i, source[i], place_of)
        start = pl.multiple_of(place_of * rows, rows)
        out_ref[pl.ds(start, rows), :] = piece[...]


def vmem():
    return pl.BlockSpec(memory_space=pltpu.VMEM)


def smem():
    return pl.BlockSpec(memory_space=pltpu.SMEM)


def hbm():
    return pl.BlockSpec(memory_space=pltpu.HBM)


def in_hbm(array):
    return pltpu.with_memory_space_constraint(array, pltpu.HBM)


def even_odd_columns():
    wide = lax.broadcasted_iota(jnp.int32, (DIM, 2 * DIM), 1)
    dim = lax.broadcasted_iota(jnp.int32, (DIM, 2 * DIM), 0)
    wanted = 2 * jnp.bitwise_and(wide, 63) + jnp.right_shift(wide, 7)
    return jnp.where(wanted == dim, 1.0, 0.0).astype(jnp.bfloat16)


def look_up(nibbles, halves):
    index = jnp.bitwise_and(nibbles, 7)
    lower = jnp.take_along_axis(halves[0], index, axis=0)
    upper = jnp.take_along_axis(halves[1], index, axis=0)
    return jnp.where(nibbles >= 8, upper, lower)


def prepare_kernel(n_kept, ids_hbm, counts_hbm, codes_hbm, centroids_hbm, buckets_hbm, *refs):
    kept_hbm, refs = refs[:n_kept], refs[n_kept:]
    left, live, spread = refs[:3]
    kept, refs = refs[3 : 3 + n_kept], refs[3 + n_kept :]
    ids, counts, codes, centroids, buckets, table, anchors, sems, kept_sems = refs
    docs, columns = codes.shape
    pairs = columns // DIM
    slots = 2 * pairs

    copies = [
        pltpu.make_async_copy(source, target, sems.at[i])
        for i, (source, target) in enumerate(
            (
                (centroids_hbm, centroids),
                (ids_hbm, ids),
                (buckets_hbm, buckets),
                (counts_hbm, counts),
                (codes_hbm, codes),
            )
        )
    ]
    copies += [
        pltpu.make_async_copy(source, target, kept_sems.at[i])
        for i, (source, target) in enumerate(zip(kept_hbm, kept))
    ]
    for copy in copies:
        copy.start()
    columns_of = even_odd_columns()
    spread[...] = columns_of

    copies[2].wait()
    levels = jnp.dot(
        buckets[...].astype(jnp.bfloat16), columns_of, preferred_element_type=jnp.float32
    )
    tables = [[levels[i : i + 8, k : k + DIM] for i in (0, 8)] for k in (0, DIM)]

    copies[0].wait()
    chunk = 512

    def widen(i, carry):
        start = pl.multiple_of(i * chunk, chunk)
        table[pl.ds(start, chunk), :] = centroids[pl.ds(start, chunk), :].astype(jnp.float32)
        return carry

    lax.fori_loop(0, centroids.shape[0] // chunk, widen, 0)

    copies[1].wait()
    copies[3].wait()
    doc_row = lax.broadcasted_iota(jnp.int32, (8, DIM), 0)
    for b in range(docs // 8):
        block = jnp.zeros((8, DIM), jnp.int32)
        for n in range(8):
            block = jnp.where(doc_row == n, counts[0, b * 8 + n], block)
        live[b * 8 : b * 8 + 8, :] = block

    copies[4].wait()
    for pair in range(pairs):
        start = pair * docs
        for k in range(2):

            def fetch(n, carry, first=2 * start + k * docs, slot=2 * pair + k):
                row = ids[0, n * slots + slot]
                anchors[pl.ds(first + n, 1), :] = table[pl.ds(row, 1), :]
                return carry

            lax.fori_loop(0, docs, fetch, 0, unroll=True)
        lows, highs = [], []
        for b in range(docs // 8):
            code = codes[b * 8 : b * 8 + 8, pair * DIM : (pair + 1) * DIM]
            lows.append(look_up(jnp.bitwise_and(code, 15), tables[0]))
            highs.append(look_up(jnp.right_shift(code, 4), tables[1]))
        rows = slice(start, start + docs)
        left[rows, 2 * DIM : 3 * DIM] = jnp.concatenate(lows, axis=0).astype(jnp.bfloat16)
        left[rows, 3 * DIM :] = jnp.concatenate(highs, axis=0).astype(jnp.bfloat16)
        for k in range(2):
            found = anchors[2 * start + k * docs : 2 * start + (k + 1) * docs, :]
            left[rows, k * DIM : (k + 1) * DIM] = found.astype(jnp.bfloat16)
    for copy in copies[5:]:
        copy.wait()


def prepare(ids, counts, codes, centroids, buckets, kept):
    docs, columns = codes.shape
    pairs = columns // DIM
    shape = jax.ShapeDtypeStruct
    return pl.pallas_call(
        functools.partial(prepare_kernel, len(kept)),
        out_shape=[
            shape((pairs * docs, 4 * DIM), jnp.bfloat16),
            shape((docs, DIM), jnp.int32),
            shape((DIM, 2 * DIM), jnp.bfloat16),
        ]
        + [shape(array.shape, array.dtype) for array in kept],
        in_specs=[hbm()] * (5 + len(kept)),
        out_specs=[vmem()] * (3 + len(kept)),
        scratch_shapes=[
            pltpu.SMEM(ids.shape, jnp.int32),
            pltpu.SMEM(counts.shape, jnp.int32),
            pltpu.VMEM(codes.shape, jnp.int32),
            pltpu.VMEM(centroids.shape, jnp.bfloat16),
            pltpu.VMEM(buckets.shape, jnp.float32),
            pltpu.VMEM(centroids.shape, jnp.float32),
            pltpu.VMEM((2 * pairs * docs, DIM), jnp.float32),
            pltpu.SemaphoreType.DMA((5,)),
            pltpu.SemaphoreType.DMA((len(kept),)),
        ],
        compiler_params=pltpu.CompilerParams(vmem_limit_bytes=24 * 2**20),
        cost_estimate=pl.CostEstimate(flops=4 * 10**9, bytes_accessed=2**22, transcendentals=0),
        name="prepare",
    )(*[in_hbm(x) for x in (ids, counts, codes, centroids, buckets, *kept)])


def score_kernel(sources, docs, left, live, spread, *refs):
    pieces, (out_ref, queries, right) = refs[: len(sources)], refs[len(sources) :]
    query_rows = queries.shape[0]
    pairs = left.shape[0] // docs
    place(pieces, sources, queries, MEMBERS)
    query_bf = queries[...].astype(jnp.bfloat16)
    query_pair = jnp.dot(query_bf, spread[...], preferred_element_type=jnp.float32)
    lane = lax.broadcasted_iota(jnp.int32, (query_rows, 2 * DIM), 1)
    first = jnp.bitwise_and(lane, 64) == 0
    none = jnp.zeros((query_rows, DIM), jnp.bfloat16)
    right[:query_rows, :DIM] = query_bf
    right[:query_rows, DIM : 2 * DIM] = none
    right[:query_rows, 2 * DIM :] = jnp.where(first, query_pair, 0.0).astype(jnp.bfloat16)
    right[query_rows:, :DIM] = none
    right[query_rows:, DIM : 2 * DIM] = query_bf
    right[query_rows:, 2 * DIM :] = jnp.where(first, 0.0, query_pair).astype(jnp.bfloat16)

    counts = jnp.concatenate([live[...]] * (query_rows // DIM), axis=1)
    block = pairs if query_rows == DIM else 4

    def score(i, best):
        start = pl.multiple_of(i * block * docs, block * docs)
        scores = lax.dot_general(
            left[pl.ds(start, block * docs), :],
            right[...],
            (((1,), (1,)), ((), ())),
            preferred_element_type=jnp.float32,
        )
        for k in range(block):
            slot = 2 * (i * block + k)
            rows = scores[k * docs : (k + 1) * docs]
            best = jnp.maximum(best, jnp.where(counts > slot, rows[:, :query_rows], NOTHING))
            best = jnp.maximum(best, jnp.where(counts > slot + 1, rows[:, query_rows:], NOTHING))
        return best

    best = jnp.full((docs, query_rows), NOTHING, jnp.float32)
    if block == pairs:
        out_ref[...] = score(0, best)
    else:
        out_ref[...] = lax.fori_loop(0, pairs // block, score, best)


def local_maxima(left, live, spread, pieces, sources):
    docs = live.shape[0]
    query_rows = sum(piece.shape[0] for piece in pieces)
    return pl.pallas_call(
        functools.partial(score_kernel, sources, docs),
        out_shape=jax.ShapeDtypeStruct((docs, query_rows), jnp.float32),
        in_specs=[vmem()] * (3 + len(pieces)),
        out_specs=vmem(),
        scratch_shapes=[
            pltpu.VMEM((query_rows, DIM), jnp.float32),
            pltpu.VMEM((2 * query_rows, 4 * DIM), jnp.bfloat16),
        ],
        compiler_params=pltpu.CompilerParams(vmem_limit_bytes=24 * 2**20),
        name="local_maxima",
    )(left, live, spread, *pieces)


def rms_scale(values, gain):
    mean_square = jnp.mean(values * values, axis=-1, keepdims=True)
    return (values * lax.rsqrt(mean_square + 1e-06) * gain).astype(jnp.bfloat16)


def product(left, right):
    return jnp.dot(left, right, preferred_element_type=jnp.float32)


def rerank_kernel(sources, *refs):
    pieces, refs = refs[: len(sources)], refs[len(sources) :]
    (
        candidates,
        input_proj,
        gain_one,
        query_proj,
        key_proj,
        value_proj,
        output_proj,
        gain_two,
        up_proj,
        down_proj,
        out_ref,
        maxima,
        first,
        hidden,
        normed,
    ) = refs
    cand = candidates.shape[1]
    rows = out_ref.shape[0]
    place(pieces, sources, maxima, "docs")

    doc = lax.broadcasted_iota(jnp.int32, (maxima.shape[0], cand), 0)
    chosen = jnp.where(doc == candidates[...], 1.0, 0.0).astype(jnp.bfloat16)
    rest = maxima[...]
    features = None
    for _ in range(3):
        part = rest.astype(jnp.bfloat16)
        rest = rest - part.astype(jnp.float32)
        taken = lax.dot_general(
            chosen, part, (((0,), (0,)), ((), ())), preferred_element_type=jnp.float32
        )
        features = taken if features is None else features + taken

    first[...] = jnp.zeros_like(first)
    start = pl.multiple_of(lax.axis_index("docs") * QT, QT)
    first[pl.ds(start, QT), :] = input_proj[...]
    all_hidden = jnp.dot(
        features,
        first[...],
        precision=lax.Precision.HIGHEST,
        preferred_element_type=jnp.float32,
    )
    all_normed = rms_scale(all_hidden, gain_one[...])
    hidden[...] = all_hidden
    normed[...] = all_normed
    mine = pl.multiple_of(lax.axis_index(MEMBERS) * rows, rows)
    hidden_zero = hidden[pl.ds(mine, rows), :]
    query_heads = product(normed[pl.ds(mine, rows), :], query_proj[...]).astype(jnp.bfloat16)
    key_heads = product(all_normed, key_proj[...]).astype(jnp.bfloat16)
    value_heads = product(all_normed, value_proj[...]).astype(jnp.bfloat16)

    head_of = jnp.right_shift(lax.broadcasted_iota(jnp.int32, (rows, H), 1), 6)
    split = [jnp.where(head_of == h, query_heads, jnp.zeros_like(query_heads)) for h in range(HEADS)]
    scores = lax.dot_general(
        jnp.concatenate(split, axis=0),
        key_heads,
        (((1,), (1,)), ((), ())),
        preferred_element_type=jnp.float32,
    ) * (HEAD ** (-0.5))
    expon = jnp.exp(scores - jnp.max(scores, axis=-1, keepdims=True))
    summed = jnp.sum(expon, axis=-1, keepdims=True)
    spread = product(expon.astype(jnp.bfloat16), value_heads) / summed
    attended = spread[:rows]
    for h in range(1, HEADS):
        attended = jnp.where(head_of == h, spread[h * rows : (h + 1) * rows], attended)
    hidden_one = hidden_zero + product(attended.astype(jnp.bfloat16), output_proj[...])
    normed_two = rms_scale(hidden_one, gain_two[...])
    inner = jax.nn.gelu(product(normed_two, up_proj[...])).astype(jnp.bfloat16)
    out_ref[...] = hidden_one + product(inner, down_proj[...])


def rerank(pieces, sources, arrays, rows):
    docs_all = sum(piece.shape[0] for piece in pieces)
    query_rows = pieces[0].shape[1]
    cand = arrays[0].shape[1]
    return pl.pallas_call(
        functools.partial(rerank_kernel, sources),
        out_shape=jax.ShapeDtypeStruct((rows, H), jnp.float32),
        in_specs=[vmem()] * (len(pieces) + len(arrays)),
        out_specs=vmem(),
        scratch_shapes=[
            pltpu.VMEM((docs_all, query_rows), jnp.float32),
            pltpu.VMEM((query_rows, H), jnp.float32),
            pltpu.VMEM((cand, H), jnp.float32),
            pltpu.VMEM((cand, H), jnp.bfloat16),
        ],
        compiler_params=pltpu.CompilerParams(vmem_limit_bytes=32 * 2**20),
        name="rerank",
    )(*pieces, *arrays)


def on_device(
    queries,
    token_codes,
    centroid_ids,
    slot_counts,
    centroids,
    bucket_values,
    candidates,
    input_proj,
    gain_one,
    query_proj,
    key_proj,
    value_proj,
    output_proj,
    gain_two,
    up_proj,
    down_proj,
):
    kept = (
        candidates,
        input_proj,
        gain_one[None, :],
        query_proj,
        key_proj,
        value_proj,
        output_proj,
        gain_two[None, :],
        up_proj,
        down_proj,
    )
    query_pieces, query_sources = gather_queries(queries)
    left, live, spread, *kept = prepare(
        centroid_ids, slot_counts, token_codes[0], centroids, bucket_values, kept
    )
    local_best = local_maxima(left, live, spread, query_pieces, query_sources)
    doc_pieces, doc_sources = gather_docs(best_of_members(local_best))
    rows = candidates.shape[1] // lax.axis_size(MEMBERS)
    return rerank(doc_pieces, doc_sources, kept, rows)[None]


def solution(mesh):
    in_specs = (
        P(("groups", "cent", "sub"), None),
        P(("cent", "sub"), ("groups", "docs"), None),
        P(("cent", "sub"), ("groups", "docs")),
        P(("cent", "sub"), ("groups", "docs")),
        P(("cent", "sub"), None),
        P(),
        P(("groups", "docs"), None),
        P(),
        P(),
        P(),
        P(),
        P(),
        P(),
        P(),
        P(),
        P(),
    )
    out_specs = P(("groups", "docs"), ("cent", "sub"), None)
    return jax.shard_map(
        on_device, mesh=mesh, in_specs=in_specs, out_specs=out_specs, check_vma=False
    )
```

time: 36.7 us -> 23.2 us (0.63)
  local copies, waits for them, and re-layouts: 5.22 us -> 0.01 us
  waiting for transfers between devices: 9.07 us -> 5 us
  Pallas kernels: 11.9 us -> 8.42 us
  starting transfers between devices: 10 us -> 9.61 us
    unnamed x32 -> x2, local copies, waits for them, and re-layouts: 5.22 us -> 0.01 us
    ppermute x9 -> x8, waiting for transfers between devices: 9.07 us -> 5 us  [the longest x3 2.71 us: gather_docs(): pieces.append(lax.ppermute(values, ('docs', 'sub'), pairs))]
    pallas_call x2 -> x3, Pallas kernels: 11.9 us -> 8.42 us  [the longest x1 5.43 us: prepare(): pl.pallas_call(functools.partial(prepare_kernel, len(kept)), out_shape=[s...]
    ppermute x9 -> x8, starting transfers between devices: 10 us -> 9.61 us  [the longest x3 4.35 us: gather_docs(): pieces.append(lax.ppermute(values, ('docs', 'sub'), pairs))]
  transfers between devices with their start and end apart: 9 -> 8, of which waited for: 6 -> 5; matrix products, arithmetic and copies ran while one was open for 0% -> 0% of each run, Pallas kernels for 0% -> 24%
where the time goes in v2:
time: 23.2 us; the launch traced here: 23.1 us
  starting transfers between devices  9.61 us (41%)
  Pallas kernels  8.42 us (36%)
  waiting for transfers between devices  5 us (22%)
    pallas_call x1, Pallas kernels, prepare(): pl.pallas_call(functools.partial(prepare_kernel, len(kept)), out_shape=[s...  5.43 us
    ppermute x3, starting transfers between devices, gather_docs(): pieces.append(lax.ppermute(values, ('docs', 'sub'), pairs))  4.35 us
    ppermute x3, starting transfers between devices, gather_queries(): lax.ppermute(queries, MEMBERS, [(i, i ^ step) for i in range(4)])  3.06 us
    ppermute x3, waiting for transfers between devices, gather_docs(): pieces.append(lax.ppermute(values, ('docs', 'sub'), pairs))  2.71 us
    pallas_call x1, Pallas kernels, rerank(): pl.pallas_call(functools.partial(rerank_kernel, sources), out_shape=jax.S...  2.12 us
    ppermute x1, starting transfers between devices, best_of_members(): lax.ppermute(values, MEMBERS, [(i, i ^ 3) for i in range(4)])  1.74 us
    ppermute x1, waiting for transfers between devices, best_of_members(): lax.ppermute(values, MEMBERS, [(i, i ^ 3) for i in range(4)])  1.44 us
    pallas_call x1, Pallas kernels, local_maxima(): pl.pallas_call(functools.partial(score_kernel, sources, docs), out_shape=...  0.87 us
  transfers between devices with their start and end apart: 8, of which 5 were waited for; matrix products, arithmetic and copies ran while one was open for 0% of the time, Pallas kernels for 24%

profile of v2, /device:TPU:0, one launch (start us, length us, event | category | flops | bytes accessed | tf_op | source)
XLA Modules:
  0.0 23.1 jit_solution(752415904060207050)
XLA Ops:
  0.0 2.9 %collective-permute-start.1 = (f32[32,128]{1,0:T(8,128)}, f32[32,128]{1,0:T(8,128)S(1)}, u32[]{:S(2)}, u32[]{:S(2)}) collective-permute-start(f32[32,128]{1,0:T(8,128)} %refs_0_.3), channel_id=1, source_target_pairs={{0,2},{1,3},{2,0},{3,1},{4,6},{5,7},{6,4},{7,5},{8,10},{9,11},{10,... | collective-permute-start | bytes 49160 | tf_op jit(solution)/shard_map/ppermute | solution.py:34
  2.9 0.0 collective-permute-start
  2.9 0.1 collective-permute-start.2
  3.1 0.0 copy-start
  3.1 5.4 %prepare.1 = (bf16[2048,512]{1,0:T(8,128)(2,1)S(1)}, s32[32,128]{1,0:T(8,128)S(1)}, bf16[128,256]{1,0:T(8,128)(2,1)S(1)}, s32[1,64]{1,0:T(1,128)S(1)}, f32[32,25...) custom-call(s32[1,4096]{1,0:T(1,128)} %ids_hbm.1, ...), custom_call_target="tpu_custom_call" | custom-call | flops 4000000000 | bytes 4194304 | tf_op jit(solution)/shard_map/prepare/pallas_call | solution.py:185
  8.5 0.0 collective-permute-done.1.refs_2_
  8.5 0.0 collective-permute-done.refs_1_
  8.5 0.0 collective-permute-done.2.refs_3_
  8.5 0.0 copy-done
  8.5 0.9 %local_maxima.1 = f32[32,128]{1,0:T(8,128)S(1)} custom-call(bf16[2048,512]{1,0:T(8,128)(2,1)S(1)} %get-tuple-element.18.left, s32[32,128]{1,0:T(8,128)S(1)} %get-tuple-element.19.live, bf16[128,256]{1,0:T(8,128)(2,1)S(1)} %get-tuple-element.20.spread, f32[32,128]{1,0:T(8,128)S(1)} %copy-done, f32[32,128]{1,0:T(8,128)S(1)} %collective-permute-done.refs_1_, ...), custom_call_target="tpu_custom_call" | custom-call | tf_op jit(solution)/shard_map/local_maxima/pallas_call | solution.py:257
  9.4 0.5 %collective-permute-start.3 = (f32[32,128]{1,0:T(8,128)S(1)}, f32[32,128]{1,0:T(8,128)S(1)}, u32[]{:S(2)}, u32[]{:S(2)}) collective-permute-start(f32[32,128]{1,0:T(8,128)S(1)} %local_maxima.1), channel_id=1, source_target_pairs={{0,1},{1,0},{2,3},{3,2},{4,5},{5,4},{6,7},{7,6},{8,9},{9,8},{10,11... | collective-permute-start | bytes 49160 | tf_op jit(solution)/shard_map/ppermute | solution.py:41
  9.9 0.8 %collective-permute-done.3 = f32[32,128]{1,0:T(8,128)S(1)} collective-permute-done((f32[32,128]{1,0:T(8,128)S(1)}, f32[32,128]{1,0:T(8,128)S(1)}, u32[]{:S(2)}, u32[]{:S(2)}) %collective-permute-start.3) | collective-permute-done | bytes 16416 | tf_op jit(solution)/shard_map/ppermute | solution.py:41
  10.7 1.7 %collective-permute-start.4 = (f32[32,128]{1,0:T(8,128)S(1)}, f32[32,128]{1,0:T(8,128)S(1)}, u32[]{:S(2)}, u32[]{:S(2)}) collective-permute-start(f32[32,128]{1,0:T(8,128)S(1)} %max.6), channel_id=1, source_target_pairs={{0,3},{1,2},{2,1},{3,0},{4,7},{5,6},{6,5},{7,4},{8,11},{9,10},{10,... | collective-permute-start | bytes 49160 | tf_op jit(solution)/shard_map/ppermute | solution.py:42
  12.5 1.4 %collective-permute-done.4 = f32[32,128]{1,0:T(8,128)S(1)} collective-permute-done((f32[32,128]{1,0:T(8,128)S(1)}, f32[32,128]{1,0:T(8,128)S(1)}, u32[]{:S(2)}, u32[]{:S(2)}) %collective-permute-start.4) | collective-permute-done | bytes 16416 | tf_op jit(solution)/shard_map/ppermute | solution.py:42
  13.9 2.8 %collective-permute-start.7 = (f32[32,128]{1,0:T(8,128)S(1)}, f32[32,128]{1,0:T(8,128)S(1)}, u32[]{:S(2)}, u32[]{:S(2)}) collective-permute-start(f32[32,128]{1,0:T(8,128)S(1)} %max.7.refs_0_), channel_id=1, source_target_pairs={{0,9},{1,8},{4,13},{5,12},{8,5},{9,4},{12,1},{13,0},{2,11},{3,10},... | collective-permute-start | bytes 49160 | tf_op jit(solution)/shard_map/ppermute | solution.py:51
  16.7 1.1 %collective-permute-start.6 = (f32[32,128]{1,0:T(8,128)S(1)}, f32[32,128]{1,0:T(8,128)S(1)}, u32[]{:S(2)}, u32[]{:S(2)}) collective-permute-start(f32[32,128]{1,0:T(8,128)S(1)} %max.7.refs_0_), channel_id=1, source_target_pairs={{0,13},{1,12},{4,9},{5,8},{8,1},{9,0},{12,5},{13,4},{2,15},{3,14},... | collective-permute-start | bytes 49160 | tf_op jit(solution)/shard_map/ppermute | solution.py:51
  17.8 0.5 %collective-permute-start.5 = (f32[32,128]{1,0:T(8,128)S(1)}, f32[32,128]{1,0:T(8,128)S(1)}, u32[]{:S(2)}, u32[]{:S(2)}) collective-permute-start(f32[32,128]{1,0:T(8,128)S(1)} %max.7.refs_0_), channel_id=1, source_target_pairs={{0,5},{1,4},{4,1},{5,0},{8,13},{9,12},{12,9},{13,8},{2,7},{3,6},{6... | collective-permute-start | bytes 49160 | tf_op jit(solution)/shard_map/ppermute | solution.py:51
  18.3 0.9 %collective-permute-done.7.refs_3_ = f32[32,128]{1,0:T(8,128)S(1)} collective-permute-done((f32[32,128]{1,0:T(8,128)S(1)}, f32[32,128]{1,0:T(8,128)S(1)}, u32[]{:S(2)}, u32[]{:S(2)}) %collective-permute-start.7) | collective-permute-done | bytes 16416 | tf_op jit(solution)/shard_map/ppermute | solution.py:51
  19.2 1.6 %collective-permute-done.6.refs_2_ = f32[32,128]{1,0:T(8,128)S(1)} collective-permute-done((f32[32,128]{1,0:T(8,128)S(1)}, f32[32,128]{1,0:T(8,128)S(1)}, u32[]{:S(2)}, u32[]{:S(2)}) %collective-permute-start.6) | collective-permute-done | bytes 16416 | tf_op jit(solution)/shard_map/ppermute | solution.py:51
  20.8 0.2 collective-permute-done.5.refs_1_
  21.0 2.1 %rerank.1 = f32[16,256]{1,0:T(8,128)} custom-call(f32[32,128]{1,0:T(8,128)S(1)} %max.7.refs_0_, f32[32,128]{1,0:T(8,128)S(1)} %collective-permute-done.5.refs_1_, f32[32,128]{1,0:T(8,128)S(1)} %collective-permute-done.6.refs_2_, f32[32,128]{1,0:T(8,128)S(1)} %collective-permute-done.7.refs_3_, s32[1,64]{1,0:T(1,128)S(1)} %get-tuple-element.21.refs_4_, ...), custom_call_target="tpu_custom_call" | custom-call | tf_op jit(solution)/shard_map/rerank/pallas_call | solution.py:357
  (2 shorter events, 0.0 us)
Async XLA Ops:
  0.0 8.5 %collective-permute-start.1 = (f32[32,128]{1,0:T(8,128)}, f32[32,128]{1,0:T(8,128)S(1)}, u32[]{:S(2)}, u32[]{:S(2)}) collective-permute-start(f32[32,128]{1,0:T(8,128)} %refs_0_.3), channel_id=1, source_target_pairs={{0,2},{1,3},{2,0},{3,1},{4,6},{5,7},{6,4},{7,5},{8,10},{9,11},{10,... | collective-permute-start | bytes 49160 | tf_op jit(solution)/shard_map/ppermute | solution.py:34
  2.9 5.6 %collective-permute-start = (f32[32,128]{1,0:T(8,128)}, f32[32,128]{1,0:T(8,128)S(1)}, u32[]{:S(2)}, u32[]{:S(2)}) collective-permute-start(f32[32,128]{1,0:T(8,128)} %refs_0_.3), channel_id=1, source_target_pairs={{0,1},{1,0},{2,3},{3,2},{4,5},{5,4},{6,7},{7,6},{8,9},{9,8},{10,11... | collective-permute-start | bytes 49160 | tf_op jit(solution)/shard_map/ppermute | solution.py:34
  2.9 5.6 %collective-permute-start.2 = (f32[32,128]{1,0:T(8,128)}, f32[32,128]{1,0:T(8,128)S(1)}, u32[]{:S(2)}, u32[]{:S(2)}) collective-permute-start(f32[32,128]{1,0:T(8,128)} %refs_0_.3), channel_id=1, source_target_pairs={{0,3},{1,2},{2,1},{3,0},{4,7},{5,6},{6,5},{7,4},{8,11},{9,10},{10,... | collective-permute-start | bytes 49160 | tf_op jit(solution)/shard_map/ppermute | solution.py:34
  3.1 5.5 %copy-start = (f32[32,128]{1,0:T(8,128)S(1)}, f32[32,128]{1,0:T(8,128)}, u32[]{:S(2)}) copy-start(f32[32,128]{1,0:T(8,128)} %refs_0_.3) | copy-start | bytes 49156
  9.4 1.3 %collective-permute-start.3 = (f32[32,128]{1,0:T(8,128)S(1)}, f32[32,128]{1,0:T(8,128)S(1)}, u32[]{:S(2)}, u32[]{:S(2)}) collective-permute-start(f32[32,128]{1,0:T(8,128)S(1)} %local_maxima.1), channel_id=1, source_target_pairs={{0,1},{1,0},{2,3},{3,2},{4,5},{5,4},{6,7},{7,6},{8,9},{9,8},{10,11... | collective-permute-start | bytes 49160 | tf_op jit(solution)/shard_map/ppermute | solution.py:41
  10.7 3.2 %collective-permute-start.4 = (f32[32,128]{1,0:T(8,128)S(1)}, f32[32,128]{1,0:T(8,128)S(1)}, u32[]{:S(2)}, u32[]{:S(2)}) collective-permute-start(f32[32,128]{1,0:T(8,128)S(1)} %max.6), channel_id=1, source_target_pairs={{0,3},{1,2},{2,1},{3,0},{4,7},{5,6},{6,5},{7,4},{8,11},{9,10},{10,... | collective-permute-start | bytes 49160 | tf_op jit(solution)/shard_map/ppermute | solution.py:42
  13.9 5.3 %collective-permute-start.7 = (f32[32,128]{1,0:T(8,128)S(1)}, f32[32,128]{1,0:T(8,128)S(1)}, u32[]{:S(2)}, u32[]{:S(2)}) collective-permute-start(f32[32,128]{1,0:T(8,128)S(1)} %max.7.refs_0_), channel_id=1, source_target_pairs={{0,9},{1,8},{4,13},{5,12},{8,5},{9,4},{12,1},{13,0},{2,11},{3,10},... | collective-permute-start | bytes 49160 | tf_op jit(solution)/shard_map/ppermute | solution.py:51
  16.7 4.1 %collective-permute-start.6 = (f32[32,128]{1,0:T(8,128)S(1)}, f32[32,128]{1,0:T(8,128)S(1)}, u32[]{:S(2)}, u32[]{:S(2)}) collective-permute-start(f32[32,128]{1,0:T(8,128)S(1)} %max.7.refs_0_), channel_id=1, source_target_pairs={{0,13},{1,12},{4,9},{5,8},{8,1},{9,0},{12,5},{13,4},{2,15},{3,14},... | collective-permute-start | bytes 49160 | tf_op jit(solution)/shard_map/ppermute | solution.py:51
  17.8 3.2 %collective-permute-start.5 = (f32[32,128]{1,0:T(8,128)S(1)}, f32[32,128]{1,0:T(8,128)S(1)}, u32[]{:S(2)}, u32[]{:S(2)}) collective-permute-start(f32[32,128]{1,0:T(8,128)S(1)} %max.7.refs_0_), channel_id=1, source_target_pairs={{0,5},{1,4},{4,1},{5,0},{8,13},{9,12},{12,9},{13,8},{2,7},{3,6},{6... | collective-permute-start | bytes 49160 | tf_op jit(solution)/shard_map/ppermute | solution.py:51

commit v3 on v2

--- a/solution.py
+++ b/solution.py
@@ -14,6 +14,8 @@
 HEAD = 64
 MEMBERS = ("cent", "sub")
 NOTHING = -1e30
+CHUNKS = 4
+PART_PAIRS = ((0, 0), (0, 1), (0, 2), (1, 0), (1, 1), (2, 0))
 DOC_STEPS = ((2, 3, 1, 0), (3, 2, 0, 1), (1, 0, 3, 2))
 
 
@@ -90,6 +92,15 @@
     return jnp.where(wanted == dim, 1.0, 0.0).astype(jnp.bfloat16)
 
 
+def three_parts(values):
+    parts = []
+    for _ in range(3):
+        part = values.astype(jnp.bfloat16)
+        values = values - part.astype(jnp.float32)
+        parts.append(part)
+    return parts
+
+
 def look_up(nibbles, halves):
     index = jnp.bitwise_and(nibbles, 7)
     lower = jnp.take_along_axis(halves[0], index, axis=0)
@@ -97,54 +108,63 @@
     return jnp.where(nibbles >= 8, upper, lower)
 
 
-def prepare_kernel(n_kept, ids_hbm, counts_hbm, codes_hbm, centroids_hbm, buckets_hbm, *refs):
-    kept_hbm, refs = refs[:n_kept], refs[n_kept:]
-    left, live, spread = refs[:3]
-    kept, refs = refs[3 : 3 + n_kept], refs[3 + n_kept :]
-    ids, counts, codes, centroids, buckets, table, anchors, sems, kept_sems = refs
+def prepare_kernel(n_kept, *refs):
+    ids_hbm, counts_hbm, candidates_hbm, codes_hbm, centroids_hbm, buckets_hbm, proj_hbm = refs[:7]
+    kept_hbm, refs = refs[7 : 7 + n_kept], refs[7 + n_kept :]
+    left, live, spread, chosen, proj_parts = refs[:5]
+    kept, refs = refs[5 : 5 + n_kept], refs[5 + n_kept :]
+    ids, counts, candidates, codes, centroids, buckets, proj, table, sems, chunk_sems, code_sems, kept_sems = refs
     docs, columns = codes.shape
     pairs = columns // DIM
     slots = 2 * pairs
-
-    copies = [
+    cand = candidates.shape[1]
+    rows_dev = chosen.shape[0] - cand
+
+    chunk = centroids.shape[0] // CHUNKS
+    chunks = [
+        pltpu.make_async_copy(
+            centroids_hbm.at[pl.ds(i * chunk, chunk), :],
+            centroids.at[pl.ds(i * chunk, chunk), :],
+            chunk_sems.at[i],
+        )
+        for i in range(CHUNKS)
+    ]
+    small = [
         pltpu.make_async_copy(source, target, sems.at[i])
         for i, (source, target) in enumerate(
             (
-                (centroids_hbm, centroids),
                 (ids_hbm, ids),
                 (buckets_hbm, buckets),
                 (counts_hbm, counts),
-                (codes_hbm, codes),
+                (candidates_hbm, candidates),
+                (proj_hbm, proj),
             )
         )
     ]
-    copies += [
+    part = columns // CHUNKS
+    code_chunks = [
+        pltpu.make_async_copy(
+            codes_hbm.at[:, pl.ds(i * part, part)],
+            codes.at[:, pl.ds(i * part, part)],
+            code_sems.at[i],
+        )
+        for i in range(CHUNKS)
+    ]
+    late = [
         pltpu.make_async_copy(source, target, kept_sems.at[i])
         for i, (source, target) in enumerate(zip(kept_hbm, kept))
     ]
-    for copy in copies:
+    for copy in small + chunks + code_chunks:
         copy.start()
     columns_of = even_odd_columns()
     spread[...] = columns_of
 
-    copies[2].wait()
+    small[1].wait()
     levels = jnp.dot(
         buckets[...].astype(jnp.bfloat16), columns_of, preferred_element_type=jnp.float32
     )
     tables = [[levels[i : i + 8, k : k + DIM] for i in (0, 8)] for k in (0, DIM)]
-
-    copies[0].wait()
-    chunk = 512
-
-    def widen(i, carry):
-        start = pl.multiple_of(i * chunk, chunk)
-        table[pl.ds(start, chunk), :] = centroids[pl.ds(start, chunk), :].astype(jnp.float32)
-        return carry
-
-    lax.fori_loop(0, centroids.shape[0] // chunk, widen, 0)
-
-    copies[1].wait()
-    copies[3].wait()
+    small[2].wait()
     doc_row = lax.broadcasted_iota(jnp.int32, (8, DIM), 0)
     for b in range(docs // 8):
         block = jnp.zeros((8, DIM), jnp.int32)
@@ -152,33 +172,71 @@
             block = jnp.where(doc_row == n, counts[0, b * 8 + n], block)
         live[b * 8 : b * 8 + 8, :] = block
 
-    copies[4].wait()
-    for pair in range(pairs):
-        start = pair * docs
-        for k in range(2):
-
-            def fetch(n, carry, first=2 * start + k * docs, slot=2 * pair + k):
-                row = ids[0, n * slots + slot]
-                anchors[pl.ds(first + n, 1), :] = table[pl.ds(row, 1), :]
-                return carry
-
-            lax.fori_loop(0, docs, fetch, 0, unroll=True)
-        lows, highs = [], []
-        for b in range(docs // 8):
-            code = codes[b * 8 : b * 8 + 8, pair * DIM : (pair + 1) * DIM]
-            lows.append(look_up(jnp.bitwise_and(code, 15), tables[0]))
-            highs.append(look_up(jnp.right_shift(code, 4), tables[1]))
-        rows = slice(start, start + docs)
-        left[rows, 2 * DIM : 3 * DIM] = jnp.concatenate(lows, axis=0).astype(jnp.bfloat16)
-        left[rows, 3 * DIM :] = jnp.concatenate(highs, axis=0).astype(jnp.bfloat16)
-        for k in range(2):
-            found = anchors[2 * start + k * docs : 2 * start + (k + 1) * docs, :]
-            left[rows, k * DIM : (k + 1) * DIM] = found.astype(jnp.bfloat16)
-    for copy in copies[5:]:
+    small[3].wait()
+    docs_all = chosen.shape[1]
+    member = lax.axis_index(MEMBERS)
+    doc = lax.broadcasted_iota(jnp.int32, (16, docs_all), 1)
+    place_in = lax.broadcasted_iota(jnp.int32, (16, docs_all), 0)
+
+    def choose(i, carry):
+        start = pl.multiple_of(i * 16, 16)
+        source = jnp.where(start < cand, start, start - cand + member * rows_dev)
+        wanted = jnp.zeros((16, docs_all), jnp.int32)
+        for n in range(16):
+            wanted = jnp.where(place_in == n, candidates[0, source + n], wanted)
+        chosen[pl.ds(start, 16), :] = jnp.where(doc == wanted, 1.0, 0.0).astype(jnp.bfloat16)
+        return carry
+
+    lax.fori_loop(0, chosen.shape[0] // 16, choose, 0)
+    small[4].wait()
+    parts = three_parts(proj[...])
+    for i, k in enumerate(PART_PAIRS):
+        proj_parts[i * QT : (i + 1) * QT, :] = parts[k[1]]
+
+    for i, copy in enumerate(chunks):
         copy.wait()
-
-
-def prepare(ids, counts, codes, centroids, buckets, kept):
+        for first in range(i * chunk, (i + 1) * chunk, 256):
+            table[first : first + 256, :] = centroids[first : first + 256, :].astype(jnp.float32)
+    small[0].wait()
+    row_bits = [jnp.bitwise_and(doc_row, bit) != 0 for bit in (1, 2, 4)]
+
+    def fetch(slot, first):
+        rows = []
+        for n in range(first, first + 8):
+            row = table[pl.ds(ids[0, n * slots + slot], 1), :]
+            rows.append(jnp.broadcast_to(row, (8, DIM)))
+        for bit in row_bits:
+            rows = [jnp.where(bit, rows[i + 1], rows[i]) for i in range(0, len(rows), 2)]
+        return rows[0]
+
+    def one_pair(pair, carry):
+        start = pl.multiple_of(pair * docs, docs)
+        column = pl.multiple_of(pair * DIM, DIM)
+        parts = [[], [], [], []]
+        for b in range(0, docs, 8):
+            code = codes[b : b + 8, pl.ds(column, DIM)]
+            parts[0].append(fetch(2 * pair, b))
+            parts[1].append(fetch(2 * pair + 1, b))
+            parts[2].append(look_up(jnp.bitwise_and(code, 15), tables[0]))
+            parts[3].append(look_up(jnp.right_shift(code, 4), tables[1]))
+        for k, part in enumerate(parts):
+            columns = slice(k * DIM, (k + 1) * DIM)
+            left[pl.ds(start, docs), columns] = jnp.concatenate(part, axis=0).astype(jnp.bfloat16)
+        return carry
+
+    for i, copy in enumerate(code_chunks):
+        copy.wait()
+        if i == 1:
+            for other in late:
+                other.start()
+        lax.fori_loop(
+            i * pairs // CHUNKS, (i + 1) * pairs // CHUNKS, one_pair, 0, unroll=True
+        )
+    for copy in late:
+        copy.wait()
+
+
+def prepare(ids, counts, candidates, codes, centroids, buckets, input_proj, docs_all, rows, kept):
     docs, columns = codes.shape
     pairs = columns // DIM
     shape = jax.ShapeDtypeStruct
@@ -188,25 +246,35 @@
             shape((pairs * docs, 4 * DIM), jnp.bfloat16),
             shape((docs, DIM), jnp.int32),
             shape((DIM, 2 * DIM), jnp.bfloat16),
+            shape((candidates.shape[1] + rows, docs_all), jnp.bfloat16),
+            shape((len(PART_PAIRS) * QT, H), jnp.bfloat16),
         ]
         + [shape(array.shape, array.dtype) for array in kept],
-        in_specs=[hbm()] * (5 + len(kept)),
-        out_specs=[vmem()] * (3 + len(kept)),
+        in_specs=[hbm()] * (7 + len(kept)),
+        out_specs=[vmem()] * (5 + len(kept)),
         scratch_shapes=[
             pltpu.SMEM(ids.shape, jnp.int32),
             pltpu.SMEM(counts.shape, jnp.int32),
+            pltpu.SMEM(candidates.shape, jnp.int32),
             pltpu.VMEM(codes.shape, jnp.int32),
             pltpu.VMEM(centroids.shape, jnp.bfloat16),
             pltpu.VMEM(buckets.shape, jnp.float32),
+            pltpu.VMEM(input_proj.shape, jnp.float32),
             pltpu.VMEM(centroids.shape, jnp.float32),
-            pltpu.VMEM((2 * pairs * docs, DIM), jnp.float32),
             pltpu.SemaphoreType.DMA((5,)),
+            pltpu.SemaphoreType.DMA((CHUNKS,)),
+            pltpu.SemaphoreType.DMA((CHUNKS,)),
             pltpu.SemaphoreType.DMA((len(kept),)),
         ],
         compiler_params=pltpu.CompilerParams(vmem_limit_bytes=24 * 2**20),
         cost_estimate=pl.CostEstimate(flops=4 * 10**9, bytes_accessed=2**22, transcendentals=0),
         name="prepare",
-    )(*[in_hbm(x) for x in (ids, counts, codes, centroids, buckets, *kept)])
+    )(
+        *[
+            in_hbm(x)
+            for x in (ids, counts, candidates, codes, centroids, buckets, input_proj, *kept)
+        ]
+    )
 
 
 def score_kernel(sources, docs, left, live, spread, *refs):
@@ -280,8 +348,8 @@
 def rerank_kernel(sources, *refs):
     pieces, refs = refs[: len(sources)], refs[len(sources) :]
     (
-        candidates,
-        input_proj,
+        chosen,
+        proj_parts,
         gain_one,
         query_proj,
         key_proj,
@@ -292,43 +360,22 @@
         down_proj,
         out_ref,
         maxima,
-        first,
-        hidden,
-        normed,
     ) = refs
-    cand = candidates.shape[1]
     rows = out_ref.shape[0]
+    cand = chosen.shape[0] - rows
     place(pieces, sources, maxima, "docs")
 
-    doc = lax.broadcasted_iota(jnp.int32, (maxima.shape[0], cand), 0)
-    chosen = jnp.where(doc == candidates[...], 1.0, 0.0).astype(jnp.bfloat16)
-    rest = maxima[...]
-    features = None
-    for _ in range(3):
-        part = rest.astype(jnp.bfloat16)
-        rest = rest - part.astype(jnp.float32)
-        taken = lax.dot_general(
-            chosen, part, (((0,), (0,)), ((), ())), preferred_element_type=jnp.float32
-        )
-        features = taken if features is None else features + taken
-
-    first[...] = jnp.zeros_like(first)
-    start = pl.multiple_of(lax.axis_index("docs") * QT, QT)
-    first[pl.ds(start, QT), :] = input_proj[...]
-    all_hidden = jnp.dot(
-        features,
-        first[...],
-        precision=lax.Precision.HIGHEST,
-        preferred_element_type=jnp.float32,
-    )
-    all_normed = rms_scale(all_hidden, gain_one[...])
-    hidden[...] = all_hidden
-    normed[...] = all_normed
-    mine = pl.multiple_of(lax.axis_index(MEMBERS) * rows, rows)
-    hidden_zero = hidden[pl.ds(mine, rows), :]
-    query_heads = product(normed[pl.ds(mine, rows), :], query_proj[...]).astype(jnp.bfloat16)
-    key_heads = product(all_normed, key_proj[...]).astype(jnp.bfloat16)
-    value_heads = product(all_normed, value_proj[...]).astype(jnp.bfloat16)
+    width = maxima.shape[1]
+    own = pltpu.roll(maxima[...], lax.rem(width - lax.axis_index("docs") * QT, width), 1)
+    parts = three_parts(own[:, :QT])
+    stacked = jnp.concatenate([parts[k[0]] for k in PART_PAIRS], axis=1)
+    features = product(chosen[...], stacked).astype(jnp.bfloat16)
+    all_hidden = product(features, proj_parts[...])
+    hidden_zero = all_hidden[cand:]
+    normed = rms_scale(all_hidden, gain_one[...])
+    query_heads = product(normed[cand:], query_proj[...]).astype(jnp.bfloat16)
+    key_heads = product(normed[:cand], key_proj[...]).astype(jnp.bfloat16)
+    value_heads = product(normed[:cand], value_proj[...]).astype(jnp.bfloat16)
 
     head_of = jnp.right_shift(lax.broadcasted_iota(jnp.int32, (rows, H), 1), 6)
     split = [jnp.where(head_of == h, query_heads, jnp.zeros_like(query_heads)) for h in range(HEADS)]
@@ -353,18 +400,12 @@
 def rerank(pieces, sources, arrays, rows):
     docs_all = sum(piece.shape[0] for piece in pieces)
     query_rows = pieces[0].shape[1]
-    cand = arrays[0].shape[1]
     return pl.pallas_call(
         functools.partial(rerank_kernel, sources),
         out_shape=jax.ShapeDtypeStruct((rows, H), jnp.float32),
         in_specs=[vmem()] * (len(pieces) + len(arrays)),
         out_specs=vmem(),
-        scratch_shapes=[
-            pltpu.VMEM((docs_all, query_rows), jnp.float32),
-            pltpu.VMEM((query_rows, H), jnp.float32),
-            pltpu.VMEM((cand, H), jnp.float32),
-            pltpu.VMEM((cand, H), jnp.bfloat16),
-        ],
+        scratch_shapes=[pltpu.VMEM((docs_all, query_rows), jnp.float32)],
         compiler_params=pltpu.CompilerParams(vmem_limit_bytes=32 * 2**20),
         name="rerank",
     )(*pieces, *arrays)
@@ -389,8 +430,6 @@
     down_proj,
 ):
     kept = (
-        candidates,
-        input_proj,
         gain_one[None, :],
         query_proj,
         key_proj,
@@ -400,14 +439,24 @@
         up_proj,
         down_proj,
     )
+    docs_all = slot_counts.shape[1] * lax.axis_size("docs")
+    rows = candidates.shape[1] // lax.axis_size(MEMBERS)
     query_pieces, query_sources = gather_queries(queries)
-    left, live, spread, *kept = prepare(
-        centroid_ids, slot_counts, token_codes[0], centroids, bucket_values, kept
+    left, live, spread, *staged = prepare(
+        centroid_ids,
+        slot_counts,
+        candidates,
+        token_codes[0],
+        centroids,
+        bucket_values,
+        input_proj,
+        docs_all,
+        rows,
+        kept,
     )
     local_best = local_maxima(left, live, spread, query_pieces, query_sources)
     doc_pieces, doc_sources = gather_docs(best_of_members(local_best))
-    rows = candidates.shape[1] // lax.axis_size(MEMBERS)
-    return rerank(doc_pieces, doc_sources, kept, rows)[None]
+    return rerank(doc_pieces, doc_sources, staged, rows)[None]
 
 
 def solution(mesh):

time: 23.2 us -> 21.8 us (0.940)
  Pallas kernels: 8.42 us -> 7 us
    pallas_call x1, Pallas kernels: 5.43 us -> 4.01 us  [prepare(): pl.pallas_call(functools.partial(prepare_kernel, len(kept)), out_shape=[s...]
  transfers between devices with their start and end apart: 8 -> 8, of which waited for: 5 -> 5; matrix products, arithmetic and copies ran while one was open for 0% -> 0% of each run, Pallas kernels for 24% -> 18%
where the time goes in v3:
time: 21.8 us; the launch traced here: 21.7 us
  starting transfers between devices  9.61 us (44%)
  Pallas kernels  7 us (32%)
  waiting for transfers between devices  5 us (23%)
    ppermute x3, starting transfers between devices, gather_docs(): pieces.append(lax.ppermute(values, ('docs', 'sub'), pairs))  4.35 us
    pallas_call x1, Pallas kernels, prepare(): pl.pallas_call(functools.partial(prepare_kernel, len(kept)), out_shape=[s...  4.01 us
    ppermute x3, starting transfers between devices, gather_queries(): lax.ppermute(queries, MEMBERS, [(i, i ^ step) for i in range(4)])  3.06 us
    ppermute x3, waiting for transfers between devices, gather_docs(): pieces.append(lax.ppermute(values, ('docs', 'sub'), pairs))  2.71 us
    pallas_call x1, Pallas kernels, rerank(): pl.pallas_call(functools.partial(rerank_kernel, sources), out_shape=jax.S...  2.12 us
    ppermute x1, starting transfers between devices, best_of_members(): lax.ppermute(values, MEMBERS, [(i, i ^ 3) for i in range(4)])  1.74 us
    ppermute x1, waiting for transfers between devices, best_of_members(): lax.ppermute(values, MEMBERS, [(i, i ^ 3) for i in range(4)])  1.44 us
    pallas_call x1, Pallas kernels, local_maxima(): pl.pallas_call(functools.partial(score_kernel, sources, docs), out_shape=...  0.86 us
  transfers between devices with their start and end apart: 8, of which 5 were waited for; matrix products, arithmetic and copies ran while one was open for 0% of the time, Pallas kernels for 18%

profile of v3, /device:TPU:0, one launch (start us, length us, event | category | flops | bytes accessed | tf_op | source)
XLA Modules:
  0.0 21.7 jit_solution(675282869328621054)
XLA Ops:
  0.0 2.9 %collective-permute-start.1 = (f32[32,128]{1,0:T(8,128)}, f32[32,128]{1,0:T(8,128)S(1)}, u32[]{:S(2)}, u32[]{:S(2)}) collective-permute-start(f32[32,128]{1,0:T(8,128)} %refs_0_.3), channel_id=1, source_target_pairs={{0,2},{1,3},{2,0},{3,1},{4,6},{5,7},{6,4},{7,5},{8,10},{9,11},{10,... | collective-permute-start | bytes 49160 | tf_op jit(solution)/shard_map/ppermute | solution.py:36
  2.9 0.0 collective-permute-start
  2.9 0.1 collective-permute-start.2
  3.1 0.0 copy-start
  3.1 4.0 %prepare.1 = (bf16[2048,512]{1,0:T(8,128)(2,1)S(1)}, s32[32,128]{1,0:T(8,128)S(1)}, bf16[128,256]{1,0:T(8,128)(2,1)S(1)}, bf16[80,128]{1,0:T(8,128)(2,1)S(1)}, b...) custom-call(s32[1,4096]{1,0:T(1,128)} %refs_0_.2, ...), custom_call_target="tpu_custom_call" | custom-call | flops 4000000000 | bytes 4194304 | tf_op jit(solution)/shard_map/prepare/pallas_call | solution.py:243
  7.1 0.0 collective-permute-done.1.refs_2_
  7.1 0.0 collective-permute-done.refs_1_
  7.1 0.0 collective-permute-done.2.refs_3_
  7.1 0.0 copy-done
  7.1 0.9 %local_maxima.1 = f32[32,128]{1,0:T(8,128)S(1)} custom-call(bf16[2048,512]{1,0:T(8,128)(2,1)S(1)} %get-tuple-element.18.left, s32[32,128]{1,0:T(8,128)S(1)} %get-tuple-element.19.live, bf16[128,256]{1,0:T(8,128)(2,1)S(1)} %get-tuple-element.20.spread, f32[32,128]{1,0:T(8,128)S(1)} %copy-done, f32[32,128]{1,0:T(8,128)S(1)} %collective-permute-done.refs_1_, ...), custom_call_target="tpu_custom_call" | custom-call | tf_op jit(solution)/shard_map/local_maxima/pallas_call | solution.py:325
  8.0 0.5 %collective-permute-start.3 = (f32[32,128]{1,0:T(8,128)S(1)}, f32[32,128]{1,0:T(8,128)S(1)}, u32[]{:S(2)}, u32[]{:S(2)}) collective-permute-start(f32[32,128]{1,0:T(8,128)S(1)} %local_maxima.1), channel_id=1, source_target_pairs={{0,1},{1,0},{2,3},{3,2},{4,5},{5,4},{6,7},{7,6},{8,9},{9,8},{10,11... | collective-permute-start | bytes 49160 | tf_op jit(solution)/shard_map/ppermute | solution.py:43
  8.5 0.8 %collective-permute-done.3 = f32[32,128]{1,0:T(8,128)S(1)} collective-permute-done((f32[32,128]{1,0:T(8,128)S(1)}, f32[32,128]{1,0:T(8,128)S(1)}, u32[]{:S(2)}, u32[]{:S(2)}) %collective-permute-start.3) | collective-permute-done | bytes 16416 | tf_op jit(solution)/shard_map/ppermute | solution.py:43
  9.3 1.7 %collective-permute-start.4 = (f32[32,128]{1,0:T(8,128)S(1)}, f32[32,128]{1,0:T(8,128)S(1)}, u32[]{:S(2)}, u32[]{:S(2)}) collective-permute-start(f32[32,128]{1,0:T(8,128)S(1)} %max.6), channel_id=1, source_target_pairs={{0,3},{1,2},{2,1},{3,0},{4,7},{5,6},{6,5},{7,4},{8,11},{9,10},{10,... | collective-permute-start | bytes 49160 | tf_op jit(solution)/shard_map/ppermute | solution.py:44
  11.0 1.4 %collective-permute-done.4 = f32[32,128]{1,0:T(8,128)S(1)} collective-permute-done((f32[32,128]{1,0:T(8,128)S(1)}, f32[32,128]{1,0:T(8,128)S(1)}, u32[]{:S(2)}, u32[]{:S(2)}) %collective-permute-start.4) | collective-permute-done | bytes 16416 | tf_op jit(solution)/shard_map/ppermute | solution.py:44
  12.5 2.8 %collective-permute-start.7 = (f32[32,128]{1,0:T(8,128)S(1)}, f32[32,128]{1,0:T(8,128)S(1)}, u32[]{:S(2)}, u32[]{:S(2)}) collective-permute-start(f32[32,128]{1,0:T(8,128)S(1)} %max.7.refs_0_), channel_id=1, source_target_pairs={{0,9},{1,8},{4,13},{5,12},{8,5},{9,4},{12,1},{13,0},{2,11},{3,10},... | collective-permute-start | bytes 49160 | tf_op jit(solution)/shard_map/ppermute | solution.py:53
  15.3 1.1 %collective-permute-start.6 = (f32[32,128]{1,0:T(8,128)S(1)}, f32[32,128]{1,0:T(8,128)S(1)}, u32[]{:S(2)}, u32[]{:S(2)}) collective-permute-start(f32[32,128]{1,0:T(8,128)S(1)} %max.7.refs_0_), channel_id=1, source_target_pairs={{0,13},{1,12},{4,9},{5,8},{8,1},{9,0},{12,5},{13,4},{2,15},{3,14},... | collective-permute-start | bytes 49160 | tf_op jit(solution)/shard_map/ppermute | solution.py:53
  16.4 0.5 %collective-permute-start.5 = (f32[32,128]{1,0:T(8,128)S(1)}, f32[32,128]{1,0:T(8,128)S(1)}, u32[]{:S(2)}, u32[]{:S(2)}) collective-permute-start(f32[32,128]{1,0:T(8,128)S(1)} %max.7.refs_0_), channel_id=1, source_target_pairs={{0,5},{1,4},{4,1},{5,0},{8,13},{9,12},{12,9},{13,8},{2,7},{3,6},{6... | collective-permute-start | bytes 49160 | tf_op jit(solution)/shard_map/ppermute | solution.py:53
  16.8 0.9 %collective-permute-done.7.refs_3_ = f32[32,128]{1,0:T(8,128)S(1)} collective-permute-done((f32[32,128]{1,0:T(8,128)S(1)}, f32[32,128]{1,0:T(8,128)S(1)}, u32[]{:S(2)}, u32[]{:S(2)}) %collective-permute-start.7) | collective-permute-done | bytes 16416 | tf_op jit(solution)/shard_map/ppermute | solution.py:53
  17.7 1.6 %collective-permute-done.6.refs_2_ = f32[32,128]{1,0:T(8,128)S(1)} collective-permute-done((f32[32,128]{1,0:T(8,128)S(1)}, f32[32,128]{1,0:T(8,128)S(1)}, u32[]{:S(2)}, u32[]{:S(2)}) %collective-permute-start.6) | collective-permute-done | bytes 16416 | tf_op jit(solution)/shard_map/ppermute | solution.py:53
  19.4 0.2 collective-permute-done.5.refs_1_
  19.5 2.1 %rerank.1 = f32[16,256]{1,0:T(8,128)} custom-call(f32[32,128]{1,0:T(8,128)S(1)} %max.7.refs_0_, f32[32,128]{1,0:T(8,128)S(1)} %collective-permute-done.5.refs_1_, f32[32,128]{1,0:T(8,128)S(1)} %collective-permute-done.6.refs_2_, f32[32,128]{1,0:T(8,128)S(1)} %collective-permute-done.7.refs_3_, bf16[80,128]{1,0:T(8,128)(2,1)S(1)} %get-tuple-element.21.refs_4_, ...), custom_call_target="tpu_custom_call" | custom-call | tf_op jit(solution)/shard_map/rerank/pallas_call | solution.py:403
  (2 shorter events, 0.0 us)
Async XLA Ops:
  0.0 7.1 %collective-permute-start.1 = (f32[32,128]{1,0:T(8,128)}, f32[32,128]{1,0:T(8,128)S(1)}, u32[]{:S(2)}, u32[]{:S(2)}) collective-permute-start(f32[32,128]{1,0:T(8,128)} %refs_0_.3), channel_id=1, source_target_pairs={{0,2},{1,3},{2,0},{3,1},{4,6},{5,7},{6,4},{7,5},{8,10},{9,11},{10,... | collective-permute-start | bytes 49160 | tf_op jit(solution)/shard_map/ppermute | solution.py:36
  2.9 4.1 %collective-permute-start = (f32[32,128]{1,0:T(8,128)}, f32[32,128]{1,0:T(8,128)S(1)}, u32[]{:S(2)}, u32[]{:S(2)}) collective-permute-start(f32[32,128]{1,0:T(8,128)} %refs_0_.3), channel_id=1, source_target_pairs={{0,1},{1,0},{2,3},{3,2},{4,5},{5,4},{6,7},{7,6},{8,9},{9,8},{10,11... | collective-permute-start | bytes 49160 | tf_op jit(solution)/shard_map/ppermute | solution.py:36
  2.9 4.2 %collective-permute-start.2 = (f32[32,128]{1,0:T(8,128)}, f32[32,128]{1,0:T(8,128)S(1)}, u32[]{:S(2)}, u32[]{:S(2)}) collective-permute-start(f32[32,128]{1,0:T(8,128)} %refs_0_.3), channel_id=1, source_target_pairs={{0,3},{1,2},{2,1},{3,0},{4,7},{5,6},{6,5},{7,4},{8,11},{9,10},{10,... | collective-permute-start | bytes 49160 | tf_op jit(solution)/shard_map/ppermute | solution.py:36
  3.1 4.0 %copy-start = (f32[32,128]{1,0:T(8,128)S(1)}, f32[32,128]{1,0:T(8,128)}, u32[]{:S(2)}) copy-start(f32[32,128]{1,0:T(8,128)} %refs_0_.3) | copy-start | bytes 49156
  8.0 1.3 %collective-permute-start.3 = (f32[32,128]{1,0:T(8,128)S(1)}, f32[32,128]{1,0:T(8,128)S(1)}, u32[]{:S(2)}, u32[]{:S(2)}) collective-permute-start(f32[32,128]{1,0:T(8,128)S(1)} %local_maxima.1), channel_id=1, source_target_pairs={{0,1},{1,0},{2,3},{3,2},{4,5},{5,4},{6,7},{7,6},{8,9},{9,8},{10,11... | collective-permute-start | bytes 49160 | tf_op jit(solution)/shard_map/ppermute | solution.py:43
  9.3 3.2 %collective-permute-start.4 = (f32[32,128]{1,0:T(8,128)S(1)}, f32[32,128]{1,0:T(8,128)S(1)}, u32[]{:S(2)}, u32[]{:S(2)}) collective-permute-start(f32[32,128]{1,0:T(8,128)S(1)} %max.6), channel_id=1, source_target_pairs={{0,3},{1,2},{2,1},{3,0},{4,7},{5,6},{6,5},{7,4},{8,11},{9,10},{10,... | collective-permute-start | bytes 49160 | tf_op jit(solution)/shard_map/ppermute | solution.py:44
  12.5 5.3 %collective-permute-start.7 = (f32[32,128]{1,0:T(8,128)S(1)}, f32[32,128]{1,0:T(8,128)S(1)}, u32[]{:S(2)}, u32[]{:S(2)}) collective-permute-start(f32[32,128]{1,0:T(8,128)S(1)} %max.7.refs_0_), channel_id=1, source_target_pairs={{0,9},{1,8},{4,13},{5,12},{8,5},{9,4},{12,1},{13,0},{2,11},{3,10},... | collective-permute-start | bytes 49160 | tf_op jit(solution)/shard_map/ppermute | solution.py:53
  15.3 4.1 %collective-permute-start.6 = (f32[32,128]{1,0:T(8,128)S(1)}, f32[32,128]{1,0:T(8,128)S(1)}, u32[]{:S(2)}, u32[]{:S(2)}) collective-permute-start(f32[32,128]{1,0:T(8,128)S(1)} %max.7.refs_0_), channel_id=1, source_target_pairs={{0,13},{1,12},{4,9},{5,8},{8,1},{9,0},{12,5},{13,4},{2,15},{3,14},... | collective-permute-start | bytes 49160 | tf_op jit(solution)/shard_map/ppermute | solution.py:53
  16.4 3.2 %collective-permute-start.5 = (f32[32,128]{1,0:T(8,128)S(1)}, f32[32,128]{1,0:T(8,128)S(1)}, u32[]{:S(2)}, u32[]{:S(2)}) collective-permute-start(f32[32,128]{1,0:T(8,128)S(1)} %max.7.refs_0_), channel_id=1, source_target_pairs={{0,5},{1,4},{4,1},{5,0},{8,13},{9,12},{12,9},{13,8},{2,7},{3,6},{6... | collective-permute-start | bytes 49160 | tf_op jit(solution)/shard_map/ppermute | solution.py:53

commit v4 on v3

--- a/solution.py
+++ b/solution.py
@@ -16,14 +16,15 @@
 NOTHING = -1e30
 CHUNKS = 4
 PART_PAIRS = ((0, 0), (0, 1), (0, 2), (1, 0), (1, 1), (2, 0))
-DOC_STEPS = ((2, 3, 1, 0), (3, 2, 0, 1), (1, 0, 3, 2))
+FIRST_STEP = ((2, 3, 0, 1), (1, 2, 3, 0))
+SECOND_STEP = (3, 0, 1, 2)
 
 
 def compact():
     return (
         lax.axis_size("cent") == 2
         and lax.axis_size("sub") == 2
-        and lax.axis_size("docs") == len(DOC_STEPS) + 1
+        and lax.axis_size("docs") == len(SECOND_STEP)
     )
 
 
@@ -47,12 +48,20 @@
 def gather_docs(values):
     if not compact():
         return [lax.all_gather(values, "docs", axis=0, tiled=True)], [None]
-    pieces, sources = [values], [[0, 1, 2, 3]]
-    for step in reversed(DOC_STEPS):
-        pairs = [(2 * d + c, 2 * step[d] + 1 - c) for d in range(4) for c in range(2)]
-        pieces.append(lax.ppermute(values, ("docs", "sub"), pairs))
-        sources.append([step.index(d) for d in range(4)])
-    return pieces, sources
+    axes = ("docs", "sub")
+    places = [(d, c) for d in range(4) for c in range(2)]
+    first = lax.ppermute(values, axes, [(2 * d + c, 2 * FIRST_STEP[c][d] + c) for d, c in places])
+    second = lax.ppermute(
+        values, axes, [(2 * d + c, 2 * SECOND_STEP[d] + 1 - c) for d, c in places]
+    )
+    other = lax.ppermute(first, "sub", [(0, 1), (1, 0)])
+    sources = [
+        [d for d, _ in places],
+        [FIRST_STEP[c].index(d) for d, c in places],
+        [FIRST_STEP[1 - c].index(d) for d, c in places],
+        [SECOND_STEP.index(d) for d, _ in places],
+    ]
+    return [values, first, other, second], sources
 
 
 def place(pieces, sources, out_ref, axes):
@@ -363,7 +372,7 @@
     ) = refs
     rows = out_ref.shape[0]
     cand = chosen.shape[0] - rows
-    place(pieces, sources, maxima, "docs")
+    place(pieces, sources, maxima, ("docs", "sub"))
 
     width = maxima.shape[1]
     own = pltpu.roll(maxima[...], lax.rem(width - lax.axis_index("docs") * QT, width), 1)

time: 21.8 us -> 21 us (0.963)
  waiting for transfers between devices: 5 us -> 4.34 us
    ppermute x3, waiting for transfers between devices: 2.71 us -> 2.05 us  [the longest x1 1.17 us: gather_docs(): lax.ppermute(values, axes, [(2 * d + c, 2 * SECOND_STEP[d] + 1 - c) for d...]
  transfers between devices with their start and end apart: 8 -> 8, of which waited for: 5 -> 4; matrix products, arithmetic and copies ran while one was open for 0% -> 0% of each run, Pallas kernels for 18% -> 19%
where the time goes in v4:
time: 21 us; the launch traced here: 20.9 us
  starting transfers between devices  9.46 us (45%)
  Pallas kernels  7 us (33%)
  waiting for transfers between devices  4.34 us (21%)
    pallas_call x1, Pallas kernels, prepare(): pl.pallas_call(functools.partial(prepare_kernel, len(kept)), out_shape=[s...  4 us
    ppermute x3, starting transfers between devices, gather_queries(): lax.ppermute(queries, MEMBERS, [(i, i ^ step) for i in range(4)])  3.06 us
    ppermute x1, starting transfers between devices, gather_docs(): lax.ppermute(values, axes, [(2 * d + c, 2 * FIRST_STEP[c][d] + c) for d,...  3.04 us
    pallas_call x1, Pallas kernels, rerank(): pl.pallas_call(functools.partial(rerank_kernel, sources), out_shape=jax.S...  2.13 us
    ppermute x1, starting transfers between devices, best_of_members(): lax.ppermute(values, MEMBERS, [(i, i ^ 3) for i in range(4)])  1.74 us
    ppermute x1, waiting for transfers between devices, best_of_members(): lax.ppermute(values, MEMBERS, [(i, i ^ 3) for i in range(4)])  1.44 us
    ppermute x1, waiting for transfers between devices, gather_docs(): lax.ppermute(values, axes, [(2 * d + c, 2 * SECOND_STEP[d] + 1 - c) for d...  1.17 us
    ppermute x1, waiting for transfers between devices, gather_docs(): lax.ppermute(values, axes, [(2 * d + c, 2 * FIRST_STEP[c][d] + c) for d,...  0.87 us
  transfers between devices with their start and end apart: 8, of which 4 were waited for; matrix products, arithmetic and copies ran while one was open for 0% of the time, Pallas kernels for 19%

profile of v4, /device:TPU:0, one launch (start us, length us, event | category | flops | bytes accessed | tf_op | source)
XLA Modules:
  0.0 20.9 jit_solution(16303877366150521368)
XLA Ops:
  0.0 2.9 %collective-permute-start.1 = (f32[32,128]{1,0:T(8,128)}, f32[32,128]{1,0:T(8,128)S(1)}, u32[]{:S(2)}, u32[]{:S(2)}) collective-permute-start(f32[32,128]{1,0:T(8,128)} %refs_0_.3), channel_id=1, source_target_pairs={{0,2},{1,3},{2,0},{3,1},{4,6},{5,7},{6,4},{7,5},{8,10},{9,11},{10,... | collective-permute-start | bytes 49160 | tf_op jit(solution)/shard_map/ppermute | solution.py:37
  2.9 0.0 collective-permute-start
  2.9 0.1 collective-permute-start.2
  3.1 0.0 copy-start
  3.1 4.0 %prepare.1 = (bf16[2048,512]{1,0:T(8,128)(2,1)S(1)}, s32[32,128]{1,0:T(8,128)S(1)}, bf16[128,256]{1,0:T(8,128)(2,1)S(1)}, bf16[80,128]{1,0:T(8,128)(2,1)S(1)}, b...) custom-call(s32[1,4096]{1,0:T(1,128)} %refs_0_.2, ...), custom_call_target="tpu_custom_call" | custom-call | flops 4000000000 | bytes 4194304 | tf_op jit(solution)/shard_map/prepare/pallas_call | solution.py:252
  7.1 0.0 collective-permute-done.1.refs_2_
  7.1 0.0 collective-permute-done.refs_1_
  7.1 0.0 collective-permute-done.2.refs_3_
  7.1 0.0 copy-done
  7.1 0.9 %local_maxima.1 = f32[32,128]{1,0:T(8,128)S(1)} custom-call(bf16[2048,512]{1,0:T(8,128)(2,1)S(1)} %get-tuple-element.18.left, s32[32,128]{1,0:T(8,128)S(1)} %get-tuple-element.19.live, bf16[128,256]{1,0:T(8,128)(2,1)S(1)} %get-tuple-element.20.spread, f32[32,128]{1,0:T(8,128)S(1)} %copy-done, f32[32,128]{1,0:T(8,128)S(1)} %collective-permute-done.refs_1_, ...), custom_call_target="tpu_custom_call" | custom-call | tf_op jit(solution)/shard_map/local_maxima/pallas_call | solution.py:334
  8.0 0.5 %collective-permute-start.3 = (f32[32,128]{1,0:T(8,128)S(1)}, f32[32,128]{1,0:T(8,128)S(1)}, u32[]{:S(2)}, u32[]{:S(2)}) collective-permute-start(f32[32,128]{1,0:T(8,128)S(1)} %local_maxima.1), channel_id=1, source_target_pairs={{0,1},{1,0},{2,3},{3,2},{4,5},{5,4},{6,7},{7,6},{8,9},{9,8},{10,11... | collective-permute-start | bytes 49160 | tf_op jit(solution)/shard_map/ppermute | solution.py:44
  8.5 0.8 %collective-permute-done.3 = f32[32,128]{1,0:T(8,128)S(1)} collective-permute-done((f32[32,128]{1,0:T(8,128)S(1)}, f32[32,128]{1,0:T(8,128)S(1)}, u32[]{:S(2)}, u32[]{:S(2)}) %collective-permute-start.3) | collective-permute-done | bytes 16416 | tf_op jit(solution)/shard_map/ppermute | solution.py:44
  9.3 1.7 %collective-permute-start.4 = (f32[32,128]{1,0:T(8,128)S(1)}, f32[32,128]{1,0:T(8,128)S(1)}, u32[]{:S(2)}, u32[]{:S(2)}) collective-permute-start(f32[32,128]{1,0:T(8,128)S(1)} %max.6), channel_id=1, source_target_pairs={{0,3},{1,2},{2,1},{3,0},{4,7},{5,6},{6,5},{7,4},{8,11},{9,10},{10,... | collective-permute-start | bytes 49160 | tf_op jit(solution)/shard_map/ppermute | solution.py:45
  11.0 1.4 %collective-permute-done.4 = f32[32,128]{1,0:T(8,128)S(1)} collective-permute-done((f32[32,128]{1,0:T(8,128)S(1)}, f32[32,128]{1,0:T(8,128)S(1)}, u32[]{:S(2)}, u32[]{:S(2)}) %collective-permute-start.4) | collective-permute-done | bytes 16416 | tf_op jit(solution)/shard_map/ppermute | solution.py:45
  12.5 3.0 %collective-permute-start.5 = (f32[32,128]{1,0:T(8,128)S(1)}, f32[32,128]{1,0:T(8,128)S(1)}, u32[]{:S(2)}, u32[]{:S(2)}) collective-permute-start(f32[32,128]{1,0:T(8,128)S(1)} %max.7.refs_0_), channel_id=1, source_target_pairs={{0,8},{1,5},{4,12},{5,9},{8,0},{9,13},{12,4},{13,1},{2,10},{3,7},{... | collective-permute-start | bytes 49160 | tf_op jit(solution)/shard_map/ppermute | solution.py:53
  15.5 0.8 %collective-permute-start.7 = (f32[32,128]{1,0:T(8,128)S(1)}, f32[32,128]{1,0:T(8,128)S(1)}, u32[]{:S(2)}, u32[]{:S(2)}) collective-permute-start(f32[32,128]{1,0:T(8,128)S(1)} %max.7.refs_0_), channel_id=1, source_target_pairs={{0,13},{1,12},{4,1},{5,0},{8,5},{9,4},{12,9},{13,8},{2,15},{3,14},... | collective-permute-start | bytes 49160 | tf_op jit(solution)/shard_map/ppermute | solution.py:54
  16.4 0.9 %collective-permute-done.5.refs_1_ = f32[32,128]{1,0:T(8,128)S(1)} collective-permute-done((f32[32,128]{1,0:T(8,128)S(1)}, f32[32,128]{1,0:T(8,128)S(1)}, u32[]{:S(2)}, u32[]{:S(2)}) %collective-permute-start.5) | collective-permute-done | bytes 16416 | tf_op jit(solution)/shard_map/ppermute | solution.py:53
  17.2 0.3 %collective-permute-start.6 = (f32[32,128]{1,0:T(8,128)S(1)}, f32[32,128]{1,0:T(8,128)S(1)}, u32[]{:S(2)}, u32[]{:S(2)}) collective-permute-start(f32[32,128]{1,0:T(8,128)S(1)} %collective-permute-done.5.refs_1_), channel_id=1, source_target_pairs={{0,1},{1,0},{2,3},{3,2},{4,5},{5,4},{6,7},{7,6},{8,9},{9,8},{10,11... | collective-permute-start | bytes 49160 | tf_op jit(solution)/shard_map/ppermute | solution.py:57
  17.6 1.2 %collective-permute-done.7.refs_3_ = f32[32,128]{1,0:T(8,128)S(1)} collective-permute-done((f32[32,128]{1,0:T(8,128)S(1)}, f32[32,128]{1,0:T(8,128)S(1)}, u32[]{:S(2)}, u32[]{:S(2)}) %collective-permute-start.7) | collective-permute-done | bytes 16416 | tf_op jit(solution)/shard_map/ppermute | solution.py:54
  18.7 0.0 collective-permute-done.6.refs_2_
  18.7 2.1 %rerank.1 = f32[16,256]{1,0:T(8,128)} custom-call(f32[32,128]{1,0:T(8,128)S(1)} %max.7.refs_0_, f32[32,128]{1,0:T(8,128)S(1)} %collective-permute-done.5.refs_1_, f32[32,128]{1,0:T(8,128)S(1)} %collective-permute-done.6.refs_2_, f32[32,128]{1,0:T(8,128)S(1)} %collective-permute-done.7.refs_3_, bf16[80,128]{1,0:T(8,128)(2,1)S(1)} %get-tuple-element.21.refs_4_, ...), custom_call_target="tpu_custom_call" | custom-call | tf_op jit(solution)/shard_map/rerank/pallas_call | solution.py:412
  (2 shorter events, 0.0 us)
Async XLA Ops:
  0.0 7.1 %collective-permute-start.1 = (f32[32,128]{1,0:T(8,128)}, f32[32,128]{1,0:T(8,128)S(1)}, u32[]{:S(2)}, u32[]{:S(2)}) collective-permute-start(f32[32,128]{1,0:T(8,128)} %refs_0_.3), channel_id=1, source_target_pairs={{0,2},{1,3},{2,0},{3,1},{4,6},{5,7},{6,4},{7,5},{8,10},{9,11},{10,... | collective-permute-start | bytes 49160 | tf_op jit(solution)/shard_map/ppermute | solution.py:37
  2.9 4.1 %collective-permute-start = (f32[32,128]{1,0:T(8,128)}, f32[32,128]{1,0:T(8,128)S(1)}, u32[]{:S(2)}, u32[]{:S(2)}) collective-permute-start(f32[32,128]{1,0:T(8,128)} %refs_0_.3), channel_id=1, source_target_pairs={{0,1},{1,0},{2,3},{3,2},{4,5},{5,4},{6,7},{7,6},{8,9},{9,8},{10,11... | collective-permute-start | bytes 49160 | tf_op jit(solution)/shard_map/ppermute | solution.py:37
  2.9 4.2 %collective-permute-start.2 = (f32[32,128]{1,0:T(8,128)}, f32[32,128]{1,0:T(8,128)S(1)}, u32[]{:S(2)}, u32[]{:S(2)}) collective-permute-start(f32[32,128]{1,0:T(8,128)} %refs_0_.3), channel_id=1, source_target_pairs={{0,3},{1,2},{2,1},{3,0},{4,7},{5,6},{6,5},{7,4},{8,11},{9,10},{10,... | collective-permute-start | bytes 49160 | tf_op jit(solution)/shard_map/ppermute | solution.py:37
  3.1 4.0 %copy-start = (f32[32,128]{1,0:T(8,128)S(1)}, f32[32,128]{1,0:T(8,128)}, u32[]{:S(2)}) copy-start(f32[32,128]{1,0:T(8,128)} %refs_0_.3) | copy-start | bytes 49156
  8.0 1.3 %collective-permute-start.3 = (f32[32,128]{1,0:T(8,128)S(1)}, f32[32,128]{1,0:T(8,128)S(1)}, u32[]{:S(2)}, u32[]{:S(2)}) collective-permute-start(f32[32,128]{1,0:T(8,128)S(1)} %local_maxima.1), channel_id=1, source_target_pairs={{0,1},{1,0},{2,3},{3,2},{4,5},{5,4},{6,7},{7,6},{8,9},{9,8},{10,11... | collective-permute-start | bytes 49160 | tf_op jit(solution)/shard_map/ppermute | solution.py:44
  9.3 3.2 %collective-permute-start.4 = (f32[32,128]{1,0:T(8,128)S(1)}, f32[32,128]{1,0:T(8,128)S(1)}, u32[]{:S(2)}, u32[]{:S(2)}) collective-permute-start(f32[32,128]{1,0:T(8,128)S(1)} %max.6), channel_id=1, source_target_pairs={{0,3},{1,2},{2,1},{3,0},{4,7},{5,6},{6,5},{7,4},{8,11},{9,10},{10,... | collective-permute-start | bytes 49160 | tf_op jit(solution)/shard_map/ppermute | solution.py:45
  12.5 4.8 %collective-permute-start.5 = (f32[32,128]{1,0:T(8,128)S(1)}, f32[32,128]{1,0:T(8,128)S(1)}, u32[]{:S(2)}, u32[]{:S(2)}) collective-permute-start(f32[32,128]{1,0:T(8,128)S(1)} %max.7.refs_0_), channel_id=1, source_target_pairs={{0,8},{1,5},{4,12},{5,9},{8,0},{9,13},{12,4},{13,1},{2,10},{3,7},{... | collective-permute-start | bytes 49160 | tf_op jit(solution)/shard_map/ppermute | solution.py:53
  15.5 3.2 %collective-permute-start.7 = (f32[32,128]{1,0:T(8,128)S(1)}, f32[32,128]{1,0:T(8,128)S(1)}, u32[]{:S(2)}, u32[]{:S(2)}) collective-permute-start(f32[32,128]{1,0:T(8,128)S(1)} %max.7.refs_0_), channel_id=1, source_target_pairs={{0,13},{1,12},{4,1},{5,0},{8,5},{9,4},{12,9},{13,8},{2,15},{3,14},... | collective-permute-start | bytes 49160 | tf_op jit(solution)/shard_map/ppermute | solution.py:54
  17.2 1.5 %collective-permute-start.6 = (f32[32,128]{1,0:T(8,128)S(1)}, f32[32,128]{1,0:T(8,128)S(1)}, u32[]{:S(2)}, u32[]{:S(2)}) collective-permute-start(f32[32,128]{1,0:T(8,128)S(1)} %collective-permute-done.5.refs_1_), channel_id=1, source_target_pairs={{0,1},{1,0},{2,3},{3,2},{4,5},{5,4},{6,7},{7,6},{8,9},{9,8},{10,11... | collective-permute-start | bytes 49160 | tf_op jit(solution)/shard_map/ppermute | solution.py:57

commit v5 on v4

--- a/solution.py
+++ b/solution.py
@@ -14,8 +14,8 @@
 HEAD = 64
 MEMBERS = ("cent", "sub")
 NOTHING = -1e30
-CHUNKS = 4
 PART_PAIRS = ((0, 0), (0, 1), (0, 2), (1, 0), (1, 1), (2, 0))
+QUERY_STEPS = ((2, 3, 1, 0), (1, 0, 3, 2), (3, 2, 0, 1))
 FIRST_STEP = ((2, 3, 0, 1), (1, 2, 3, 0))
 SECOND_STEP = (3, 0, 1, 2)
 
@@ -32,9 +32,9 @@
     if not compact():
         return [lax.all_gather(queries, MEMBERS, axis=0, tiled=True)], [None]
     pieces, sources = [queries], [[0, 1, 2, 3]]
-    for step in (1, 2, 3):
-        sources.append([i ^ step for i in range(4)])
-        pieces.append(lax.ppermute(queries, MEMBERS, [(i, i ^ step) for i in range(4)]))
+    for step in QUERY_STEPS:
+        sources.append([step.index(i) for i in range(4)])
+        pieces.append(lax.ppermute(queries, MEMBERS, list(enumerate(step))))
     return pieces, sources
 
 
@@ -95,10 +95,14 @@
 
 
 def even_odd_columns():
-    wide = lax.broadcasted_iota(jnp.int32, (DIM, 2 * DIM), 1)
-    dim = lax.broadcasted_iota(jnp.int32, (DIM, 2 * DIM), 0)
-    wanted = 2 * jnp.bitwise_and(wide, 63) + jnp.right_shift(wide, 7)
+    column = lax.broadcasted_iota(jnp.int32, (DIM, DIM), 1)
+    dim = lax.broadcasted_iota(jnp.int32, (DIM, DIM), 0)
+    wanted = 2 * jnp.bitwise_and(column, 63) + jnp.right_shift(column, 6)
     return jnp.where(wanted == dim, 1.0, 0.0).astype(jnp.bfloat16)
+
+
+def product(left, right):
+    return jnp.dot(left, right, preferred_element_type=jnp.float32)
 
 
 def three_parts(values):
@@ -117,71 +121,120 @@
     return jnp.where(nibbles >= 8, upper, lower)
 
 
-def prepare_kernel(n_kept, *refs):
-    ids_hbm, counts_hbm, candidates_hbm, codes_hbm, centroids_hbm, buckets_hbm, proj_hbm = refs[:7]
-    kept_hbm, refs = refs[7 : 7 + n_kept], refs[7 + n_kept :]
-    left, live, spread, chosen, proj_parts = refs[:5]
-    kept, refs = refs[5 : 5 + n_kept], refs[5 + n_kept :]
-    ids, counts, candidates, codes, centroids, buckets, proj, table, sems, chunk_sems, code_sems, kept_sems = refs
+def early_kernel(spread):
+    spread[...] = even_odd_columns()
+
+
+def early():
+    return pl.pallas_call(
+        early_kernel,
+        out_shape=jax.ShapeDtypeStruct((DIM, DIM), jnp.bfloat16),
+        out_specs=vmem(),
+        compiler_params=pltpu.CompilerParams(vmem_limit_bytes=4 * 2**20),
+        cost_estimate=pl.CostEstimate(flops=4 * 10**9, bytes_accessed=0, transcendentals=0),
+        name="early",
+    )()
+
+
+def prepare_kernel(n_kept, ids_vmem, codes, centroids, buckets, spread, counts_hbm, *refs):
+    kept_hbm, (left, live), refs = refs[:n_kept], refs[n_kept : n_kept + 2], refs[n_kept + 2 :]
+    kept, (ids, counts, table, sems, kept_sems) = refs[:n_kept], refs[n_kept:]
     docs, columns = codes.shape
     pairs = columns // DIM
     slots = 2 * pairs
-    cand = candidates.shape[1]
-    rows_dev = chosen.shape[0] - cand
-
-    chunk = centroids.shape[0] // CHUNKS
-    chunks = [
-        pltpu.make_async_copy(
-            centroids_hbm.at[pl.ds(i * chunk, chunk), :],
-            centroids.at[pl.ds(i * chunk, chunk), :],
-            chunk_sems.at[i],
-        )
-        for i in range(CHUNKS)
-    ]
-    small = [
+    scalars = [
         pltpu.make_async_copy(source, target, sems.at[i])
-        for i, (source, target) in enumerate(
-            (
-                (ids_hbm, ids),
-                (buckets_hbm, buckets),
-                (counts_hbm, counts),
-                (candidates_hbm, candidates),
-                (proj_hbm, proj),
-            )
-        )
-    ]
-    part = columns // CHUNKS
-    code_chunks = [
-        pltpu.make_async_copy(
-            codes_hbm.at[:, pl.ds(i * part, part)],
-            codes.at[:, pl.ds(i * part, part)],
-            code_sems.at[i],
-        )
-        for i in range(CHUNKS)
+        for i, (source, target) in enumerate(((ids_vmem, ids), (counts_hbm, counts)))
     ]
     late = [
         pltpu.make_async_copy(source, target, kept_sems.at[i])
         for i, (source, target) in enumerate(zip(kept_hbm, kept))
     ]
-    for copy in small + chunks + code_chunks:
+    for copy in scalars + late:
         copy.start()
-    columns_of = even_odd_columns()
-    spread[...] = columns_of
-
-    small[1].wait()
-    levels = jnp.dot(
-        buckets[...].astype(jnp.bfloat16), columns_of, preferred_element_type=jnp.float32
-    )
-    tables = [[levels[i : i + 8, k : k + DIM] for i in (0, 8)] for k in (0, DIM)]
-    small[2].wait()
+    levels = sum(product(part, spread[...]) for part in three_parts(buckets[...]))
+    halves = [levels[:8], levels[8:]]
+    for first in range(0, centroids.shape[0], 512):
+        table[first : first + 512, :] = product(centroids[first : first + 512, :], spread[...])
+    first_half = lax.broadcasted_iota(jnp.int32, (8, DIM), 1) < DIM // 2
     doc_row = lax.broadcasted_iota(jnp.int32, (8, DIM), 0)
+    scalars[0].wait()
+    row_bits = [jnp.bitwise_and(doc_row, bit) != 0 for bit in (1, 2, 4)]
+
+    def fetch(slot, first):
+        rows = []
+        for n in range(first, first + 8):
+            row = table[pl.ds(ids[0, n * slots + slot], 1), :]
+            rows.append(jnp.broadcast_to(row, (8, DIM)))
+        for bit in row_bits:
+            rows = [jnp.where(bit, rows[i + 1], rows[i]) for i in range(0, len(rows), 2)]
+        return rows[0]
+
+    def one_pair(pair, carry):
+        start = pl.multiple_of(pair * docs, docs)
+        column = pl.multiple_of(pair * DIM, DIM)
+        parts = [[], []]
+        for b in range(0, docs, 8):
+            code = codes[b : b + 8, pl.ds(column, DIM)]
+            other = pltpu.roll(code, DIM // 2, 1)
+            nibbles = (
+                jnp.where(first_half, jnp.bitwise_and(code, 15), jnp.right_shift(other, 4)),
+                jnp.where(first_half, jnp.bitwise_and(other, 15), jnp.right_shift(code, 4)),
+            )
+            for k in range(2):
+                parts[k].append(fetch(2 * pair + k, b) + look_up(nibbles[k], halves))
+        for k, part in enumerate(parts):
+            columns = slice(k * DIM, (k + 1) * DIM)
+            left[pl.ds(start, docs), columns] = jnp.concatenate(part, axis=0).astype(jnp.bfloat16)
+        return carry
+
+    lax.fori_loop(0, pairs, one_pair, 0, unroll=True)
+    scalars[1].wait()
     for b in range(docs // 8):
         block = jnp.zeros((8, DIM), jnp.int32)
         for n in range(8):
             block = jnp.where(doc_row == n, counts[0, b * 8 + n], block)
         live[b * 8 : b * 8 + 8, :] = block
-
-    small[3].wait()
+    for copy in late:
+        copy.wait()
+
+
+def prepare(ids, counts, codes, centroids, buckets, spread, kept):
+    docs, columns = codes.shape
+    pairs = columns // DIM
+    shape = jax.ShapeDtypeStruct
+    return pl.pallas_call(
+        functools.partial(prepare_kernel, len(kept)),
+        out_shape=[
+            shape((pairs * docs, 2 * DIM), jnp.bfloat16),
+            shape((docs, DIM), jnp.int32),
+        ]
+        + [shape(array.shape, array.dtype) for array in kept],
+        in_specs=[vmem()] * 5 + [hbm()] * (1 + len(kept)),
+        out_specs=[vmem()] * (2 + len(kept)),
+        scratch_shapes=[
+            pltpu.SMEM(ids.shape, jnp.int32),
+            pltpu.SMEM(counts.shape, jnp.int32),
+            pltpu.VMEM(centroids.shape, jnp.float32),
+            pltpu.SemaphoreType.DMA((2,)),
+            pltpu.SemaphoreType.DMA((len(kept),)),
+        ],
+        compiler_params=pltpu.CompilerParams(vmem_limit_bytes=24 * 2**20),
+        cost_estimate=pl.CostEstimate(flops=4 * 10**9, bytes_accessed=2**22, transcendentals=0),
+        name="prepare",
+    )(ids, codes, centroids, buckets, spread, *[in_hbm(x) for x in (counts, *kept)])
+
+
+def tables_kernel(candidates_vmem, proj, _, chosen, proj_parts, candidates, sem):
+    cand = candidates.shape[1]
+    rows_dev = chosen.shape[0] - cand
+    copy = pltpu.make_async_copy(candidates_vmem, candidates, sem)
+    copy.start()
+    parts = three_parts(proj[...])
+    for i, k in enumerate(PART_PAIRS):
+        proj_parts[i * QT : (i + 1) * QT, :] = parts[k[1]]
+
+    copy.wait()
     docs_all = chosen.shape[1]
     member = lax.axis_index(MEMBERS)
     doc = lax.broadcasted_iota(jnp.int32, (16, docs_all), 1)
@@ -197,93 +250,23 @@
         return carry
 
     lax.fori_loop(0, chosen.shape[0] // 16, choose, 0)
-    small[4].wait()
-    parts = three_parts(proj[...])
-    for i, k in enumerate(PART_PAIRS):
-        proj_parts[i * QT : (i + 1) * QT, :] = parts[k[1]]
-
-    for i, copy in enumerate(chunks):
-        copy.wait()
-        for first in range(i * chunk, (i + 1) * chunk, 256):
-            table[first : first + 256, :] = centroids[first : first + 256, :].astype(jnp.float32)
-    small[0].wait()
-    row_bits = [jnp.bitwise_and(doc_row, bit) != 0 for bit in (1, 2, 4)]
-
-    def fetch(slot, first):
-        rows = []
-        for n in range(first, first + 8):
-            row = table[pl.ds(ids[0, n * slots + slot], 1), :]
-            rows.append(jnp.broadcast_to(row, (8, DIM)))
-        for bit in row_bits:
-            rows = [jnp.where(bit, rows[i + 1], rows[i]) for i in range(0, len(rows), 2)]
-        return rows[0]
-
-    def one_pair(pair, carry):
-        start = pl.multiple_of(pair * docs, docs)
-        column = pl.multiple_of(pair * DIM, DIM)
-        parts = [[], [], [], []]
-        for b in range(0, docs, 8):
-            code = codes[b : b + 8, pl.ds(column, DIM)]
-            parts[0].append(fetch(2 * pair, b))
-            parts[1].append(fetch(2 * pair + 1, b))
-            parts[2].append(look_up(jnp.bitwise_and(code, 15), tables[0]))
-            parts[3].append(look_up(jnp.right_shift(code, 4), tables[1]))
-        for k, part in enumerate(parts):
-            columns = slice(k * DIM, (k + 1) * DIM)
-            left[pl.ds(start, docs), columns] = jnp.concatenate(part, axis=0).astype(jnp.bfloat16)
-        return carry
-
-    for i, copy in enumerate(code_chunks):
-        copy.wait()
-        if i == 1:
-            for other in late:
-                other.start()
-        lax.fori_loop(
-            i * pairs // CHUNKS, (i + 1) * pairs // CHUNKS, one_pair, 0, unroll=True
-        )
-    for copy in late:
-        copy.wait()
-
-
-def prepare(ids, counts, candidates, codes, centroids, buckets, input_proj, docs_all, rows, kept):
-    docs, columns = codes.shape
-    pairs = columns // DIM
+
+
+def make_tables(candidates, input_proj, best, docs_all, rows):
     shape = jax.ShapeDtypeStruct
     return pl.pallas_call(
-        functools.partial(prepare_kernel, len(kept)),
+        tables_kernel,
         out_shape=[
-            shape((pairs * docs, 4 * DIM), jnp.bfloat16),
-            shape((docs, DIM), jnp.int32),
-            shape((DIM, 2 * DIM), jnp.bfloat16),
             shape((candidates.shape[1] + rows, docs_all), jnp.bfloat16),
             shape((len(PART_PAIRS) * QT, H), jnp.bfloat16),
-        ]
-        + [shape(array.shape, array.dtype) for array in kept],
-        in_specs=[hbm()] * (7 + len(kept)),
-        out_specs=[vmem()] * (5 + len(kept)),
-        scratch_shapes=[
-            pltpu.SMEM(ids.shape, jnp.int32),
-            pltpu.SMEM(counts.shape, jnp.int32),
-            pltpu.SMEM(candidates.shape, jnp.int32),
-            pltpu.VMEM(codes.shape, jnp.int32),
-            pltpu.VMEM(centroids.shape, jnp.bfloat16),
-            pltpu.VMEM(buckets.shape, jnp.float32),
-            pltpu.VMEM(input_proj.shape, jnp.float32),
-            pltpu.VMEM(centroids.shape, jnp.float32),
-            pltpu.SemaphoreType.DMA((5,)),
-            pltpu.SemaphoreType.DMA((CHUNKS,)),
-            pltpu.SemaphoreType.DMA((CHUNKS,)),
-            pltpu.SemaphoreType.DMA((len(kept),)),
         ],
-        compiler_params=pltpu.CompilerParams(vmem_limit_bytes=24 * 2**20),
-        cost_estimate=pl.CostEstimate(flops=4 * 10**9, bytes_accessed=2**22, transcendentals=0),
-        name="prepare",
-    )(
-        *[
-            in_hbm(x)
-            for x in (ids, counts, candidates, codes, centroids, buckets, input_proj, *kept)
-        ]
-    )
+        in_specs=[vmem(), vmem(), pl.BlockSpec(memory_space=pl.ANY)],
+        out_specs=[vmem()] * 2,
+        scratch_shapes=[pltpu.SMEM(candidates.shape, jnp.int32), pltpu.SemaphoreType.DMA],
+        compiler_params=pltpu.CompilerParams(vmem_limit_bytes=16 * 2**20),
+        cost_estimate=pl.CostEstimate(flops=5 * 10**8, bytes_accessed=0, transcendentals=0),
+        name="make_tables",
+    )(candidates, input_proj, best)
 
 
 def score_kernel(sources, docs, left, live, spread, *refs):
@@ -292,16 +275,12 @@
     pairs = left.shape[0] // docs
     place(pieces, sources, queries, MEMBERS)
     query_bf = queries[...].astype(jnp.bfloat16)
-    query_pair = jnp.dot(query_bf, spread[...], preferred_element_type=jnp.float32)
-    lane = lax.broadcasted_iota(jnp.int32, (query_rows, 2 * DIM), 1)
-    first = jnp.bitwise_and(lane, 64) == 0
+    query_bf = product(query_bf, spread[...]).astype(jnp.bfloat16)
     none = jnp.zeros((query_rows, DIM), jnp.bfloat16)
     right[:query_rows, :DIM] = query_bf
-    right[:query_rows, DIM : 2 * DIM] = none
-    right[:query_rows, 2 * DIM :] = jnp.where(first, query_pair, 0.0).astype(jnp.bfloat16)
+    right[:query_rows, DIM:] = none
     right[query_rows:, :DIM] = none
-    right[query_rows:, DIM : 2 * DIM] = query_bf
-    right[query_rows:, 2 * DIM :] = jnp.where(first, 0.0, query_pair).astype(jnp.bfloat16)
+    right[query_rows:, DIM:] = query_bf
 
     counts = jnp.concatenate([live[...]] * (query_rows // DIM), axis=1)
     block = pairs if query_rows == DIM else 4
@@ -338,7 +317,7 @@
         out_specs=vmem(),
         scratch_shapes=[
             pltpu.VMEM((query_rows, DIM), jnp.float32),
-            pltpu.VMEM((2 * query_rows, 4 * DIM), jnp.bfloat16),
+            pltpu.VMEM((2 * query_rows, 2 * DIM), jnp.bfloat16),
         ],
         compiler_params=pltpu.CompilerParams(vmem_limit_bytes=24 * 2**20),
         name="local_maxima",
@@ -348,10 +327,6 @@
 def rms_scale(values, gain):
     mean_square = jnp.mean(values * values, axis=-1, keepdims=True)
     return (values * lax.rsqrt(mean_square + 1e-06) * gain).astype(jnp.bfloat16)
-
-
-def product(left, right):
-    return jnp.dot(left, right, preferred_element_type=jnp.float32)
 
 
 def rerank_kernel(sources, *refs):
@@ -451,21 +426,14 @@
     docs_all = slot_counts.shape[1] * lax.axis_size("docs")
     rows = candidates.shape[1] // lax.axis_size(MEMBERS)
     query_pieces, query_sources = gather_queries(queries)
-    left, live, spread, *staged = prepare(
-        centroid_ids,
-        slot_counts,
-        candidates,
-        token_codes[0],
-        centroids,
-        bucket_values,
-        input_proj,
-        docs_all,
-        rows,
-        kept,
+    spread = early()
+    left, live, *staged = prepare(
+        centroid_ids, slot_counts, token_codes[0], centroids, bucket_values, spread, kept
     )
     local_best = local_maxima(left, live, spread, query_pieces, query_sources)
+    tables = make_tables(candidates, input_proj, local_best, docs_all, rows)
     doc_pieces, doc_sources = gather_docs(best_of_members(local_best))
-    return rerank(doc_pieces, doc_sources, staged, rows)[None]
+    return rerank(doc_pieces, doc_sources, [*tables, *staged], rows)[None]
 
 
 def solution(mesh):

time: 21 us -> 20.3 us (0.967)
  starting transfers between devices: 9.46 us -> 7.94 us
  waiting for transfers between devices: 4.34 us -> 5.39 us
  Pallas kernels: 7 us -> 6.66 us
    pallas_call x1, Pallas kernels: 4 us -> 3.25 us  [prepare(): pl.pallas_call(functools.partial(prepare_kernel, len(kept)), out_shape=[s...]
    ppermute x1, waiting for transfers between devices: 1.17 us -> 0.49 us  [gather_docs(): lax.ppermute(values, axes, [(2 * d + c, 2 * SECOND_STEP[d] + 1 - c) for d...]
    pallas_call x0 -> x2, Pallas kernels: none -> 0.66 us  [the longest x1 0.65 us: make_tables(): pl.pallas_call(tables_kernel, out_shape=[shape((candidates.shape[1] + row...]
    ppermute x3, waiting for transfers between devices: 0.01 us -> 0.53 us  [gather_queries(): pieces.append(lax.ppermute(queries, MEMBERS, list(enumerate(step))))]
    ppermute x1, waiting for transfers between devices: 1.44 us -> 1.96 us  [best_of_members(): lax.ppermute(values, MEMBERS, [(i, i ^ 3) for i in range(4)])]
    ppermute x1, starting transfers between devices: 1.74 us -> 1.27 us  [best_of_members(): lax.ppermute(values, MEMBERS, [(i, i ^ 3) for i in range(4)])]
    ppermute x1, starting transfers between devices: 3.04 us -> 2.6 us  [gather_docs(): lax.ppermute(values, axes, [(2 * d + c, 2 * FIRST_STEP[c][d] + c) for d,...]
    ppermute x1, starting transfers between devices: 0.47 us -> 0.07 us  [best_of_members(): values = jnp.maximum(values, lax.ppermute(values, 'sub', [(0, 1), (1, 0)]))]
  transfers between devices with their start and end apart: 8 -> 8, of which waited for: 4 -> 5; matrix products, arithmetic and copies ran while one was open for 0% -> 0% of each run, Pallas kernels for 19% -> 19%
where the time goes in v5:
time: 20.3 us; the launch traced here: 20.1 us
  starting transfers between devices  7.94 us (39%)
  Pallas kernels  6.66 us (33%)
  waiting for transfers between devices  5.39 us (27%)
    pallas_call x1, Pallas kernels, prepare(): pl.pallas_call(functools.partial(prepare_kernel, len(kept)), out_shape=[s...  3.25 us
    ppermute x3, starting transfers between devices, gather_queries(): pieces.append(lax.ppermute(queries, MEMBERS, list(enumerate(step))))  3.16 us
    ppermute x1, starting transfers between devices, gather_docs(): lax.ppermute(values, axes, [(2 * d + c, 2 * FIRST_STEP[c][d] + c) for d,...  2.6 us
    pallas_call x1, Pallas kernels, rerank(): pl.pallas_call(functools.partial(rerank_kernel, sources), out_shape=jax.S...  2.13 us
    ppermute x1, waiting for transfers between devices, best_of_members(): lax.ppermute(values, MEMBERS, [(i, i ^ 3) for i in range(4)])  1.96 us
    ppermute x1, starting transfers between devices, best_of_members(): lax.ppermute(values, MEMBERS, [(i, i ^ 3) for i in range(4)])  1.27 us
    ppermute x1, waiting for transfers between devices, gather_docs(): lax.ppermute(values, axes, [(2 * d + c, 2 * FIRST_STEP[c][d] + c) for d,...  1.21 us
    ppermute x1, waiting for transfers between devices, best_of_members(): values = jnp.maximum(values, lax.ppermute(values, 'sub', [(0, 1), (1, 0)]))  1.17 us
  transfers between devices with their start and end apart: 8, of which 5 were waited for; matrix products, arithmetic and copies ran while one was open for 0% of the time, Pallas kernels for 19%

profile of v5, /device:TPU:0, one launch (start us, length us, event | category | flops | bytes accessed | tf_op | source)
XLA Modules:
  0.0 20.1 jit_solution(3841745698316912246)
XLA Ops:
  0.0 0.0 copy-start.5
  0.0 0.0 copy-start.2
  0.0 0.0 copy-start.1
  0.0 0.5 %collective-permute-start.1 = (f32[32,128]{1,0:T(8,128)}, f32[32,128]{1,0:T(8,128)S(1)}, u32[]{:S(2)}, u32[]{:S(2)}) collective-permute-start(f32[32,128]{1,0:T(8,128)} %refs_0_.1), channel_id=1, source_target_pairs={{0,1},{1,0},{2,3},{3,2},{4,5},{5,4},{6,7},{7,6},{8,9},{9,8},{10,11... | collective-permute-start | bytes 49160 | tf_op jit(solution)/shard_map/ppermute | solution.py:37
  0.5 2.6 %collective-permute-start = (f32[32,128]{1,0:T(8,128)}, f32[32,128]{1,0:T(8,128)S(1)}, u32[]{:S(2)}, u32[]{:S(2)}) collective-permute-start(f32[32,128]{1,0:T(8,128)} %refs_0_.1), channel_id=1, source_target_pairs={{0,2},{1,3},{2,1},{3,0},{4,6},{5,7},{6,5},{7,4},{8,10},{9,11},{10,... | collective-permute-start | bytes 49160 | tf_op jit(solution)/shard_map/ppermute | solution.py:37
  3.1 0.1 collective-permute-start.2
  3.2 0.0 copy-done.5
  3.2 0.0 copy-done.2
  3.2 0.0 copy-done.4
  3.2 0.0 copy-done.1
  3.2 0.0 copy-start
  3.2 3.2 %prepare.1 = (bf16[2048,256]{1,0:T(8,128)(2,1)S(1)}, s32[32,128]{1,0:T(8,128)S(1)}, f32[1,256]{1,0:T(1,128)S(1)}, bf16[256,256]{1,0:T(8,128)(2,1)S(1)}, bf16[256...) custom-call(s32[1,4096]{1,0:T(1,128)S(1)} %copy-done.4, ...), custom_call_target="tpu_custom_call" | custom-call | flops 4000000000 | bytes 4194304 | tf_op jit(solution)/shard_map/prepare/pallas_call | solution.py:206
  6.5 0.0 collective-permute-done.1.refs_2_
  6.5 0.0 collective-permute-done.refs_1_
  6.5 0.5 %collective-permute-done.2.refs_3_ = f32[32,128]{1,0:T(8,128)S(1)} collective-permute-done((f32[32,128]{1,0:T(8,128)}, f32[32,128]{1,0:T(8,128)S(1)}, u32[]{:S(2)}, u32[]{:S(2)}) %collective-permute-start.2) | collective-permute-done | bytes 16416 | tf_op jit(solution)/shard_map/ppermute | solution.py:37
  7.0 0.0 copy-done
  7.0 0.6 %local_maxima.1._ = f32[32,128]{1,0:T(8,128)S(1)} custom-call(bf16[2048,256]{1,0:T(8,128)(2,1)S(1)} %get-tuple-element.17.left, s32[32,128]{1,0:T(8,128)S(1)} %get-tuple-element.18.live, bf16[128,128]{1,0:T(8,128)(2,1)S(1)} %early.1.spread, f32[32,128]{1,0:T(8,128)S(1)} %copy-done, f32[32,128]{1,0:T(8,128)S(1)} %collective-permute-done.refs_1_, ...), custom_call_target="tpu_custom_call" | custom-call | tf_op jit(solution)/shard_map/local_maxima/pallas_call | solution.py:313
  7.7 0.1 collective-permute-start.3
  7.8 1.2 %collective-permute-done.3 = f32[32,128]{1,0:T(8,128)S(1)} collective-permute-done((f32[32,128]{1,0:T(8,128)S(1)}, f32[32,128]{1,0:T(8,128)S(1)}, u32[]{:S(2)}, u32[]{:S(2)}) %collective-permute-start.3) | collective-permute-done | bytes 16416 | tf_op jit(solution)/shard_map/ppermute | solution.py:44
  8.9 0.0 copy-start.3
  8.9 1.3 %collective-permute-start.4 = (f32[32,128]{1,0:T(8,128)S(1)}, f32[32,128]{1,0:T(8,128)S(1)}, u32[]{:S(2)}, u32[]{:S(2)}) collective-permute-start(f32[32,128]{1,0:T(8,128)S(1)} %max.6), channel_id=1, source_target_pairs={{0,3},{1,2},{2,1},{3,0},{4,7},{5,6},{6,5},{7,4},{8,11},{9,10},{10,... | collective-permute-start | bytes 49160 | tf_op jit(solution)/shard_map/ppermute | solution.py:45
  10.2 2.0 %collective-permute-done.4 = f32[32,128]{1,0:T(8,128)S(1)} collective-permute-done((f32[32,128]{1,0:T(8,128)S(1)}, f32[32,128]{1,0:T(8,128)S(1)}, u32[]{:S(2)}, u32[]{:S(2)}) %collective-permute-start.4) | collective-permute-done | bytes 16416 | tf_op jit(solution)/shard_map/ppermute | solution.py:45
  12.2 2.6 %collective-permute-start.5 = (f32[32,128]{1,0:T(8,128)S(1)}, f32[32,128]{1,0:T(8,128)S(1)}, u32[]{:S(2)}, u32[]{:S(2)}) collective-permute-start(f32[32,128]{1,0:T(8,128)S(1)} %max.7.refs_0_), channel_id=1, source_target_pairs={{0,8},{1,5},{4,12},{5,9},{8,0},{9,13},{12,4},{13,1},{2,10},{3,7},{... | collective-permute-start | bytes 49160 | tf_op jit(solution)/shard_map/ppermute | solution.py:53
  14.8 0.8 %collective-permute-start.7 = (f32[32,128]{1,0:T(8,128)S(1)}, f32[32,128]{1,0:T(8,128)S(1)}, u32[]{:S(2)}, u32[]{:S(2)}) collective-permute-start(f32[32,128]{1,0:T(8,128)S(1)} %max.7.refs_0_), channel_id=1, source_target_pairs={{0,13},{1,12},{4,1},{5,0},{8,5},{9,4},{12,9},{13,8},{2,15},{3,14},... | collective-permute-start | bytes 49160 | tf_op jit(solution)/shard_map/ppermute | solution.py:54
  15.6 1.2 %collective-permute-done.5.refs_1_ = f32[32,128]{1,0:T(8,128)S(1)} collective-permute-done((f32[32,128]{1,0:T(8,128)S(1)}, f32[32,128]{1,0:T(8,128)S(1)}, u32[]{:S(2)}, u32[]{:S(2)}) %collective-permute-start.5) | collective-permute-done | bytes 16416 | tf_op jit(solution)/shard_map/ppermute | solution.py:53
  16.8 0.0 collective-permute-start.6
  16.8 0.0 copy-done.3
  16.8 0.0 copy-done.6
  16.8 0.6 %make_tables.1 = (bf16[80,128]{1,0:T(8,128)(2,1)S(1)}, bf16[192,256]{1,0:T(8,128)(2,1)S(1)}) custom-call(s32[1,64]{1,0:T(1,128)S(1)} %copy-done.6, f32[32,256]{1,0:T(8,128)S(1)} %copy-done.3, f32[32,128]{1,0:T(8,128)S(1)} %local_maxima.1._), custom_call_target="tpu_custom_call" | custom-call | flops 500000000 | tf_op jit(solution)/shard_map/make_tables/pallas_call | solution.py:257
  17.5 0.5 %collective-permute-done.7.refs_3_ = f32[32,128]{1,0:T(8,128)S(1)} collective-permute-done((f32[32,128]{1,0:T(8,128)S(1)}, f32[32,128]{1,0:T(8,128)S(1)}, u32[]{:S(2)}, u32[]{:S(2)}) %collective-permute-start.7) | collective-permute-done | bytes 16416 | tf_op jit(solution)/shard_map/ppermute | solution.py:54
  18.0 0.0 collective-permute-done.6.refs_2_
  18.0 2.1 %rerank.1 = f32[16,256]{1,0:T(8,128)} custom-call(f32[32,128]{1,0:T(8,128)S(1)} %max.7.refs_0_, f32[32,128]{1,0:T(8,128)S(1)} %collective-permute-done.5.refs_1_, f32[32,128]{1,0:T(8,128)S(1)} %collective-permute-done.6.refs_2_, f32[32,128]{1,0:T(8,128)S(1)} %collective-permute-done.7.refs_3_, bf16[80,128]{1,0:T(8,128)(2,1)S(1)} %get-tuple-element.19.refs_4_, ...), custom_call_target="tpu_custom_call" | custom-call | tf_op jit(solution)/shard_map/rerank/pallas_call | solution.py:387
  (5 shorter events, 0.0 us)
Async XLA Ops:
  0.0 3.2 %copy-start.5 = (f32[16,128]{1,0:T(8,128)S(1)}, f32[16,128]{1,0:T(8,128)}, u32[]{:S(2)}) copy-start(f32[16,128]{1,0:T(8,128)} %buckets.1) | copy-start | bytes 24580
  0.0 3.2 %copy-start.2 = (bf16[4096,128]{1,0:T(8,128)(2,1)S(1)}, bf16[4096,128]{1,0:T(8,128)(2,1)}, u32[]{:S(2)}) copy-start(bf16[4096,128]{1,0:T(8,128)(2,1)} %centroids.1) | copy-start | bytes 3145732
  0.0 3.2 %copy-start.4 = (s32[1,4096]{1,0:T(1,128)S(1)}, s32[1,4096]{1,0:T(1,128)}, u32[]{:S(2)}) copy-start(s32[1,4096]{1,0:T(1,128)} %ids_vmem.1) | copy-start | bytes 49156
  0.0 3.2 %copy-start.1 = (s32[1,32,8192]{2,1,0:T(8,128)S(1)}, s32[1,32,8192]{2,1,0:T(8,128)}, u32[]{:S(2)}) copy-start(s32[1,32,8192]{2,1,0:T(8,128)} %param.17) | copy-start | bytes 3145732
  0.0 6.5 %collective-permute-start.1 = (f32[32,128]{1,0:T(8,128)}, f32[32,128]{1,0:T(8,128)S(1)}, u32[]{:S(2)}, u32[]{:S(2)}) collective-permute-start(f32[32,128]{1,0:T(8,128)} %refs_0_.1), channel_id=1, source_target_pairs={{0,1},{1,0},{2,3},{3,2},{4,5},{5,4},{6,7},{7,6},{8,9},{9,8},{10,11... | collective-permute-start | bytes 49160 | tf_op jit(solution)/shard_map/ppermute | solution.py:37
  0.5 6.0 %collective-permute-start = (f32[32,128]{1,0:T(8,128)}, f32[32,128]{1,0:T(8,128)S(1)}, u32[]{:S(2)}, u32[]{:S(2)}) collective-permute-start(f32[32,128]{1,0:T(8,128)} %refs_0_.1), channel_id=1, source_target_pairs={{0,2},{1,3},{2,1},{3,0},{4,6},{5,7},{6,5},{7,4},{8,10},{9,11},{10,... | collective-permute-start | bytes 49160 | tf_op jit(solution)/shard_map/ppermute | solution.py:37
  3.1 3.9 %collective-permute-start.2 = (f32[32,128]{1,0:T(8,128)}, f32[32,128]{1,0:T(8,128)S(1)}, u32[]{:S(2)}, u32[]{:S(2)}) collective-permute-start(f32[32,128]{1,0:T(8,128)} %refs_0_.1), channel_id=1, source_target_pairs={{0,3},{1,2},{2,0},{3,1},{4,7},{5,6},{6,4},{7,5},{8,11},{9,10},{10,... | collective-permute-start | bytes 49160 | tf_op jit(solution)/shard_map/ppermute | solution.py:37
  3.2 3.8 %copy-start = (f32[32,128]{1,0:T(8,128)S(1)}, f32[32,128]{1,0:T(8,128)}, u32[]{:S(2)}) copy-start(f32[32,128]{1,0:T(8,128)} %refs_0_.1) | copy-start | bytes 49156
  7.7 1.2 %collective-permute-start.3 = (f32[32,128]{1,0:T(8,128)S(1)}, f32[32,128]{1,0:T(8,128)S(1)}, u32[]{:S(2)}, u32[]{:S(2)}) collective-permute-start(f32[32,128]{1,0:T(8,128)S(1)} %local_maxima.1._), channel_id=1, source_target_pairs={{0,1},{1,0},{2,3},{3,2},{4,5},{5,4},{6,7},{7,6},{8,9},{9,8},{10,11... | collective-permute-start | bytes 49160 | tf_op jit(solution)/shard_map/ppermute | solution.py:44
  8.9 7.9 %copy-start.3 = (f32[32,256]{1,0:T(8,128)S(1)}, f32[32,256]{1,0:T(8,128)}, u32[]{:S(2)}) copy-start(f32[32,256]{1,0:T(8,128)} %proj.1) | copy-start | bytes 98308
  8.9 7.9 %copy-start.6 = (s32[1,64]{1,0:T(1,128)S(1)}, s32[1,64]{1,0:T(1,128)}, u32[]{:S(2)}) copy-start(s32[1,64]{1,0:T(1,128)} %candidates_vmem.1) | copy-start | bytes 772
  8.9 3.2 %collective-permute-start.4 = (f32[32,128]{1,0:T(8,128)S(1)}, f32[32,128]{1,0:T(8,128)S(1)}, u32[]{:S(2)}, u32[]{:S(2)}) collective-permute-start(f32[32,128]{1,0:T(8,128)S(1)} %max.6), channel_id=1, source_target_pairs={{0,3},{1,2},{2,1},{3,0},{4,7},{5,6},{6,5},{7,4},{8,11},{9,10},{10,... | collective-permute-start | bytes 49160 | tf_op jit(solution)/shard_map/ppermute | solution.py:45
  12.2 4.6 %collective-permute-start.5 = (f32[32,128]{1,0:T(8,128)S(1)}, f32[32,128]{1,0:T(8,128)S(1)}, u32[]{:S(2)}, u32[]{:S(2)}) collective-permute-start(f32[32,128]{1,0:T(8,128)S(1)} %max.7.refs_0_), channel_id=1, source_target_pairs={{0,8},{1,5},{4,12},{5,9},{8,0},{9,13},{12,4},{13,1},{2,10},{3,7},{... | collective-permute-start | bytes 49160 | tf_op jit(solution)/shard_map/ppermute | solution.py:53
  14.8 3.2 %collective-permute-start.7 = (f32[32,128]{1,0:T(8,128)S(1)}, f32[32,128]{1,0:T(8,128)S(1)}, u32[]{:S(2)}, u32[]{:S(2)}) collective-permute-start(f32[32,128]{1,0:T(8,128)S(1)} %max.7.refs_0_), channel_id=1, source_target_pairs={{0,13},{1,12},{4,1},{5,0},{8,5},{9,4},{12,9},{13,8},{2,15},{3,14},... | collective-permute-start | bytes 49160 | tf_op jit(solution)/shard_map/ppermute | solution.py:54
  16.8 1.2 %collective-permute-start.6 = (f32[32,128]{1,0:T(8,128)S(1)}, f32[32,128]{1,0:T(8,128)S(1)}, u32[]{:S(2)}, u32[]{:S(2)}) collective-permute-start(f32[32,128]{1,0:T(8,128)S(1)} %collective-permute-done.5.refs_1_), channel_id=1, source_target_pairs={{0,1},{1,0},{2,3},{3,2},{4,5},{5,4},{6,7},{7,6},{8,9},{9,8},{10,11... | collective-permute-start | bytes 49160 | tf_op jit(solution)/shard_map/ppermute | solution.py:57

commit v6 on v5

--- a/solution.py
+++ b/solution.py
@@ -16,15 +16,15 @@
 NOTHING = -1e30
 PART_PAIRS = ((0, 0), (0, 1), (0, 2), (1, 0), (1, 1), (2, 0))
 QUERY_STEPS = ((2, 3, 1, 0), (1, 0, 3, 2), (3, 2, 0, 1))
-FIRST_STEP = ((2, 3, 0, 1), (1, 2, 3, 0))
-SECOND_STEP = (3, 0, 1, 2)
+FIRST_STEP = (4, 9, 11, 6, 8, 13, 10, 15, 12, 0, 2, 14, 5, 1, 7, 3)
+SECOND_STEP = (13, 12, 15, 14, 0, 1, 3, 2, 5, 4, 6, 7, 10, 8, 11, 9)
 
 
 def compact():
     return (
         lax.axis_size("cent") == 2
         and lax.axis_size("sub") == 2
-        and lax.axis_size("docs") == len(SECOND_STEP)
+        and 4 * lax.axis_size("docs") == len(SECOND_STEP)
     )
 
 
@@ -48,18 +48,16 @@
 def gather_docs(values):
     if not compact():
         return [lax.all_gather(values, "docs", axis=0, tiled=True)], [None]
-    axes = ("docs", "sub")
-    places = [(d, c) for d in range(4) for c in range(2)]
-    first = lax.ppermute(values, axes, [(2 * d + c, 2 * FIRST_STEP[c][d] + c) for d, c in places])
-    second = lax.ppermute(
-        values, axes, [(2 * d + c, 2 * SECOND_STEP[d] + 1 - c) for d, c in places]
-    )
+    axes = ("docs", "cent", "sub")
+    first = lax.ppermute(values, axes, list(enumerate(FIRST_STEP)))
+    second = lax.ppermute(values, axes, list(enumerate(SECOND_STEP)))
     other = lax.ppermute(first, "sub", [(0, 1), (1, 0)])
+    places = range(len(FIRST_STEP))
     sources = [
-        [d for d, _ in places],
-        [FIRST_STEP[c].index(d) for d, c in places],
-        [FIRST_STEP[1 - c].index(d) for d, c in places],
-        [SECOND_STEP.index(d) for d, _ in places],
+        [i // 4 for i in places],
+        [FIRST_STEP.index(i) // 4 for i in places],
+        [FIRST_STEP.index(i ^ 1) // 4 for i in places],
+        [SECOND_STEP.index(i) // 4 for i in places],
     ]
     return [values, first, other, second], sources
 
@@ -347,7 +345,7 @@
     ) = refs
     rows = out_ref.shape[0]
     cand = chosen.shape[0] - rows
-    place(pieces, sources, maxima, ("docs", "sub"))
+    place(pieces, sources, maxima, ("docs", "cent", "sub"))
 
     width = maxima.shape[1]
     own = pltpu.roll(maxima[...], lax.rem(width - lax.axis_index("docs") * QT, width), 1)

time: 20.3 us -> 19.9 us (0.980)
  waiting for transfers between devices: 5.39 us -> 4.45 us
  starting transfers between devices: 7.94 us -> 8.51 us
    ppermute x2, waiting for transfers between devices: 1.7 us -> 0.76 us  [the longest x1 0.62 us: gather_docs(): first = lax.ppermute(values, axes, list(enumerate(FIRST_STEP)))]
    ppermute x1, starting transfers between devices: 0.01 us -> 0.56 us  [gather_docs(): other = lax.ppermute(first, 'sub', [(0, 1), (1, 0)])]
  transfers between devices with their start and end apart: 8 -> 8, of which waited for: 5 -> 5; matrix products, arithmetic and copies ran while one was open for 0% -> 0% of each run, Pallas kernels for 19% -> 20%
where the time goes in v6:
time: 19.9 us; the launch traced here: 19.8 us
  starting transfers between devices  8.51 us (43%)
  Pallas kernels  6.66 us (33%)
  waiting for transfers between devices  4.45 us (22%)
    pallas_call x1, Pallas kernels, prepare(): pl.pallas_call(functools.partial(prepare_kernel, len(kept)), out_shape=[s...  3.24 us
    ppermute x3, starting transfers between devices, gather_queries(): pieces.append(lax.ppermute(queries, MEMBERS, list(enumerate(step))))  3.16 us
    pallas_call x1, Pallas kernels, rerank(): pl.pallas_call(functools.partial(rerank_kernel, sources), out_shape=jax.S...  2.13 us
    ppermute x1, waiting for transfers between devices, best_of_members(): lax.ppermute(values, MEMBERS, [(i, i ^ 3) for i in range(4)])  1.95 us
    ppermute x1, starting transfers between devices, gather_docs(): second = lax.ppermute(values, axes, list(enumerate(SECOND_STEP)))  1.86 us
    ppermute x1, starting transfers between devices, gather_docs(): first = lax.ppermute(values, axes, list(enumerate(FIRST_STEP)))  1.58 us
    ppermute x1, starting transfers between devices, best_of_members(): lax.ppermute(values, MEMBERS, [(i, i ^ 3) for i in range(4)])  1.28 us
    ppermute x1, waiting for transfers between devices, best_of_members(): values = jnp.maximum(values, lax.ppermute(values, 'sub', [(0, 1), (1, 0)]))  1.17 us
  transfers between devices with their start and end apart: 8, of which 5 were waited for; matrix products, arithmetic and copies ran while one was open for 0% of the time, Pallas kernels for 20%

profile of v6, /device:TPU:0, one launch (start us, length us, event | category | flops | bytes accessed | tf_op | source)
XLA Modules:
  0.0 19.8 jit_solution(17542745341500596122)
XLA Ops:
  0.0 0.0 copy-start.5
  0.0 0.0 copy-start.2
  0.0 0.0 copy-start.4
  0.0 0.0 copy-start.1
  0.0 0.5 %collective-permute-start.1 = (f32[32,128]{1,0:T(8,128)}, f32[32,128]{1,0:T(8,128)S(1)}, u32[]{:S(2)}, u32[]{:S(2)}) collective-permute-start(f32[32,128]{1,0:T(8,128)} %refs_0_.1), channel_id=1, source_target_pairs={{0,1},{1,0},{2,3},{3,2},{4,5},{5,4},{6,7},{7,6},{8,9},{9,8},{10,11... | collective-permute-start | bytes 49160 | tf_op jit(solution)/shard_map/ppermute | solution.py:37
  0.5 2.6 %collective-permute-start = (f32[32,128]{1,0:T(8,128)}, f32[32,128]{1,0:T(8,128)S(1)}, u32[]{:S(2)}, u32[]{:S(2)}) collective-permute-start(f32[32,128]{1,0:T(8,128)} %refs_0_.1), channel_id=1, source_target_pairs={{0,2},{1,3},{2,1},{3,0},{4,6},{5,7},{6,5},{7,4},{8,10},{9,11},{10,... | collective-permute-start | bytes 49160 | tf_op jit(solution)/shard_map/ppermute | solution.py:37
  3.1 0.1 collective-permute-start.2
  3.2 0.0 copy-done.5
  3.2 0.0 copy-done.2
  3.2 0.0 copy-done.4
  3.2 0.0 copy-done.1
  3.2 0.0 copy-start
  3.2 3.2 %prepare.1 = (bf16[2048,256]{1,0:T(8,128)(2,1)S(1)}, s32[32,128]{1,0:T(8,128)S(1)}, f32[1,256]{1,0:T(1,128)S(1)}, bf16[256,256]{1,0:T(8,128)(2,1)S(1)}, bf16[256...) custom-call(s32[1,4096]{1,0:T(1,128)S(1)} %copy-done.4, ...), custom_call_target="tpu_custom_call" | custom-call | flops 4000000000 | bytes 4194304 | tf_op jit(solution)/shard_map/prepare/pallas_call | solution.py:204
  6.5 0.0 collective-permute-done.1.refs_2_
  6.5 0.0 collective-permute-done.refs_1_
  6.5 0.5 %collective-permute-done.2.refs_3_ = f32[32,128]{1,0:T(8,128)S(1)} collective-permute-done((f32[32,128]{1,0:T(8,128)}, f32[32,128]{1,0:T(8,128)S(1)}, u32[]{:S(2)}, u32[]{:S(2)}) %collective-permute-start.2) | collective-permute-done | bytes 16416 | tf_op jit(solution)/shard_map/ppermute | solution.py:37
  7.0 0.0 copy-done
  7.0 0.6 %local_maxima.1._ = f32[32,128]{1,0:T(8,128)S(1)} custom-call(bf16[2048,256]{1,0:T(8,128)(2,1)S(1)} %get-tuple-element.17.left, s32[32,128]{1,0:T(8,128)S(1)} %get-tuple-element.18.live, bf16[128,128]{1,0:T(8,128)(2,1)S(1)} %early.1.spread, f32[32,128]{1,0:T(8,128)S(1)} %copy-done, f32[32,128]{1,0:T(8,128)S(1)} %collective-permute-done.refs_1_, ...), custom_call_target="tpu_custom_call" | custom-call | tf_op jit(solution)/shard_map/local_maxima/pallas_call | solution.py:311
  7.7 0.1 collective-permute-start.3
  7.8 1.2 %collective-permute-done.3 = f32[32,128]{1,0:T(8,128)S(1)} collective-permute-done((f32[32,128]{1,0:T(8,128)S(1)}, f32[32,128]{1,0:T(8,128)S(1)}, u32[]{:S(2)}, u32[]{:S(2)}) %collective-permute-start.3) | collective-permute-done | bytes 16416 | tf_op jit(solution)/shard_map/ppermute | solution.py:44
  8.9 1.3 %collective-permute-start.4 = (f32[32,128]{1,0:T(8,128)S(1)}, f32[32,128]{1,0:T(8,128)S(1)}, u32[]{:S(2)}, u32[]{:S(2)}) collective-permute-start(f32[32,128]{1,0:T(8,128)S(1)} %max.6), channel_id=1, source_target_pairs={{0,3},{1,2},{2,1},{3,0},{4,7},{5,6},{6,5},{7,4},{8,11},{9,10},{10,... | collective-permute-start | bytes 49160 | tf_op jit(solution)/shard_map/ppermute | solution.py:45
  10.2 2.0 %collective-permute-done.4 = f32[32,128]{1,0:T(8,128)S(1)} collective-permute-done((f32[32,128]{1,0:T(8,128)S(1)}, f32[32,128]{1,0:T(8,128)S(1)}, u32[]{:S(2)}, u32[]{:S(2)}) %collective-permute-start.4) | collective-permute-done | bytes 16416 | tf_op jit(solution)/shard_map/ppermute | solution.py:45
  12.2 1.6 %collective-permute-start.5 = (f32[32,128]{1,0:T(8,128)S(1)}, f32[32,128]{1,0:T(8,128)S(1)}, u32[]{:S(2)}, u32[]{:S(2)}) collective-permute-start(f32[32,128]{1,0:T(8,128)S(1)} %max.7.refs_0_), channel_id=1, source_target_pairs={{0,4},{1,9},{2,11},{3,6},{4,8},{5,13},{6,10},{7,15},{8,12},{9,0},{... | collective-permute-start | bytes 49160 | tf_op jit(solution)/shard_map/ppermute | solution.py:52
  13.8 1.9 %collective-permute-start.7 = (f32[32,128]{1,0:T(8,128)S(1)}, f32[32,128]{1,0:T(8,128)S(1)}, u32[]{:S(2)}, u32[]{:S(2)}) collective-permute-start(f32[32,128]{1,0:T(8,128)S(1)} %max.7.refs_0_), channel_id=1, source_target_pairs={{0,13},{1,12},{2,15},{3,14},{4,0},{5,1},{6,3},{7,2},{8,5},{9,4},{1... | collective-permute-start | bytes 49160 | tf_op jit(solution)/shard_map/ppermute | solution.py:53
  15.6 0.6 %collective-permute-done.5.refs_1_ = f32[32,128]{1,0:T(8,128)S(1)} collective-permute-done((f32[32,128]{1,0:T(8,128)S(1)}, f32[32,128]{1,0:T(8,128)S(1)}, u32[]{:S(2)}, u32[]{:S(2)}) %collective-permute-start.5) | collective-permute-done | bytes 16416 | tf_op jit(solution)/shard_map/ppermute | solution.py:52
  16.2 0.6 %collective-permute-start.6 = (f32[32,128]{1,0:T(8,128)S(1)}, f32[32,128]{1,0:T(8,128)S(1)}, u32[]{:S(2)}, u32[]{:S(2)}) collective-permute-start(f32[32,128]{1,0:T(8,128)S(1)} %collective-permute-done.5.refs_1_), channel_id=1, source_target_pairs={{0,1},{1,0},{2,3},{3,2},{4,5},{5,4},{6,7},{7,6},{8,9},{9,8},{10,11... | collective-permute-start | bytes 49160 | tf_op jit(solution)/shard_map/ppermute | solution.py:54
  16.8 0.0 copy-done.3
  16.8 0.0 copy-done.6
  16.8 0.6 %make_tables.1 = (bf16[80,128]{1,0:T(8,128)(2,1)S(1)}, bf16[192,256]{1,0:T(8,128)(2,1)S(1)}) custom-call(s32[1,64]{1,0:T(1,128)S(1)} %copy-done.6, f32[32,256]{1,0:T(8,128)S(1)} %copy-done.3, f32[32,128]{1,0:T(8,128)S(1)} %local_maxima.1._), custom_call_target="tpu_custom_call" | custom-call | flops 500000000 | tf_op jit(solution)/shard_map/make_tables/pallas_call | solution.py:255
  17.5 0.1 collective-permute-done.7.refs_3_
  17.6 0.0 collective-permute-done.6.refs_2_
  17.6 2.1 %rerank.1 = f32[16,256]{1,0:T(8,128)} custom-call(f32[32,128]{1,0:T(8,128)S(1)} %max.7.refs_0_, f32[32,128]{1,0:T(8,128)S(1)} %collective-permute-done.5.refs_1_, f32[32,128]{1,0:T(8,128)S(1)} %collective-permute-done.6.refs_2_, f32[32,128]{1,0:T(8,128)S(1)} %collective-permute-done.7.refs_3_, bf16[80,128]{1,0:T(8,128)(2,1)S(1)} %get-tuple-element.19.refs_4_, ...), custom_call_target="tpu_custom_call" | custom-call | tf_op jit(solution)/shard_map/rerank/pallas_call | solution.py:385
  (5 shorter events, 0.0 us)
Async XLA Ops:
  0.0 3.2 %copy-start.5 = (f32[16,128]{1,0:T(8,128)S(1)}, f32[16,128]{1,0:T(8,128)}, u32[]{:S(2)}) copy-start(f32[16,128]{1,0:T(8,128)} %buckets.1) | copy-start | bytes 24580
  0.0 3.2 %copy-start.2 = (bf16[4096,128]{1,0:T(8,128)(2,1)S(1)}, bf16[4096,128]{1,0:T(8,128)(2,1)}, u32[]{:S(2)}) copy-start(bf16[4096,128]{1,0:T(8,128)(2,1)} %centroids.1) | copy-start | bytes 3145732
  0.0 3.2 %copy-start.4 = (s32[1,4096]{1,0:T(1,128)S(1)}, s32[1,4096]{1,0:T(1,128)}, u32[]{:S(2)}) copy-start(s32[1,4096]{1,0:T(1,128)} %ids_vmem.1) | copy-start | bytes 49156
  0.0 3.2 %copy-start.1 = (s32[1,32,8192]{2,1,0:T(8,128)S(1)}, s32[1,32,8192]{2,1,0:T(8,128)}, u32[]{:S(2)}) copy-start(s32[1,32,8192]{2,1,0:T(8,128)} %param.17) | copy-start | bytes 3145732
  0.0 6.5 %collective-permute-start.1 = (f32[32,128]{1,0:T(8,128)}, f32[32,128]{1,0:T(8,128)S(1)}, u32[]{:S(2)}, u32[]{:S(2)}) collective-permute-start(f32[32,128]{1,0:T(8,128)} %refs_0_.1), channel_id=1, source_target_pairs={{0,1},{1,0},{2,3},{3,2},{4,5},{5,4},{6,7},{7,6},{8,9},{9,8},{10,11... | collective-permute-start | bytes 49160 | tf_op jit(solution)/shard_map/ppermute | solution.py:37
  0.5 6.0 %collective-permute-start = (f32[32,128]{1,0:T(8,128)}, f32[32,128]{1,0:T(8,128)S(1)}, u32[]{:S(2)}, u32[]{:S(2)}) collective-permute-start(f32[32,128]{1,0:T(8,128)} %refs_0_.1), channel_id=1, source_target_pairs={{0,2},{1,3},{2,1},{3,0},{4,6},{5,7},{6,5},{7,4},{8,10},{9,11},{10,... | collective-permute-start | bytes 49160 | tf_op jit(solution)/shard_map/ppermute | solution.py:37
  3.1 3.9 %collective-permute-start.2 = (f32[32,128]{1,0:T(8,128)}, f32[32,128]{1,0:T(8,128)S(1)}, u32[]{:S(2)}, u32[]{:S(2)}) collective-permute-start(f32[32,128]{1,0:T(8,128)} %refs_0_.1), channel_id=1, source_target_pairs={{0,3},{1,2},{2,0},{3,1},{4,7},{5,6},{6,4},{7,5},{8,11},{9,10},{10,... | collective-permute-start | bytes 49160 | tf_op jit(solution)/shard_map/ppermute | solution.py:37
  3.2 3.8 %copy-start = (f32[32,128]{1,0:T(8,128)S(1)}, f32[32,128]{1,0:T(8,128)}, u32[]{:S(2)}) copy-start(f32[32,128]{1,0:T(8,128)} %refs_0_.1) | copy-start | bytes 49156
  7.7 1.2 %collective-permute-start.3 = (f32[32,128]{1,0:T(8,128)S(1)}, f32[32,128]{1,0:T(8,128)S(1)}, u32[]{:S(2)}, u32[]{:S(2)}) collective-permute-start(f32[32,128]{1,0:T(8,128)S(1)} %local_maxima.1._), channel_id=1, source_target_pairs={{0,1},{1,0},{2,3},{3,2},{4,5},{5,4},{6,7},{7,6},{8,9},{9,8},{10,11... | collective-permute-start | bytes 49160 | tf_op jit(solution)/shard_map/ppermute | solution.py:44
  8.9 7.9 %copy-start.3 = (f32[32,256]{1,0:T(8,128)S(1)}, f32[32,256]{1,0:T(8,128)}, u32[]{:S(2)}) copy-start(f32[32,256]{1,0:T(8,128)} %proj.1) | copy-start | bytes 98308
  8.9 7.9 %copy-start.6 = (s32[1,64]{1,0:T(1,128)S(1)}, s32[1,64]{1,0:T(1,128)}, u32[]{:S(2)}) copy-start(s32[1,64]{1,0:T(1,128)} %candidates_vmem.1) | copy-start | bytes 772
  8.9 3.2 %collective-permute-start.4 = (f32[32,128]{1,0:T(8,128)S(1)}, f32[32,128]{1,0:T(8,128)S(1)}, u32[]{:S(2)}, u32[]{:S(2)}) collective-permute-start(f32[32,128]{1,0:T(8,128)S(1)} %max.6), channel_id=1, source_target_pairs={{0,3},{1,2},{2,1},{3,0},{4,7},{5,6},{6,5},{7,4},{8,11},{9,10},{10,... | collective-permute-start | bytes 49160 | tf_op jit(solution)/shard_map/ppermute | solution.py:45
  12.2 4.1 %collective-permute-start.5 = (f32[32,128]{1,0:T(8,128)S(1)}, f32[32,128]{1,0:T(8,128)S(1)}, u32[]{:S(2)}, u32[]{:S(2)}) collective-permute-start(f32[32,128]{1,0:T(8,128)S(1)} %max.7.refs_0_), channel_id=1, source_target_pairs={{0,4},{1,9},{2,11},{3,6},{4,8},{5,13},{6,10},{7,15},{8,12},{9,0},{... | collective-permute-start | bytes 49160 | tf_op jit(solution)/shard_map/ppermute | solution.py:52
  13.8 3.8 %collective-permute-start.7 = (f32[32,128]{1,0:T(8,128)S(1)}, f32[32,128]{1,0:T(8,128)S(1)}, u32[]{:S(2)}, u32[]{:S(2)}) collective-permute-start(f32[32,128]{1,0:T(8,128)S(1)} %max.7.refs_0_), channel_id=1, source_target_pairs={{0,13},{1,12},{2,15},{3,14},{4,0},{5,1},{6,3},{7,2},{8,5},{9,4},{1... | collective-permute-start | bytes 49160 | tf_op jit(solution)/shard_map/ppermute | solution.py:53
  16.2 1.4 %collective-permute-start.6 = (f32[32,128]{1,0:T(8,128)S(1)}, f32[32,128]{1,0:T(8,128)S(1)}, u32[]{:S(2)}, u32[]{:S(2)}) collective-permute-start(f32[32,128]{1,0:T(8,128)S(1)} %collective-permute-done.5.refs_1_), channel_id=1, source_target_pairs={{0,1},{1,0},{2,3},{3,2},{4,5},{5,4},{6,7},{7,6},{8,9},{9,8},{10,11... | collective-permute-start | bytes 49160 | tf_op jit(solution)/shard_map/ppermute | solution.py:54

commit v7 on v6

--- a/solution.py
+++ b/solution.py
@@ -14,7 +14,7 @@
 HEAD = 64
 MEMBERS = ("cent", "sub")
 NOTHING = -1e30
-PART_PAIRS = ((0, 0), (0, 1), (0, 2), (1, 0), (1, 1), (2, 0))
+PARTS = 3
 QUERY_STEPS = ((2, 3, 1, 0), (1, 0, 3, 2), (3, 2, 0, 1))
 FIRST_STEP = (4, 9, 11, 6, 8, 13, 10, 15, 12, 0, 2, 14, 5, 1, 7, 3)
 SECOND_STEP = (13, 12, 15, 14, 0, 1, 3, 2, 5, 4, 6, 7, 10, 8, 11, 9)
@@ -64,7 +64,7 @@
 
 def place(pieces, sources, out_ref, axes):
     if len(pieces) == 1:
-        out_ref[...] = pieces[0][...]
+        out_ref[...] = pieces[0][...].astype(out_ref.dtype)
         return
     me = lax.axis_index(axes)
     for piece, source in zip(pieces, sources):
@@ -73,7 +73,7 @@
         for i in range(1, len(source)):
             place_of = jnp.where(me == i, source[i], place_of)
         start = pl.multiple_of(place_of * rows, rows)
-        out_ref[pl.ds(start, rows), :] = piece[...]
+        out_ref[pl.ds(start, rows), :] = piece[...].astype(out_ref.dtype)
 
 
 def vmem():
@@ -105,7 +105,7 @@
 
 def three_parts(values):
     parts = []
-    for _ in range(3):
+    for _ in range(PARTS):
         part = values.astype(jnp.bfloat16)
         values = values - part.astype(jnp.float32)
         parts.append(part)
@@ -229,8 +229,8 @@
     copy = pltpu.make_async_copy(candidates_vmem, candidates, sem)
     copy.start()
     parts = three_parts(proj[...])
-    for i, k in enumerate(PART_PAIRS):
-        proj_parts[i * QT : (i + 1) * QT, :] = parts[k[1]]
+    for i, part in enumerate(parts):
+        proj_parts[i * QT : (i + 1) * QT, :] = part
 
     copy.wait()
     docs_all = chosen.shape[1]
@@ -256,7 +256,7 @@
         tables_kernel,
         out_shape=[
             shape((candidates.shape[1] + rows, docs_all), jnp.bfloat16),
-            shape((len(PART_PAIRS) * QT, H), jnp.bfloat16),
+            shape((PARTS * QT, H), jnp.bfloat16),
         ],
         in_specs=[vmem(), vmem(), pl.BlockSpec(memory_space=pl.ANY)],
         out_specs=[vmem()] * 2,
@@ -300,9 +300,9 @@
 
     best = jnp.full((docs, query_rows), NOTHING, jnp.float32)
     if block == pairs:
-        out_ref[...] = score(0, best)
+        out_ref[...] = score(0, best).astype(out_ref.dtype)
     else:
-        out_ref[...] = lax.fori_loop(0, pairs // block, score, best)
+        out_ref[...] = lax.fori_loop(0, pairs // block, score, best).astype(out_ref.dtype)
 
 
 def local_maxima(left, live, spread, pieces, sources):
@@ -310,7 +310,7 @@
     query_rows = sum(piece.shape[0] for piece in pieces)
     return pl.pallas_call(
         functools.partial(score_kernel, sources, docs),
-        out_shape=jax.ShapeDtypeStruct((docs, query_rows), jnp.float32),
+        out_shape=jax.ShapeDtypeStruct((docs, query_rows), jnp.bfloat16),
         in_specs=[vmem()] * (3 + len(pieces)),
         out_specs=vmem(),
         scratch_shapes=[
@@ -349,8 +349,7 @@
 
     width = maxima.shape[1]
     own = pltpu.roll(maxima[...], lax.rem(width - lax.axis_index("docs") * QT, width), 1)
-    parts = three_parts(own[:, :QT])
-    stacked = jnp.concatenate([parts[k[0]] for k in PART_PAIRS], axis=1)
+    stacked = jnp.concatenate([own[:, :QT].astype(jnp.bfloat16)] * PARTS, axis=1)
     features = product(chosen[...], stacked).astype(jnp.bfloat16)
     all_hidden = product(features, proj_parts[...])
     hidden_zero = all_hidden[cand:]

time: 19.9 us -> 19.7 us (0.990)
  transfers between devices with their start and end apart: 8 -> 8, of which waited for: 5 -> 6; matrix products, arithmetic and copies ran while one was open for 0% -> 0% of each run, Pallas kernels for 20% -> 20%
where the time goes in v7:
time: 19.7 us; the launch traced here: 19.5 us
  starting transfers between devices  8.4 us (43%)
  Pallas kernels  6.65 us (34%)
  waiting for transfers between devices  4.33 us (22%)
    pallas_call x1, Pallas kernels, prepare(): pl.pallas_call(functools.partial(prepare_kernel, len(kept)), out_shape=[s...  3.25 us
    ppermute x3, starting transfers between devices, gather_queries(): pieces.append(lax.ppermute(queries, MEMBERS, list(enumerate(step))))  3.16 us
    pallas_call x1, Pallas kernels, rerank(): pl.pallas_call(functools.partial(rerank_kernel, sources), out_shape=jax.S...  2.11 us
    ppermute x1, waiting for transfers between devices, best_of_members(): lax.ppermute(values, MEMBERS, [(i, i ^ 3) for i in range(4)])  1.91 us
    ppermute x1, starting transfers between devices, gather_docs(): second = lax.ppermute(values, axes, list(enumerate(SECOND_STEP)))  1.83 us
    ppermute x1, starting transfers between devices, gather_docs(): first = lax.ppermute(values, axes, list(enumerate(FIRST_STEP)))  1.58 us
    ppermute x1, starting transfers between devices, best_of_members(): lax.ppermute(values, MEMBERS, [(i, i ^ 3) for i in range(4)])  1.22 us
    ppermute x1, waiting for transfers between devices, best_of_members(): values = jnp.maximum(values, lax.ppermute(values, 'sub', [(0, 1), (1, 0)]))  1.16 us
  transfers between devices with their start and end apart: 8, of which 6 were waited for; matrix products, arithmetic and copies ran while one was open for 0% of the time, Pallas kernels for 20%

profile of v7, /device:TPU:0, one launch (start us, length us, event | category | flops | bytes accessed | tf_op | source)
XLA Modules:
  0.0 19.5 jit_solution(11867603996534115784)
XLA Ops:
  0.0 0.0 copy-start.5
  0.0 0.0 copy-start.2
  0.0 0.0 copy-start.4
  0.0 0.5 %collective-permute-start.1 = (f32[32,128]{1,0:T(8,128)}, f32[32,128]{1,0:T(8,128)S(1)}, u32[]{:S(2)}, u32[]{:S(2)}) collective-permute-start(f32[32,128]{1,0:T(8,128)} %refs_0_.1), channel_id=1, source_target_pairs={{0,1},{1,0},{2,3},{3,2},{4,5},{5,4},{6,7},{7,6},{8,9},{9,8},{10,11... | collective-permute-start | bytes 49160 | tf_op jit(solution)/shard_map/ppermute | solution.py:37
  0.5 2.6 %collective-permute-start = (f32[32,128]{1,0:T(8,128)}, f32[32,128]{1,0:T(8,128)S(1)}, u32[]{:S(2)}, u32[]{:S(2)}) collective-permute-start(f32[32,128]{1,0:T(8,128)} %refs_0_.1), channel_id=1, source_target_pairs={{0,2},{1,3},{2,1},{3,0},{4,6},{5,7},{6,5},{7,4},{8,10},{9,11},{10,... | collective-permute-start | bytes 49160 | tf_op jit(solution)/shard_map/ppermute | solution.py:37
  3.1 0.1 collective-permute-start.2
  3.2 0.0 copy-done.5
  3.2 0.0 copy-done.2
  3.2 0.0 copy-done.4
  3.2 0.0 copy-done.1
  3.2 0.0 copy-start
  3.2 3.3 %prepare.1 = (bf16[2048,256]{1,0:T(8,128)(2,1)S(1)}, s32[32,128]{1,0:T(8,128)S(1)}, f32[1,256]{1,0:T(1,128)S(1)}, bf16[256,256]{1,0:T(8,128)(2,1)S(1)}, bf16[256...) custom-call(s32[1,4096]{1,0:T(1,128)S(1)} %copy-done.4, ...), custom_call_target="tpu_custom_call" | custom-call | flops 4000000000 | bytes 4194304 | tf_op jit(solution)/shard_map/prepare/pallas_call | solution.py:204
  6.5 0.0 collective-permute-done.1.refs_2_
  6.5 0.0 collective-permute-done.refs_1_
  6.5 0.5 %collective-permute-done.2.refs_3_ = f32[32,128]{1,0:T(8,128)S(1)} collective-permute-done((f32[32,128]{1,0:T(8,128)}, f32[32,128]{1,0:T(8,128)S(1)}, u32[]{:S(2)}, u32[]{:S(2)}) %collective-permute-start.2) | collective-permute-done | bytes 16416 | tf_op jit(solution)/shard_map/ppermute | solution.py:37
  7.0 0.0 copy-done
  7.0 0.6 %local_maxima.1._ = bf16[32,128]{1,0:T(8,128)(2,1)S(1)} custom-call(bf16[2048,256]{1,0:T(8,128)(2,1)S(1)} %get-tuple-element.17.left, s32[32,128]{1,0:T(8,128)S(1)} %get-tuple-element.18.live, bf16[128,128]{1,0:T(8,128)(2,1)S(1)} %early.1.spread, f32[32,128]{1,0:T(8,128)S(1)} %copy-done, f32[32,128]{1,0:T(8,128)S(1)} %collective-permute-done.refs_1_, ...), custom_call_target="tpu_custom_call" | custom-call | tf_op jit(solution)/shard_map/local_maxima/pallas_call | solution.py:311
  7.7 0.0 copy-start.3
  7.7 0.1 collective-permute-start.3
  7.8 1.2 %collective-permute-done.3 = bf16[32,128]{1,0:T(8,128)(2,1)S(1)} collective-permute-done((bf16[32,128]{1,0:T(8,128)(2,1)S(1)}, bf16[32,128]{1,0:T(8,128)(2,1)S(1)}, u32[]{:S(2)}, u32[]{:S(2)}) %collective-permute-start.3) | collective-permute-done | bytes 8224 | tf_op jit(solution)/shard_map/ppermute | solution.py:44
  8.9 1.2 %collective-permute-start.4 = (bf16[32,128]{1,0:T(8,128)(2,1)S(1)}, bf16[32,128]{1,0:T(8,128)(2,1)S(1)}, u32[]{:S(2)}, u32[]{:S(2)}) collective-permute-start(bf16[32,128]{1,0:T(8,128)(2,1)S(1)} %max.6), channel_id=1, source_target_pairs={{0,3},{1,2},{2,1},{3,0},{4,7},{5,6},{6,5},{7,4},{8,11},{9,10},{10,... | collective-permute-start | bytes 24584 | tf_op jit(solution)/shard_map/ppermute | solution.py:45
  10.2 1.9 %collective-permute-done.4 = bf16[32,128]{1,0:T(8,128)(2,1)S(1)} collective-permute-done((bf16[32,128]{1,0:T(8,128)(2,1)S(1)}, bf16[32,128]{1,0:T(8,128)(2,1)S(1)}, u32[]{:S(2)}, u32[]{:S(2)}) %collective-permute-start.4) | collective-permute-done | bytes 8224 | tf_op jit(solution)/shard_map/ppermute | solution.py:45
  12.1 1.6 %collective-permute-start.5 = (bf16[32,128]{1,0:T(8,128)(2,1)S(1)}, bf16[32,128]{1,0:T(8,128)(2,1)S(1)}, u32[]{:S(2)}, u32[]{:S(2)}) collective-permute-start(bf16[32,128]{1,0:T(8,128)(2,1)S(1)} %max.7.refs_0_), channel_id=1, source_target_pairs={{0,4},{1,9},{2,11},{3,6},{4,8},{5,13},{6,10},{7,15},{8,12},{9,0},{... | collective-permute-start | bytes 24584 | tf_op jit(solution)/shard_map/ppermute | solution.py:52
  13.7 1.8 %collective-permute-start.7 = (bf16[32,128]{1,0:T(8,128)(2,1)S(1)}, bf16[32,128]{1,0:T(8,128)(2,1)S(1)}, u32[]{:S(2)}, u32[]{:S(2)}) collective-permute-start(bf16[32,128]{1,0:T(8,128)(2,1)S(1)} %max.7.refs_0_), channel_id=1, source_target_pairs={{0,13},{1,12},{2,15},{3,14},{4,0},{5,1},{6,3},{7,2},{8,5},{9,4},{1... | collective-permute-start | bytes 24584 | tf_op jit(solution)/shard_map/ppermute | solution.py:53
  15.5 0.6 %collective-permute-done.5.refs_1_ = bf16[32,128]{1,0:T(8,128)(2,1)S(1)} collective-permute-done((bf16[32,128]{1,0:T(8,128)(2,1)S(1)}, bf16[32,128]{1,0:T(8,128)(2,1)S(1)}, u32[]{:S(2)}, u32[]{:S(2)}) %collective-permute-start.5) | collective-permute-done | bytes 8224 | tf_op jit(solution)/shard_map/ppermute | solution.py:52
  16.1 0.5 %collective-permute-start.6 = (bf16[32,128]{1,0:T(8,128)(2,1)S(1)}, bf16[32,128]{1,0:T(8,128)(2,1)S(1)}, u32[]{:S(2)}, u32[]{:S(2)}) collective-permute-start(bf16[32,128]{1,0:T(8,128)(2,1)S(1)} %collective-permute-done.5.refs_1_), channel_id=1, source_target_pairs={{0,1},{1,0},{2,3},{3,2},{4,5},{5,4},{6,7},{7,6},{8,9},{9,8},{10,11... | collective-permute-start | bytes 24584 | tf_op jit(solution)/shard_map/ppermute | solution.py:54
  16.6 0.0 copy-done.3
  16.6 0.0 copy-done.6
  16.6 0.6 %make_tables.1 = (bf16[80,128]{1,0:T(8,128)(2,1)S(1)}, bf16[96,256]{1,0:T(8,128)(2,1)S(1)}) custom-call(s32[1,64]{1,0:T(1,128)S(1)} %copy-done.6, f32[32,256]{1,0:T(8,128)S(1)} %copy-done.3, bf16[32,128]{1,0:T(8,128)(2,1)S(1)} %local_maxima.1._), custom_call_target="tpu_custom_call" | custom-call | flops 500000000 | tf_op jit(solution)/shard_map/make_tables/pallas_call | solution.py:255
  17.3 0.1 collective-permute-done.7.refs_3_
  17.3 0.1 collective-permute-done.6.refs_2_
  17.4 2.1 %rerank.1 = f32[16,256]{1,0:T(8,128)} custom-call(bf16[32,128]{1,0:T(8,128)(2,1)S(1)} %max.7.refs_0_, bf16[32,128]{1,0:T(8,128)(2,1)S(1)} %collective-permute-done.5.refs_1_, bf16[32,128]{1,0:T(8,128)(2,1)S(1)} %collective-permute-done.6.refs_2_, bf16[32,128]{1,0:T(8,128)(2,1)S(1)} %collective-permute-done.7.refs_3_, ...), custom_call_target="tpu_custom_call" | custom-call | tf_op jit(solution)/shard_map/rerank/pallas_call | solution.py:384
  (5 shorter events, 0.0 us)
Async XLA Ops:
  0.0 3.2 %copy-start.5 = (f32[16,128]{1,0:T(8,128)S(1)}, f32[16,128]{1,0:T(8,128)}, u32[]{:S(2)}) copy-start(f32[16,128]{1,0:T(8,128)} %buckets.1) | copy-start | bytes 24580
  0.0 3.2 %copy-start.2 = (bf16[4096,128]{1,0:T(8,128)(2,1)S(1)}, bf16[4096,128]{1,0:T(8,128)(2,1)}, u32[]{:S(2)}) copy-start(bf16[4096,128]{1,0:T(8,128)(2,1)} %centroids.1) | copy-start | bytes 3145732
  0.0 3.2 %copy-start.4 = (s32[1,4096]{1,0:T(1,128)S(1)}, s32[1,4096]{1,0:T(1,128)}, u32[]{:S(2)}) copy-start(s32[1,4096]{1,0:T(1,128)} %ids_vmem.1) | copy-start | bytes 49156
  0.0 3.2 %copy-start.1 = (s32[1,32,8192]{2,1,0:T(8,128)S(1)}, s32[1,32,8192]{2,1,0:T(8,128)}, u32[]{:S(2)}) copy-start(s32[1,32,8192]{2,1,0:T(8,128)} %param.17) | copy-start | bytes 3145732
  0.0 6.5 %collective-permute-start.1 = (f32[32,128]{1,0:T(8,128)}, f32[32,128]{1,0:T(8,128)S(1)}, u32[]{:S(2)}, u32[]{:S(2)}) collective-permute-start(f32[32,128]{1,0:T(8,128)} %refs_0_.1), channel_id=1, source_target_pairs={{0,1},{1,0},{2,3},{3,2},{4,5},{5,4},{6,7},{7,6},{8,9},{9,8},{10,11... | collective-permute-start | bytes 49160 | tf_op jit(solution)/shard_map/ppermute | solution.py:37
  0.5 6.0 %collective-permute-start = (f32[32,128]{1,0:T(8,128)}, f32[32,128]{1,0:T(8,128)S(1)}, u32[]{:S(2)}, u32[]{:S(2)}) collective-permute-start(f32[32,128]{1,0:T(8,128)} %refs_0_.1), channel_id=1, source_target_pairs={{0,2},{1,3},{2,1},{3,0},{4,6},{5,7},{6,5},{7,4},{8,10},{9,11},{10,... | collective-permute-start | bytes 49160 | tf_op jit(solution)/shard_map/ppermute | solution.py:37
  3.1 3.9 %collective-permute-start.2 = (f32[32,128]{1,0:T(8,128)}, f32[32,128]{1,0:T(8,128)S(1)}, u32[]{:S(2)}, u32[]{:S(2)}) collective-permute-start(f32[32,128]{1,0:T(8,128)} %refs_0_.1), channel_id=1, source_target_pairs={{0,3},{1,2},{2,0},{3,1},{4,7},{5,6},{6,4},{7,5},{8,11},{9,10},{10,... | collective-permute-start | bytes 49160 | tf_op jit(solution)/shard_map/ppermute | solution.py:37
  3.2 3.8 %copy-start = (f32[32,128]{1,0:T(8,128)S(1)}, f32[32,128]{1,0:T(8,128)}, u32[]{:S(2)}) copy-start(f32[32,128]{1,0:T(8,128)} %refs_0_.1) | copy-start | bytes 49156
  7.7 8.9 %copy-start.3 = (f32[32,256]{1,0:T(8,128)S(1)}, f32[32,256]{1,0:T(8,128)}, u32[]{:S(2)}) copy-start(f32[32,256]{1,0:T(8,128)} %proj.1) | copy-start | bytes 98308
  7.7 1.2 %collective-permute-start.3 = (bf16[32,128]{1,0:T(8,128)(2,1)S(1)}, bf16[32,128]{1,0:T(8,128)(2,1)S(1)}, u32[]{:S(2)}, u32[]{:S(2)}) collective-permute-start(bf16[32,128]{1,0:T(8,128)(2,1)S(1)} %local_maxima.1._), channel_id=1, source_target_pairs={{0,1},{1,0},{2,3},{3,2},{4,5},{5,4},{6,7},{7,6},{8,9},{9,8},{10,11... | collective-permute-start | bytes 24584 | tf_op jit(solution)/shard_map/ppermute | solution.py:44
  8.9 7.7 %copy-start.6 = (s32[1,64]{1,0:T(1,128)S(1)}, s32[1,64]{1,0:T(1,128)}, u32[]{:S(2)}) copy-start(s32[1,64]{1,0:T(1,128)} %candidates_vmem.1) | copy-start | bytes 772
  8.9 3.1 %collective-permute-start.4 = (bf16[32,128]{1,0:T(8,128)(2,1)S(1)}, bf16[32,128]{1,0:T(8,128)(2,1)S(1)}, u32[]{:S(2)}, u32[]{:S(2)}) collective-permute-start(bf16[32,128]{1,0:T(8,128)(2,1)S(1)} %max.6), channel_id=1, source_target_pairs={{0,3},{1,2},{2,1},{3,0},{4,7},{5,6},{6,5},{7,4},{8,11},{9,10},{10,... | collective-permute-start | bytes 24584 | tf_op jit(solution)/shard_map/ppermute | solution.py:45
  12.1 4.0 %collective-permute-start.5 = (bf16[32,128]{1,0:T(8,128)(2,1)S(1)}, bf16[32,128]{1,0:T(8,128)(2,1)S(1)}, u32[]{:S(2)}, u32[]{:S(2)}) collective-permute-start(bf16[32,128]{1,0:T(8,128)(2,1)S(1)} %max.7.refs_0_), channel_id=1, source_target_pairs={{0,4},{1,9},{2,11},{3,6},{4,8},{5,13},{6,10},{7,15},{8,12},{9,0},{... | collective-permute-start | bytes 24584 | tf_op jit(solution)/shard_map/ppermute | solution.py:52
  13.7 3.7 %collective-permute-start.7 = (bf16[32,128]{1,0:T(8,128)(2,1)S(1)}, bf16[32,128]{1,0:T(8,128)(2,1)S(1)}, u32[]{:S(2)}, u32[]{:S(2)}) collective-permute-start(bf16[32,128]{1,0:T(8,128)(2,1)S(1)} %max.7.refs_0_), channel_id=1, source_target_pairs={{0,13},{1,12},{2,15},{3,14},{4,0},{5,1},{6,3},{7,2},{8,5},{9,4},{1... | collective-permute-start | bytes 24584 | tf_op jit(solution)/shard_map/ppermute | solution.py:53
  16.1 1.4 %collective-permute-start.6 = (bf16[32,128]{1,0:T(8,128)(2,1)S(1)}, bf16[32,128]{1,0:T(8,128)(2,1)S(1)}, u32[]{:S(2)}, u32[]{:S(2)}) collective-permute-start(bf16[32,128]{1,0:T(8,128)(2,1)S(1)} %collective-permute-done.5.refs_1_), channel_id=1, source_target_pairs={{0,1},{1,0},{2,3},{3,2},{4,5},{5,4},{6,7},{7,6},{8,9},{9,8},{10,11... | collective-permute-start | bytes 24584 | tf_op jit(solution)/shard_map/ppermute | solution.py:54

commit v8 on v7

--- a/solution.py
+++ b/solution.py
@@ -17,7 +17,8 @@
 PARTS = 3
 QUERY_STEPS = ((2, 3, 1, 0), (1, 0, 3, 2), (3, 2, 0, 1))
 FIRST_STEP = (4, 9, 11, 6, 8, 13, 10, 15, 12, 0, 2, 14, 5, 1, 7, 3)
-SECOND_STEP = (13, 12, 15, 14, 0, 1, 3, 2, 5, 4, 6, 7, 10, 8, 11, 9)
+SECOND_STEP = (13, 12, 15, 14, 0, 1, 3, 2, 5, 7, 6, 4, 10, 8, 11, 9)
+NEIGHBOUR_STEP = (3, 2, 1, 0, 6, 7, 5, 4, 11, 10, 9, 8, 15, 14, 12, 13)
 
 
 def compact():
@@ -42,7 +43,8 @@
     if not compact():
         return lax.pmax(values, MEMBERS)
     values = jnp.maximum(values, lax.ppermute(values, "sub", [(0, 1), (1, 0)]))
-    return jnp.maximum(values, lax.ppermute(values, MEMBERS, [(i, i ^ 3) for i in range(4)]))
+    axes = ("docs", "cent", "sub")
+    return jnp.maximum(values, lax.ppermute(values, axes, list(enumerate(NEIGHBOUR_STEP))))
 
 
 def gather_docs(values):

time: 19.7 us -> 19.6 us (level)
  starting transfers between devices: 8.4 us -> 8.16 us
  transfers between devices with their start and end apart: 8 -> 8, of which waited for: 6 -> 5; matrix products, arithmetic and copies ran while one was open for 0% -> 0% of each run, Pallas kernels for 20% -> 20%
where the time goes in v8:
time: 19.6 us; the launch traced here: 19.4 us
  starting transfers between devices  8.16 us (42%)
  Pallas kernels  6.64 us (34%)
  waiting for transfers between devices  4.48 us (23%)
    pallas_call x1, Pallas kernels, prepare(): pl.pallas_call(functools.partial(prepare_kernel, len(kept)), out_shape=[s...  3.24 us
    ppermute x3, starting transfers between devices, gather_queries(): pieces.append(lax.ppermute(queries, MEMBERS, list(enumerate(step))))  3.16 us
    pallas_call x1, Pallas kernels, rerank(): pl.pallas_call(functools.partial(rerank_kernel, sources), out_shape=jax.S...  2.11 us
    ppermute x1, waiting for transfers between devices, best_of_members(): lax.ppermute(values, axes, list(enumerate(NEIGHBOUR_STEP)))  1.91 us
    ppermute x1, starting transfers between devices, gather_docs(): second = lax.ppermute(values, axes, list(enumerate(SECOND_STEP)))  1.69 us
    ppermute x1, starting transfers between devices, gather_docs(): first = lax.ppermute(values, axes, list(enumerate(FIRST_STEP)))  1.58 us
    ppermute x1, starting transfers between devices, best_of_members(): lax.ppermute(values, axes, list(enumerate(NEIGHBOUR_STEP)))  1.2 us
    ppermute x1, waiting for transfers between devices, best_of_members(): values = jnp.maximum(values, lax.ppermute(values, 'sub', [(0, 1), (1, 0)]))  1.16 us
  transfers between devices with their start and end apart: 8, of which 5 were waited for; matrix products, arithmetic and copies ran while one was open for 0% of the time, Pallas kernels for 20%

profile of v8, /device:TPU:0, one launch (start us, length us, event | category | flops | bytes accessed | tf_op | source)
XLA Modules:
  0.0 19.4 jit_solution(3580859345160995255)
XLA Ops:
  0.0 0.0 copy-start.5
  0.0 0.0 copy-start.2
  0.0 0.0 copy-start.4
  0.0 0.5 %collective-permute-start.1 = (f32[32,128]{1,0:T(8,128)}, f32[32,128]{1,0:T(8,128)S(1)}, u32[]{:S(2)}, u32[]{:S(2)}) collective-permute-start(f32[32,128]{1,0:T(8,128)} %refs_0_.1), channel_id=1, source_target_pairs={{0,1},{1,0},{2,3},{3,2},{4,5},{5,4},{6,7},{7,6},{8,9},{9,8},{10,11... | collective-permute-start | bytes 49160 | tf_op jit(solution)/shard_map/ppermute | solution.py:38
  0.5 2.6 %collective-permute-start = (f32[32,128]{1,0:T(8,128)}, f32[32,128]{1,0:T(8,128)S(1)}, u32[]{:S(2)}, u32[]{:S(2)}) collective-permute-start(f32[32,128]{1,0:T(8,128)} %refs_0_.1), channel_id=1, source_target_pairs={{0,2},{1,3},{2,1},{3,0},{4,6},{5,7},{6,5},{7,4},{8,10},{9,11},{10,... | collective-permute-start | bytes 49160 | tf_op jit(solution)/shard_map/ppermute | solution.py:38
  3.1 0.1 collective-permute-start.2
  3.2 0.0 copy-done.5
  3.2 0.0 copy-done.2
  3.2 0.0 copy-done.4
  3.2 0.0 copy-done.1
  3.2 0.0 copy-start
  3.2 3.2 %prepare.1 = (bf16[2048,256]{1,0:T(8,128)(2,1)S(1)}, s32[32,128]{1,0:T(8,128)S(1)}, f32[1,256]{1,0:T(1,128)S(1)}, bf16[256,256]{1,0:T(8,128)(2,1)S(1)}, bf16[256...) custom-call(s32[1,4096]{1,0:T(1,128)S(1)} %copy-done.4, ...), custom_call_target="tpu_custom_call" | custom-call | flops 4000000000 | bytes 4194304 | tf_op jit(solution)/shard_map/prepare/pallas_call | solution.py:206
  6.5 0.0 collective-permute-done.1.refs_2_
  6.5 0.0 collective-permute-done.refs_1_
  6.5 0.5 %collective-permute-done.2.refs_3_ = f32[32,128]{1,0:T(8,128)S(1)} collective-permute-done((f32[32,128]{1,0:T(8,128)}, f32[32,128]{1,0:T(8,128)S(1)}, u32[]{:S(2)}, u32[]{:S(2)}) %collective-permute-start.2) | collective-permute-done | bytes 16416 | tf_op jit(solution)/shard_map/ppermute | solution.py:38
  7.0 0.0 copy-done
  7.0 0.6 %local_maxima.1._ = bf16[32,128]{1,0:T(8,128)(2,1)S(1)} custom-call(bf16[2048,256]{1,0:T(8,128)(2,1)S(1)} %get-tuple-element.17.left, s32[32,128]{1,0:T(8,128)S(1)} %get-tuple-element.18.live, bf16[128,128]{1,0:T(8,128)(2,1)S(1)} %early.1.spread, f32[32,128]{1,0:T(8,128)S(1)} %copy-done, f32[32,128]{1,0:T(8,128)S(1)} %collective-permute-done.refs_1_, ...), custom_call_target="tpu_custom_call" | custom-call | tf_op jit(solution)/shard_map/local_maxima/pallas_call | solution.py:313
  7.7 0.0 copy-start.3
  7.7 0.1 collective-permute-start.3
  7.8 1.2 %collective-permute-done.3 = bf16[32,128]{1,0:T(8,128)(2,1)S(1)} collective-permute-done((bf16[32,128]{1,0:T(8,128)(2,1)S(1)}, bf16[32,128]{1,0:T(8,128)(2,1)S(1)}, u32[]{:S(2)}, u32[]{:S(2)}) %collective-permute-start.3) | collective-permute-done | bytes 8224 | tf_op jit(solution)/shard_map/ppermute | solution.py:45
  8.9 1.2 %collective-permute-start.4 = (bf16[32,128]{1,0:T(8,128)(2,1)S(1)}, bf16[32,128]{1,0:T(8,128)(2,1)S(1)}, u32[]{:S(2)}, u32[]{:S(2)}) collective-permute-start(bf16[32,128]{1,0:T(8,128)(2,1)S(1)} %max.6), channel_id=1, source_target_pairs={{0,3},{1,2},{2,1},{3,0},{4,6},{5,7},{6,5},{7,4},{8,11},{9,10},{10,... | collective-permute-start | bytes 24584 | tf_op jit(solution)/shard_map/ppermute | solution.py:47
  10.1 1.9 %collective-permute-done.4 = bf16[32,128]{1,0:T(8,128)(2,1)S(1)} collective-permute-done((bf16[32,128]{1,0:T(8,128)(2,1)S(1)}, bf16[32,128]{1,0:T(8,128)(2,1)S(1)}, u32[]{:S(2)}, u32[]{:S(2)}) %collective-permute-start.4) | collective-permute-done | bytes 8224 | tf_op jit(solution)/shard_map/ppermute | solution.py:47
  12.1 1.6 %collective-permute-start.5 = (bf16[32,128]{1,0:T(8,128)(2,1)S(1)}, bf16[32,128]{1,0:T(8,128)(2,1)S(1)}, u32[]{:S(2)}, u32[]{:S(2)}) collective-permute-start(bf16[32,128]{1,0:T(8,128)(2,1)S(1)} %max.7.refs_0_), channel_id=1, source_target_pairs={{0,4},{1,9},{2,11},{3,6},{4,8},{5,13},{6,10},{7,15},{8,12},{9,0},{... | collective-permute-start | bytes 24584 | tf_op jit(solution)/shard_map/ppermute | solution.py:54
  13.7 1.7 %collective-permute-start.7 = (bf16[32,128]{1,0:T(8,128)(2,1)S(1)}, bf16[32,128]{1,0:T(8,128)(2,1)S(1)}, u32[]{:S(2)}, u32[]{:S(2)}) collective-permute-start(bf16[32,128]{1,0:T(8,128)(2,1)S(1)} %max.7.refs_0_), channel_id=1, source_target_pairs={{0,13},{1,12},{2,15},{3,14},{4,0},{5,1},{6,3},{7,2},{8,5},{9,7},{1... | collective-permute-start | bytes 24584 | tf_op jit(solution)/shard_map/ppermute | solution.py:55
  15.3 0.7 %collective-permute-done.5.refs_1_ = bf16[32,128]{1,0:T(8,128)(2,1)S(1)} collective-permute-done((bf16[32,128]{1,0:T(8,128)(2,1)S(1)}, bf16[32,128]{1,0:T(8,128)(2,1)S(1)}, u32[]{:S(2)}, u32[]{:S(2)}) %collective-permute-start.5) | collective-permute-done | bytes 8224 | tf_op jit(solution)/shard_map/ppermute | solution.py:54
  16.0 0.4 %collective-permute-start.6 = (bf16[32,128]{1,0:T(8,128)(2,1)S(1)}, bf16[32,128]{1,0:T(8,128)(2,1)S(1)}, u32[]{:S(2)}, u32[]{:S(2)}) collective-permute-start(bf16[32,128]{1,0:T(8,128)(2,1)S(1)} %collective-permute-done.5.refs_1_), channel_id=1, source_target_pairs={{0,1},{1,0},{2,3},{3,2},{4,5},{5,4},{6,7},{7,6},{8,9},{9,8},{10,11... | collective-permute-start | bytes 24584 | tf_op jit(solution)/shard_map/ppermute | solution.py:56
  16.5 0.0 copy-done.3
  16.5 0.0 copy-done.6
  16.5 0.6 %make_tables.1 = (bf16[80,128]{1,0:T(8,128)(2,1)S(1)}, bf16[96,256]{1,0:T(8,128)(2,1)S(1)}) custom-call(s32[1,64]{1,0:T(1,128)S(1)} %copy-done.6, f32[32,256]{1,0:T(8,128)S(1)} %copy-done.3, bf16[32,128]{1,0:T(8,128)(2,1)S(1)} %local_maxima.1._), custom_call_target="tpu_custom_call" | custom-call | flops 500000000 | tf_op jit(solution)/shard_map/make_tables/pallas_call | solution.py:257
  17.2 0.1 collective-permute-done.7.refs_3_
  17.3 0.0 collective-permute-done.6.refs_2_
  17.3 2.1 %rerank.1 = f32[16,256]{1,0:T(8,128)} custom-call(bf16[32,128]{1,0:T(8,128)(2,1)S(1)} %max.7.refs_0_, bf16[32,128]{1,0:T(8,128)(2,1)S(1)} %collective-permute-done.5.refs_1_, bf16[32,128]{1,0:T(8,128)(2,1)S(1)} %collective-permute-done.6.refs_2_, bf16[32,128]{1,0:T(8,128)(2,1)S(1)} %collective-permute-done.7.refs_3_, ...), custom_call_target="tpu_custom_call" | custom-call | tf_op jit(solution)/shard_map/rerank/pallas_call | solution.py:386
  (5 shorter events, 0.0 us)
Async XLA Ops:
  0.0 3.2 %copy-start.5 = (f32[16,128]{1,0:T(8,128)S(1)}, f32[16,128]{1,0:T(8,128)}, u32[]{:S(2)}) copy-start(f32[16,128]{1,0:T(8,128)} %buckets.1) | copy-start | bytes 24580
  0.0 3.2 %copy-start.2 = (bf16[4096,128]{1,0:T(8,128)(2,1)S(1)}, bf16[4096,128]{1,0:T(8,128)(2,1)}, u32[]{:S(2)}) copy-start(bf16[4096,128]{1,0:T(8,128)(2,1)} %centroids.1) | copy-start | bytes 3145732
  0.0 3.2 %copy-start.4 = (s32[1,4096]{1,0:T(1,128)S(1)}, s32[1,4096]{1,0:T(1,128)}, u32[]{:S(2)}) copy-start(s32[1,4096]{1,0:T(1,128)} %ids_vmem.1) | copy-start | bytes 49156
  0.0 3.2 %copy-start.1 = (s32[1,32,8192]{2,1,0:T(8,128)S(1)}, s32[1,32,8192]{2,1,0:T(8,128)}, u32[]{:S(2)}) copy-start(s32[1,32,8192]{2,1,0:T(8,128)} %param.17) | copy-start | bytes 3145732
  0.0 6.5 %collective-permute-start.1 = (f32[32,128]{1,0:T(8,128)}, f32[32,128]{1,0:T(8,128)S(1)}, u32[]{:S(2)}, u32[]{:S(2)}) collective-permute-start(f32[32,128]{1,0:T(8,128)} %refs_0_.1), channel_id=1, source_target_pairs={{0,1},{1,0},{2,3},{3,2},{4,5},{5,4},{6,7},{7,6},{8,9},{9,8},{10,11... | collective-permute-start | bytes 49160 | tf_op jit(solution)/shard_map/ppermute | solution.py:38
  0.5 6.0 %collective-permute-start = (f32[32,128]{1,0:T(8,128)}, f32[32,128]{1,0:T(8,128)S(1)}, u32[]{:S(2)}, u32[]{:S(2)}) collective-permute-start(f32[32,128]{1,0:T(8,128)} %refs_0_.1), channel_id=1, source_target_pairs={{0,2},{1,3},{2,1},{3,0},{4,6},{5,7},{6,5},{7,4},{8,10},{9,11},{10,... | collective-permute-start | bytes 49160 | tf_op jit(solution)/shard_map/ppermute | solution.py:38
  3.1 3.9 %collective-permute-start.2 = (f32[32,128]{1,0:T(8,128)}, f32[32,128]{1,0:T(8,128)S(1)}, u32[]{:S(2)}, u32[]{:S(2)}) collective-permute-start(f32[32,128]{1,0:T(8,128)} %refs_0_.1), channel_id=1, source_target_pairs={{0,3},{1,2},{2,0},{3,1},{4,7},{5,6},{6,4},{7,5},{8,11},{9,10},{10,... | collective-permute-start | bytes 49160 | tf_op jit(solution)/shard_map/ppermute | solution.py:38
  3.2 3.8 %copy-start = (f32[32,128]{1,0:T(8,128)S(1)}, f32[32,128]{1,0:T(8,128)}, u32[]{:S(2)}) copy-start(f32[32,128]{1,0:T(8,128)} %refs_0_.1) | copy-start | bytes 49156
  7.7 8.8 %copy-start.3 = (f32[32,256]{1,0:T(8,128)S(1)}, f32[32,256]{1,0:T(8,128)}, u32[]{:S(2)}) copy-start(f32[32,256]{1,0:T(8,128)} %proj.1) | copy-start | bytes 98308
  7.7 1.2 %collective-permute-start.3 = (bf16[32,128]{1,0:T(8,128)(2,1)S(1)}, bf16[32,128]{1,0:T(8,128)(2,1)S(1)}, u32[]{:S(2)}, u32[]{:S(2)}) collective-permute-start(bf16[32,128]{1,0:T(8,128)(2,1)S(1)} %local_maxima.1._), channel_id=1, source_target_pairs={{0,1},{1,0},{2,3},{3,2},{4,5},{5,4},{6,7},{7,6},{8,9},{9,8},{10,11... | collective-permute-start | bytes 24584 | tf_op jit(solution)/shard_map/ppermute | solution.py:45
  8.9 7.6 %copy-start.6 = (s32[1,64]{1,0:T(1,128)S(1)}, s32[1,64]{1,0:T(1,128)}, u32[]{:S(2)}) copy-start(s32[1,64]{1,0:T(1,128)} %candidates_vmem.1) | copy-start | bytes 772
  8.9 3.1 %collective-permute-start.4 = (bf16[32,128]{1,0:T(8,128)(2,1)S(1)}, bf16[32,128]{1,0:T(8,128)(2,1)S(1)}, u32[]{:S(2)}, u32[]{:S(2)}) collective-permute-start(bf16[32,128]{1,0:T(8,128)(2,1)S(1)} %max.6), channel_id=1, source_target_pairs={{0,3},{1,2},{2,1},{3,0},{4,6},{5,7},{6,5},{7,4},{8,11},{9,10},{10,... | collective-permute-start | bytes 24584 | tf_op jit(solution)/shard_map/ppermute | solution.py:47
  12.1 4.0 %collective-permute-start.5 = (bf16[32,128]{1,0:T(8,128)(2,1)S(1)}, bf16[32,128]{1,0:T(8,128)(2,1)S(1)}, u32[]{:S(2)}, u32[]{:S(2)}) collective-permute-start(bf16[32,128]{1,0:T(8,128)(2,1)S(1)} %max.7.refs_0_), channel_id=1, source_target_pairs={{0,4},{1,9},{2,11},{3,6},{4,8},{5,13},{6,10},{7,15},{8,12},{9,0},{... | collective-permute-start | bytes 24584 | tf_op jit(solution)/shard_map/ppermute | solution.py:54
  13.7 3.7 %collective-permute-start.7 = (bf16[32,128]{1,0:T(8,128)(2,1)S(1)}, bf16[32,128]{1,0:T(8,128)(2,1)S(1)}, u32[]{:S(2)}, u32[]{:S(2)}) collective-permute-start(bf16[32,128]{1,0:T(8,128)(2,1)S(1)} %max.7.refs_0_), channel_id=1, source_target_pairs={{0,13},{1,12},{2,15},{3,14},{4,0},{5,1},{6,3},{7,2},{8,5},{9,7},{1... | collective-permute-start | bytes 24584 | tf_op jit(solution)/shard_map/ppermute | solution.py:55
  16.0 1.3 %collective-permute-start.6 = (bf16[32,128]{1,0:T(8,128)(2,1)S(1)}, bf16[32,128]{1,0:T(8,128)(2,1)S(1)}, u32[]{:S(2)}, u32[]{:S(2)}) collective-permute-start(bf16[32,128]{1,0:T(8,128)(2,1)S(1)} %collective-permute-done.5.refs_1_), channel_id=1, source_target_pairs={{0,1},{1,0},{2,3},{3,2},{4,5},{5,4},{6,7},{7,6},{8,9},{9,8},{10,11... | collective-permute-start | bytes 24584 | tf_op jit(solution)/shard_map/ppermute | solution.py:56
